TPU v7x, 256 devices: a whole 4x4x8 slice. The times are simulated.
256 devices in a mesh: comp: 2 (over core), gx: 16 (over x, y), gy: 8 (over z).
Axes of the slice: x: 4, y: 4, z: 8, core: 2. Of those that a mesh axis runs over, the one named last changes fastest.
Arguments:
- state: float32 [2, 8, 384, 3072], P('comp', None, 'gx', 'gy'), may hold values from -6 to 6
- response: float32 [2, 8, 3072], P('comp'), may hold values from -0.95 to 0
- diffusion: float32 [2, 384, 3072], P('comp', 'gx', 'gy'), may hold values from 0.02 to 0.24
- land_mask: int32 [384, 3072], P('gx', 'gy'), may hold values 0 or 1
- couple_src: int32 [2, 16, 8, 128, 128], P('comp', 'gx', 'gy'), may hold values from 0 to 9215
- couple_dst: int32 [2, 16, 8, 128, 128], P('comp', 'gx', 'gy'), may hold values from 0 to 9215
- couple_weight: float32 [2, 16, 8, 128, 128], P('comp', 'gx', 'gy'), may hold values from 0.1 to 1
- couple_count: int32 [2, 16, 8, 128], P('comp', 'gx', 'gy'), may hold values from 0 to 128, as said below
Outputs:
- final_state: float32 [2, 8, 384, 3072], P('comp', None, 'gx', 'gy')
Inputs may be any that keep to these rules, and one draw needn't show every extreme that they name: `couple_count`: at most 128 live slots per ordered device pair; every sending device has one pair with exactly 128.
All inputs are finite; a program needn't handle non-finite values. No bound on the sum of `land_mask` on one device may be relied on, other than what follows from the above.
Results may differ from a plain program's by a relative error of at most 0.0095.
Values may be sent and summed in bfloat16 or wider, within the bound.
No kernel may reach another device: no remote copies, remote signals or barrier semaphores. Data moves between devices by JAX's collectives and lax.ppermute only.
A program may use at most 128 MiB of HBM per device.

v0:
```python
import math

import jax
import jax.numpy as jnp
from jax import lax
from jax.sharding import PartitionSpec as P

FC = 4


def extended(block, sides, width):
    for axis, dim in sides:
        count = lax.axis_size(axis)
        forward = [(i, i + 1) for i in range(count - 1)]
        backward = [(target, source) for source, target in forward]
        low = lax.ppermute(
            lax.slice_in_dim(block, block.shape[dim] - width, None, axis=dim), axis, forward
        )
        high = lax.ppermute(lax.slice_in_dim(block, 0, width, axis=dim), axis, backward)
        block = jnp.concatenate([low, block, high], axis=dim)
    return block


def partner(value, axis, stride):
    mask = 2**stride
    pairs = [(source, source ^ mask) for source in range(lax.axis_size(axis))]
    return lax.ppermute(value, axis, pairs)


def make_table(cols):
    rows_idx = jnp.arange(cols, dtype=jnp.int32)[:, None]
    wave_idx = jnp.arange(cols // 2, dtype=jnp.int32)[None, :]
    phase = rows_idx * wave_idx % cols
    angle = phase.astype(jnp.float32) * (2.0 * math.pi / cols)
    return jnp.concatenate([jnp.cos(angle), jnp.sin(angle)], axis=1).astype(jnp.bfloat16)


def back_transform(filtered, table_part):
    return lax.dot_general(
        filtered, table_part, (((1,), (1,)), ((), ())), preferred_element_type=jnp.float32
    )


def circle_increment(circles, resp_part, table, scale):
    count, rows_part, cols_all = circles.shape
    spec = jnp.dot(circles.reshape(-1, cols_all), table, preferred_element_type=jnp.float32)
    spec = spec.reshape(count, rows_part, cols_all)
    filtered = (spec * resp_part[:, None, :]).astype(jnp.bfloat16)
    incr = (back_transform(filtered.reshape(-1, cols_all), table) * scale).astype(jnp.bfloat16)
    return incr.reshape(count, rows_part, cols_all)


def diffuse(fields, rate):
    padded = extended(fields.astype(jnp.bfloat16), (("gx", 1),), 1).astype(fields.dtype)
    return fields + rate[None] * (padded[:, 2:] + padded[:, :-2] - 2.0 * fields)


def local(
    state, response, diffusion, land_mask, couple_src, couple_dst, couple_weight, couple_count
):
    levels, rows_dev, cols_dev = (state.shape[1], state.shape[2], state.shape[3])
    groups_x = lax.axis_size("gx")
    groups_y = lax.axis_size("gy")
    peers = groups_x * groups_y
    slots = couple_src.shape[4]
    cells = rows_dev * cols_dev
    cols_all = cols_dev * groups_y
    per_level = levels // groups_y
    section = lax.axis_index("comp")
    keep = jnp.where(section == 1, land_mask.astype(jnp.float32), jnp.float32(1.0))
    table = make_table(cols_all)
    scale = 2.0 / cols_all
    src_idx = couple_src.reshape(peers, slots)
    dst_idx = couple_dst.reshape(peers, slots)
    live = jnp.arange(slots, dtype=jnp.int32)[None, :] < couple_count.reshape(peers, 1)
    weights = jnp.where(live, couple_weight.reshape(peers, slots), jnp.float32(0.0))
    first_level = lax.axis_index("gy") * per_level
    resp_mine = lax.dynamic_slice_in_dim(response[0], first_level, per_level, 0)
    rate = diffusion[0]
    fields = state[0]
    surface = fields[:FC].reshape(FC, cells)
    outgoing = jnp.transpose(surface[:, src_idx] * weights[None], (1, 0, 2))
    crossed = partner(outgoing, "comp", 0)
    arrived = lax.all_to_all(crossed, ("gx", "gy"), split_axis=0, concat_axis=0, tiled=True)
    incoming = jnp.transpose(arrived, (1, 0, 2))
    surface = surface.at[:, dst_idx].add(incoming)
    surf = surface.reshape(FC, rows_dev, cols_dev)
    fields = jnp.concatenate([surf, fields[FC:]], axis=0)
    grid_bf = fields.astype(jnp.bfloat16)
    circles = lax.all_to_all(grid_bf, "gy", split_axis=0, concat_axis=2, tiled=True)
    incr = circle_increment(circles, resp_mine, table, scale)
    incr = lax.all_to_all(incr, "gy", split_axis=2, concat_axis=0, tiled=True)
    fields = fields + incr.astype(jnp.float32)
    fields = diffuse(fields, rate) * keep[None]
    return fields[None]


def solution(mesh):
    return jax.shard_map(
        local,
        mesh=mesh,
        in_specs=(
            P("comp", None, "gx", "gy"),
            P("comp", None, None),
            P("comp", "gx", "gy"),
            P("gx", "gy"),
            P("comp", "gx", "gy", None, None),
            P("comp", "gx", "gy", None, None),
            P("comp", "gx", "gy", None, None),
            P("comp", "gx", "gy", None),
        ),
        out_specs=P("comp", None, "gx", "gy"),
        check_vma=False,
    )
```

profile of v0, /device:TPU:2, one launch (start us, length us, event | category | flops | bytes accessed | tf_op | source)
XLA Modules:
  0.0 339.9 jit_solution(3858053618413238596)
XLA Ops:
  0.0 0.0 copy-start
  0.0 0.0 copy-start.3
  0.0 0.0 copy-start.1
  0.0 1.0 fusion.24
  1.1 3.3 copy.23
  4.4 0.9 fusion.21
  5.2 57.1 %gather_fusion = f32[16384,4]{1,0:T(8,128)} fusion(f32[4,9216]{0,1:T(8,128)} %bitcast.51, s32[16384]{0:T(1024)S(1)} %fusion.21), kind=kCustom, calls=%fused_computation | custom fusion | bytes 589824 | tf_op jit(solution)/shard_map/gather | solution.py:82
  62.4 5.2 %copy.24 = f32[128,128,4]{1,0,2:T(8,128)S(1)} copy(f32[128,128,4]{2,1,0:T(8,128)} %bitcast.54) | data formatting | bytes 524288 | tf_op jit(solution)/shard_map/gather | solution.py:82
  67.6 0.0 copy-done.3
  67.6 0.0 copy-done.1
  67.6 0.1 bitcast_select_fusion
  67.7 0.1 collective-permute-start
  67.8 1.5 collective-permute-done
  69.4 0.9 copy.25
  70.2 15.5 %all-to-all-start = ((f32[128,4,128]{2,1,0:T(4,128)}), f32[128,4,128]{2,1,0:T(4,128)S(1)}, u32[]{:S(2)}, u32[]{:S(2)}) async-start(f32[128,4,128]{2,1,0:T(4,128)} %copy.25), calls=%async_computation | async-start | bytes 524288 | tf_op jit(solution)/shard_map/all_to_all | solution.py:84
  85.8 0.0 copy-start.2
  85.8 79.5 %sine_convert_fusion = (bf16[3072,1536]{1,0:T(8,128)(2,1)}, bf16[3072,1536]{1,0:T(8,128)(2,1)}) fusion(), kind=kLoop, calls=%fused_computation.6 | loop fusion | flops 51904512 | bytes 18874368 | tf_op jit(solution)/shard_map/convert.4
  165.3 0.0 copy-done.2
  165.3 0.0 all-to-all-done
  165.4 5.1 %copy.26 = f32[16384,4]{1,0:T(8,128)} copy(f32[16384,4]{0,1:T(4,128)S(1)} %bitcast.57) | data formatting | bytes 524288 | tf_op jit(solution)/shard_map/transpose | solution.py:85
  170.5 83.3 %scatter_fusion = f32[4,9216]{0,1:T(8,128)} fusion(f32[4,9216]{0,1:T(8,128)} %bitcast.52, s32[16384]{0:T(1024)S(1)} %fusion.19, f32[16384,4]{1,0:T(8,128)} %copy.26), kind=kCustom, calls=%fused_computation.1 | custom fusion | flops 65536 | bytes 851968 | tf_op jit(solution)/shard_map/scatter-add | solution.py:86
  253.8 3.8 %copy.27 = f32[4,24,384]{2,1,0:T(8,128)S(1)} copy(f32[4,24,384]{0,2,1:T(8,128)} %bitcast.53) | data formatting | bytes 294912 | tf_op jit(solution)/shard_map/reshape | solution.py:87
  257.6 0.7 fusion.17
  258.3 6.7 %all-to-all-start.1 = ((bf16[8,24,384]{2,1,0:T(8,128)(2,1)}), bf16[8,24,384]{2,1,0:T(8,128)(2,1)S(1)}, u32[]{:S(2)}, u32[]{:S(2)}) async-start(bf16[8,24,384]{2,1,0:T(8,128)(2,1)} %fusion.17), calls=%async_computation.1 | async-start | bytes 294912 | tf_op jit(solution)/shard_map/all_to_all | solution.py:90
  264.9 0.0 copy-done
  265.0 9.2 %all-to-all-done.1 = bf16[8,24,384]{2,1,0:T(8,128)(2,1)S(1)} async-done(((bf16[8,24,384]{2,1,0:T(8,128)(2,1)}), bf16[8,24,384]{2,1,0:T(8,128)(2,1)S(1)}, u32[]{:S(2)}, u32[]{:S(2)}) %all-to-all-start.1) | async-done | bytes 147488 | tf_op jit(solution)/shard_map/all_to_all | solution.py:90
  274.2 7.8 %fusion.10 = bf16[24,3072]{1,0:T(8,128)(2,1)S(1)} fusion(bf16[24,3072]{1,0:T(8,128)(2,1)S(1)} %bitcast.59, bf16[3072,1536]{1,0:T(8,128)(2,1)} %get-tuple-element.9, bf16[3072,1536]{1,0:T(8,128)(2,1)} %get-tuple-element.10, f32[3072]{0:T(1024)S(1)} %bitcast.61), kind=kOutput, calls=%fused_computation.17 | convolution fusion | flops 490881024 | bytes 19181568 | tf_op jit(solution)/shard_map/dot_general | solution.py:46
  282.0 9.0 %fusion.11 = bf16[1,24,3072]{2,1,0:T(8,128)(2,1)S(1)} fusion(bf16[24,3072]{1,0:T(8,128)(2,1)S(1)} %fusion.10, bf16[3072,1536]{1,0:T(8,128)(2,1)} %get-tuple-element.9, bf16[3072,1536]{1,0:T(8,128)(2,1)} %get-tuple-element.10), kind=kOutput, calls=%fused_computation.18 | convolution fusion | flops 490881024 | bytes 19169280 | tf_op jit(solution)/shard_map/dot_general | solution.py:39
  291.0 1.9 copy.29
  292.9 0.5 broadcast.66
  293.4 17.0 %reduce = bf16[3072,24]{1,0:T(8,128)(2,1)S(1)} reduce(bf16[3072,1,24]{2,1,0:T(2,128)(2,1)S(1)} %bitcast.55, bf16[]{:T(256)} %broadcast.66), dimensions={1}, to_apply=%bitcast.46.reduce_sub_computation | reduce | bytes 294914
  310.4 1.6 reshape.149
  312.0 3.4 all-to-all-start.2
  315.4 9.2 %all-to-all-done.2 = bf16[8,2,4608]{2,1,0:T(2,128)(2,1)S(1)} async-done(((bf16[8,2,4608]{2,1,0:T(2,128)(2,1)}), bf16[8,2,4608]{2,1,0:T(2,128)(2,1)S(1)}, u32[]{:S(2)}, u32[]{:S(2)}) %all-to-all-start.2) | async-done | bytes 147488 | tf_op jit(solution)/shard_map/all_to_all | solution.py:92
  324.6 2.1 reshape.150
  326.7 1.7 bitcast_convert_fusion
  328.4 0.4 copy.30
  328.9 3.4 %collective-permute-start.1 = (bf16[8,1,384]{2,1,0:T(2,128)(2,1)S(1)}, bf16[8,1,384]{2,1,0:T(2,128)(2,1)S(1)}, u32[]{:S(2)}, u32[]{:S(2)}) collective-permute-start(bf16[8,1,384]{2,1,0:T(2,128)(2,1)S(1)} %get-tuple-element.7), channel_id=1, source_target_pairs={{0,8},{8,16},{16,24},{24,32},{32,40},{40,48},{48,56},{56,64},{64,7... | collective-permute-start | bytes 18440 | tf_op jit(solution)/shard_map/ppermute | solution.py:16
  332.4 4.5 %collective-permute-start.2 = (bf16[8,1,384]{2,1,0:T(2,128)(2,1)S(1)}, bf16[8,1,384]{2,1,0:T(2,128)(2,1)S(1)}, u32[]{:S(2)}, u32[]{:S(2)}) collective-permute-start(bf16[8,1,384]{2,1,0:T(2,128)(2,1)S(1)} %get-tuple-element.8), channel_id=1, source_target_pairs={{8,0},{16,8},{24,16},{32,24},{40,32},{48,40},{56,48},{64,56},{72,6... | collective-permute-start | bytes 18440 | tf_op jit(solution)/shard_map/ppermute | solution.py:19
  336.9 0.8 convert_select_fusion
  337.7 0.0 collective-permute-done.1
  337.7 0.6 collective-permute-done.2
  338.3 0.1 maximum_convert_fusion
  338.4 1.6 fusion.16
  (6 shorter events, 0.1 us)
Async XLA Ops:
  0.0 264.9 %copy-start = (f32[1,8,3072]{2,1,0:T(8,128)S(1)}, f32[1,8,3072]{2,1,0:T(8,128)}, u32[]{:S(2)}) copy-start(f32[1,8,3072]{2,1,0:T(8,128)} %param.9) | copy-start | bytes 294916
  0.0 67.6 %copy-start.3 = (s32[1,1,1,128]{3,2,1,0:T(1,128)S(1)}, s32[1,1,1,128]{3,2,1,0:T(1,128)}, u32[]{:S(2)}) copy-start(s32[1,1,1,128]{3,2,1,0:T(1,128)} %param.15) | copy-start | bytes 1540
  0.0 67.6 %copy-start.1 = (f32[1,1,1,128,128]{4,3,2,1,0:T(8,128)S(1)}, f32[1,1,1,128,128]{4,3,2,1,0:T(8,128)}, u32[]{:S(2)}) copy-start(f32[1,1,1,128,128]{4,3,2,1,0:T(8,128)} %param.14) | copy-start | bytes 196612
  67.7 1.6 collective-permute-start
  70.2 95.1 %all-to-all-start = ((f32[128,4,128]{2,1,0:T(4,128)}), f32[128,4,128]{2,1,0:T(4,128)S(1)}, u32[]{:S(2)}, u32[]{:S(2)}) async-start(f32[128,4,128]{2,1,0:T(4,128)} %copy.25), calls=%async_computation | async-start | bytes 524288 | tf_op jit(solution)/shard_map/all_to_all | solution.py:84
  85.8 79.6 %copy-start.2 = (s32[1,1,1,128,128]{4,3,2,1,0:T(8,128)S(1)}, s32[1,1,1,128,128]{4,3,2,1,0:T(8,128)}, u32[]{:S(2)}) copy-start(s32[1,1,1,128,128]{4,3,2,1,0:T(8,128)} %param.13) | copy-start | bytes 196612
  258.3 15.9 %all-to-all-start.1 = ((bf16[8,24,384]{2,1,0:T(8,128)(2,1)}), bf16[8,24,384]{2,1,0:T(8,128)(2,1)S(1)}, u32[]{:S(2)}, u32[]{:S(2)}) async-start(bf16[8,24,384]{2,1,0:T(8,128)(2,1)} %fusion.17), calls=%async_computation.1 | async-start | bytes 294912 | tf_op jit(solution)/shard_map/all_to_all | solution.py:90
  312.0 12.6 %all-to-all-start.2 = ((bf16[8,2,4608]{2,1,0:T(2,128)(2,1)}), bf16[8,2,4608]{2,1,0:T(2,128)(2,1)S(1)}, u32[]{:S(2)}, u32[]{:S(2)}) async-start(bf16[8,2,4608]{2,1,0:T(2,128)(2,1)} %reshape.149), calls=%async_computation.2 | async-start | bytes 294912 | tf_op jit(solution)/shard_map/all_to_all | solution.py:92
  328.9 8.7 %collective-permute-start.1 = (bf16[8,1,384]{2,1,0:T(2,128)(2,1)S(1)}, bf16[8,1,384]{2,1,0:T(2,128)(2,1)S(1)}, u32[]{:S(2)}, u32[]{:S(2)}) collective-permute-start(bf16[8,1,384]{2,1,0:T(2,128)(2,1)S(1)} %get-tuple-element.7), channel_id=1, source_target_pairs={{0,8},{8,16},{16,24},{24,32},{32,40},{40,48},{48,56},{56,64},{64,7... | collective-permute-start | bytes 18440 | tf_op jit(solution)/shard_map/ppermute | solution.py:16
  332.4 5.9 %collective-permute-start.2 = (bf16[8,1,384]{2,1,0:T(2,128)(2,1)S(1)}, bf16[8,1,384]{2,1,0:T(2,128)(2,1)S(1)}, u32[]{:S(2)}, u32[]{:S(2)}) collective-permute-start(bf16[8,1,384]{2,1,0:T(2,128)(2,1)S(1)} %get-tuple-element.8), channel_id=1, source_target_pairs={{8,0},{16,8},{24,16},{32,24},{40,32},{48,40},{56,48},{64,56},{72,6... | collective-permute-start | bytes 18440 | tf_op jit(solution)/shard_map/ppermute | solution.py:19
where the time goes:
time: 342 us; the launch traced here: 340 us
  other arithmetic  186 us (54%)
  local copies, waits for them, and re-layouts  83.1 us (24%)
  starting transfers between devices  33.6 us (10%)
  waiting for transfers between devices  20.5 us (6%)
  matrix products  16.8 us (5%)
    scatter-add x1, other arithmetic, local(): surface = surface.at[:, dst_idx].add(incoming)  83.3 us
    another operation x1, other arithmetic  79.5 us
    gather x2, local copies, waits for them, and re-layouts, local(): outgoing = jnp.transpose(surface[:, src_idx] * weights[None], (1, 0, 2))  62.3 us
    unnamed x1, other arithmetic  17 us
    all_to_all x1, starting transfers between devices, local(): lax.all_to_all(crossed, ('gx', 'gy'), split_axis=0, concat_axis=0, tiled=...  15.5 us
    all_to_all x1, waiting for transfers between devices, local(): lax.all_to_all(grid_bf, 'gy', split_axis=0, concat_axis=2, tiled=True)  9.22 us
    all_to_all x1, waiting for transfers between devices, local(): incr = lax.all_to_all(incr, 'gy', split_axis=2, concat_axis=0, tiled=True)  9.17 us
    dot_general x1, matrix products, back_transform(): lax.dot_general(filtered, table_part, (((1,), (1,)), ((), ())), preferred...  9.03 us
  transfers between devices with their start and end apart: 6, of which 4 were waited for; matrix products, arithmetic and copies ran while one was open for 24% of the time, Pallas kernels for 0%

commit v1 on v0

v1 whole, which is shorter than its diff:
```python
import functools
import math

import jax
import jax.numpy as jnp
import numpy as np
from jax import lax
from jax.experimental import pallas as pl
from jax.experimental.pallas import tpu as pltpu
from jax.sharding import PartitionSpec as P

FC = 4
LANES = 128
BF = jnp.bfloat16
F32 = jnp.float32
VMEM = pl.BlockSpec(memory_space=pltpu.VMEM)
SMEM = pl.BlockSpec(memory_space=pltpu.SMEM)
PARAMS = pltpu.CompilerParams(vmem_limit_bytes=32 * 2**20)


def one_hot(rows, index):
    spot = lax.broadcasted_iota(jnp.int32, (rows, index.shape[1]), 0)
    return spot == index


def split_cell(idx, cols):
    row = (idx.astype(F32) * (1.0 / cols) + 0.5 / cols).astype(jnp.int32)
    return row, idx - row * cols


def gather_kernel(group, count_ref, surf_ref, src_ref, weight_ref, out_ref):
    _, _, rows, cols = surf_ref.shape
    peers, slots = src_ref.shape
    fc = out_ref.shape[1]
    surface = surf_ref[0, :fc].reshape(fc * rows, cols).astype(BF)
    lane = lax.broadcasted_iota(jnp.int32, (1, slots), 1)

    def step(g, carry):
        base = pl.multiple_of(g * group, group)
        row, col = split_cell(src_ref[pl.ds(base, group), :], cols)
        for i in range(0, group, 2):
            pick = jnp.concatenate([one_hot(cols, col[i : i + 1]), one_hot(cols, col[i + 1 : i + 2])], axis=1)
            lines = jnp.dot(surface, jnp.where(pick, 1.0, 0.0).astype(BF), preferred_element_type=F32)
            rowpick = jnp.concatenate([one_hot(rows, row[i : i + 1]), one_hot(rows, row[i + 1 : i + 2])], axis=1)
            value = jnp.sum(jnp.where(rowpick[None], lines.reshape(fc, rows, 2 * slots), 0.0), axis=1)
            for j in range(2):
                w = jnp.where(lane < count_ref[base + i + j], weight_ref[pl.ds(base + i + j, 1), :], 0.0)
                out_ref[base + i + j] = (value[:, j * slots : (j + 1) * slots] * w).astype(BF)
        return carry

    lax.fori_loop(0, peers // group, step, 0)


def scatter_kernel(group, state_ref, arrived_ref, dst_ref, surf_ref, grid_ref):
    _, levels, rows, cols = state_ref.shape
    peers, fc, slots = arrived_ref.shape
    surf_ref[...] = state_ref[0, :fc]

    def step(g, carry):
        base = pl.multiple_of(g * group, group)
        row, col = split_cell(dst_ref[pl.ds(base, group), :], cols)
        spread, pick = [], []
        for i in range(group):
            value = arrived_ref[base + i].astype(F32)
            rowpick = one_hot(rows, row[i : i + 1])
            spread.append(jnp.where(rowpick[None], value[:, None, :], 0.0).reshape(fc * rows, slots).astype(BF))
            pick.append(jnp.where(one_hot(cols, col[i : i + 1]), 1.0, 0.0).astype(BF))
        part = lax.dot_general(
            jnp.concatenate(spread, axis=1),
            jnp.concatenate(pick, axis=1),
            (((1,), (1,)), ((), ())),
            preferred_element_type=F32,
        )
        surf_ref[...] += part.reshape(fc, rows, cols)
        return carry

    lax.fori_loop(0, peers // group, step, 0)
    grid_ref[:fc] = surf_ref[...].astype(BF)
    grid_ref[fc:] = state_ref[0, fc:].astype(BF)


def zonal_tables(blocks, cols, waves):
    total = blocks * cols
    b = np.arange(cols)
    n = np.arange(total // 2 // blocks)
    angle = 2.0 * np.pi * ((b[:, None] * n[None, :]) % cols) / cols
    pad = ((0, 0), (0, waves - len(n)))
    cos, sin = np.pad(np.cos(angle), pad), np.pad(np.sin(angle), pad)
    ahead = np.concatenate([cos, sin], axis=1)
    back = np.concatenate([cos.T, sin.T], axis=1)
    turn = 2.0 * np.pi * np.arange(blocks)[:, None] * b[None, :] / total
    twiddle = np.stack([np.cos(turn), np.sin(turn)])
    return jnp.asarray(ahead, BF), jnp.asarray(back, BF), jnp.asarray(twiddle, F32)


def zonal_kernel(scale, x_ref, resp_ref, ahead_ref, back_ref, twiddle_ref, out_ref):
    blocks, rows, cols = x_ref.shape
    waves = ahead_ref.shape[1] // 2
    half = math.sqrt(0.5)
    x = [x_ref[h].astype(F32) for h in range(blocks)]
    a = [x[i] + x[i + 4] for i in range(4)]
    b = [x[i] - x[i + 4] for i in range(4)]
    b13, d13 = half * (b[1] + b[3]), half * (b[1] - b[3])
    a02, a13 = a[0] + a[2], a[1] + a[3]
    z1 = (b[0] + d13, -(b[2] + b13))
    z2 = (a[0] - a[2], a[3] - a[1])
    z3 = (b[0] - d13, b[2] - b13)
    z = [(a02 + a13, None), z1, z2, z3, (a02 - a13, None)]
    z += [(re, -im) for re, im in (z3, z2, z1)]
    real, imag = [], []
    for r in range(blocks):
        re, im = z[r]
        ct, st = twiddle_ref[0, r : r + 1, :], twiddle_ref[1, r : r + 1, :]
        if r == 0:
            real.append(re)
        elif im is None:
            real.append(re * ct)
            imag.append(-re * st)
        else:
            real.append(re * ct + im * st)
            imag.append(im * ct - re * st)
    spec = jnp.dot(jnp.concatenate(real + imag, axis=0).astype(BF), ahead_ref[...], preferred_element_type=F32)
    cosine, sine = [], []
    for r in range(blocks):
        own = spec[r * rows : (r + 1) * rows]
        c, s = own[:, :waves], own[:, waves:]
        if r > 0:
            other = spec[(blocks + r - 1) * rows : (blocks + r) * rows]
            c, s = c + other[:, waves:], s - other[:, :waves]
        cosine.append(c * resp_ref[0, r : r + 1, :])
        sine.append(s * resp_ref[1, r : r + 1, :])
    full = jnp.dot(jnp.concatenate(cosine + sine, axis=0).astype(BF), back_ref[...], preferred_element_type=F32)
    u = []
    for r in range(blocks):
        fc = full[r * rows : (r + 1) * rows]
        fs = full[(blocks + r) * rows : (blocks + r + 1) * rows]
        re, im = fc[:, :cols] + fs[:, cols:], fc[:, cols:] - fs[:, :cols]
        ct, st = twiddle_ref[0, r : r + 1, :], twiddle_ref[1, r : r + 1, :]
        u.append((re, None) if r == 0 else (re * ct - im * st, re * st + im * ct))
    even, odd = u[0][0] + u[4][0], u[0][0] - u[4][0]
    p1, q1 = u[1][0] + u[7][0], u[1][1] - u[7][1]
    p2, q2 = u[2][0] + u[6][0], u[2][1] - u[6][1]
    p3, q3 = u[3][0] + u[5][0], u[3][1] - u[5][1]
    m1, n1 = half * (p1 - q1), half * (p1 + q1)
    m3, n3 = half * (p3 - q3), half * (p3 + q3)
    incr = [
        even + p1 + p2 + p3,
        odd + m1 - q2 - n3,
        even - q1 - p2 + q3,
        odd - n1 + q2 + m3,
        even - p1 + p2 - p3,
        odd - m1 - q2 + n3,
        even + q1 - p2 - q3,
        odd + n1 + q2 - m3,
    ]
    for h in range(blocks):
        out_ref[h] = (incr[h] * scale).astype(BF)


def halo(top, bottom):
    count = lax.axis_size("gx")
    odd = lax.axis_index("gx") % 2 == 1
    first = [(i, i ^ 1) for i in range(count)]
    second = []
    for i in range(1, count - 1, 2):
        second += [(i, i + 1), (i + 1, i)]
    got_a = lax.ppermute(jnp.where(odd, top, bottom), "gx", first)
    got_b = lax.ppermute(jnp.where(odd, bottom, top), "gx", second)
    return jnp.where(odd, got_a, got_b), jnp.where(odd, got_b, got_a)


def local(
    state, response, diffusion, land_mask, couple_src, couple_dst, couple_weight, couple_count
):
    levels, rows_dev, cols_dev = (state.shape[1], state.shape[2], state.shape[3])
    groups_x = lax.axis_size("gx")
    groups_y = lax.axis_size("gy")
    peers = groups_x * groups_y
    slots = couple_src.shape[4]
    cols_all = cols_dev * groups_y
    section = lax.axis_index("comp")
    src_idx = couple_src.reshape(peers, slots)
    dst_idx = couple_dst.reshape(peers, slots)
    weight = couple_weight.reshape(peers, slots)
    count = couple_count.reshape(peers)

    outgoing = pl.pallas_call(
        functools.partial(gather_kernel, 8),
        out_shape=jax.ShapeDtypeStruct((peers, FC, slots), BF),
        in_specs=[SMEM, VMEM, VMEM, VMEM],
        out_specs=VMEM,
        compiler_params=PARAMS,
        name="couple_gather",
    )(count, state, src_idx, weight)
    crossed = lax.ppermute(outgoing, "comp", [(0, 1), (1, 0)])
    arrived = lax.all_to_all(crossed, ("gx", "gy"), split_axis=0, concat_axis=0, tiled=True)

    surface, grid_bf = pl.pallas_call(
        functools.partial(scatter_kernel, 8),
        out_shape=(
            jax.ShapeDtypeStruct((FC, rows_dev, cols_dev), F32),
            jax.ShapeDtypeStruct((levels, rows_dev, cols_dev), BF),
        ),
        in_specs=[VMEM, VMEM, VMEM],
        out_specs=(VMEM, VMEM),
        compiler_params=PARAMS,
        name="couple_scatter",
    )(state, arrived, dst_idx)

    circles = lax.all_to_all(grid_bf, "gy", split_axis=0, concat_axis=0, tiled=True)
    waves = 256
    ahead, back, twiddle = zonal_tables(groups_y, cols_dev, waves)
    own = lax.dynamic_slice_in_dim(response[0], lax.axis_index("gy"), 1, 0)
    half = cols_all // 2 // groups_y
    resp = own.reshape(2, half, groups_y).transpose(0, 2, 1)
    resp = jnp.pad(resp, ((0, 0), (0, 0), (0, waves - half)))
    incr = pl.pallas_call(
        functools.partial(zonal_kernel, 2.0 / cols_all),
        out_shape=jax.ShapeDtypeStruct((groups_y, rows_dev, cols_dev), BF),
        in_specs=[VMEM] * 5,
        out_specs=VMEM,
        compiler_params=PARAMS,
        name="zonal_filter",
    )(circles, resp, ahead, back, twiddle)
    incr = lax.all_to_all(incr, "gy", split_axis=0, concat_axis=0, tiled=True)

    fields = jnp.concatenate([surface, state[0, FC:]], axis=0) + incr.astype(F32)
    low, high = halo(fields[:, 0].astype(BF), fields[:, -1].astype(BF))
    padded = jnp.concatenate([low[:, None].astype(F32), fields, high[:, None].astype(F32)], axis=1)
    keep = jnp.where(section == 1, land_mask.astype(F32), jnp.float32(1.0))
    rate = diffusion[0][None]
    fields = fields + rate * (padded[:, 2:] + padded[:, :-2] - 2.0 * fields)
    return (fields * keep[None])[None]


def solution(mesh):
    return jax.shard_map(
        local,
        mesh=mesh,
        in_specs=(
            P("comp", None, "gx", "gy"),
            P("comp", None, None),
            P("comp", "gx", "gy"),
            P("gx", "gy"),
            P("comp", "gx", "gy", None, None),
            P("comp", "gx", "gy", None, None),
            P("comp", "gx", "gy", None, None),
            P("comp", "gx", "gy", None),
        ),
        out_specs=P("comp", None, "gx", "gy"),
        check_vma=False,
    )
```

time: 342 us -> 81.3 us (0.24)
  other arithmetic: 186 us -> 0.89 us
  local copies, waits for them, and re-layouts: 83.1 us -> 3.72 us
  blocking collectives: 0 us -> 26.6 us
  starting transfers between devices: 33.6 us -> 11.2 us
  matrix products: 16.8 us -> 0 us
  Pallas kernels: 0 us -> 15.2 us
    scatter-add x1 -> x0, other arithmetic: 83.3 us -> none  [local(): surface = surface.at[:, dst_idx].add(incoming)]
    another operation x1 -> x0, other arithmetic: 79.5 us -> none
    gather x2 -> x0, local copies, waits for them, and re-layouts: 62.3 us -> none  [local(): outgoing = jnp.transpose(surface[:, src_idx] * weights[None], (1, 0, 2))]
    all_to_all x0 -> x1, blocking collectives: none -> 26.6 us  [local(): lax.all_to_all(crossed, ('gx', 'gy'), split_axis=0, concat_axis=0, tiled=...]
    all_to_all x3 -> x2, starting transfers between devices: 25.6 us -> 6.89 us  [the longest x1 3.51 us: local(): lax.all_to_all(grid_bf, 'gy', split_axis=0, concat_axis=0, tiled=True)]
    unnamed x1 -> x0, other arithmetic: 17 us -> none
    dot_general x2 -> x0, matrix products: 16.8 us -> none  [the longest x1 9.03 us: back_transform(): lax.dot_general(filtered, table_part, (((1,), (1,)), ((), ())), preferred...]
    pallas_call x0 -> x3, Pallas kernels: none -> 15.2 us  [the longest x1 7.03 us: local(): pl.pallas_call(functools.partial(gather_kernel, 8), out_shape=jax.ShapeDt...]
  transfers between devices with their start and end apart: 6 -> 5, of which waited for: 4 -> 5; matrix products, arithmetic and copies ran while one was open for 24% -> 0% of each run, Pallas kernels for 0% -> 0%
where the time goes in v1:
time: 81.3 us; the launch traced here: 80.8 us
  blocking collectives  26.6 us (33%)
  waiting for transfers between devices  22.9 us (28%)
  Pallas kernels  15.2 us (19%)
  starting transfers between devices  11.2 us (14%)
  local copies, waits for them, and re-layouts  3.72 us (5%)
  other arithmetic  0.89 us (1%)
    all_to_all x1, blocking collectives, local(): lax.all_to_all(crossed, ('gx', 'gy'), split_axis=0, concat_axis=0, tiled=...  26.6 us
    all_to_all x1, waiting for transfers between devices, local(): incr = lax.all_to_all(incr, 'gy', split_axis=0, concat_axis=0, tiled=True)  9.14 us
    all_to_all x1, waiting for transfers between devices, local(): lax.all_to_all(grid_bf, 'gy', split_axis=0, concat_axis=0, tiled=True)  8.86 us
    pallas_call x1, Pallas kernels, local(): pl.pallas_call(functools.partial(gather_kernel, 8), out_shape=jax.ShapeDt...  7.03 us
    pallas_call x1, Pallas kernels, local(): pl.pallas_call(functools.partial(scatter_kernel, 8), out_shape=(jax.Shape...  6.75 us
    ppermute x1, starting transfers between devices, halo(): got_b = lax.ppermute(jnp.where(odd, bottom, top), 'gx', second)  4.14 us
    all_to_all x1, starting transfers between devices, local(): lax.all_to_all(grid_bf, 'gy', split_axis=0, concat_axis=0, tiled=True)  3.51 us
    all_to_all x1, starting transfers between devices, local(): incr = lax.all_to_all(incr, 'gy', split_axis=0, concat_axis=0, tiled=True)  3.38 us
  transfers between devices with their start and end apart: 5, of which 5 were waited for; matrix products, arithmetic and copies ran while one was open for 0% of the time, Pallas kernels for 0%

profile of v1, /device:TPU:2, one launch (start us, length us, event | category | flops | bytes accessed | tf_op | source)
XLA Modules:
  0.0 80.8 jit_solution(6623138357302773962)
XLA Ops:
  0.0 0.0 copy-start
  0.0 0.0 copy-start.9
  0.0 0.7 copy-done.9
  0.7 0.0 copy-start.1
  0.7 1.0 %copy-done.1 = f32[1,8,24,384]{3,2,1,0:T(8,128)S(1)} copy-done((f32[1,8,24,384]{3,2,1,0:T(8,128)S(1)}, f32[1,8,24,384]{3,2,1,0:T(8,128)}, u32[]{:S(2)}) %copy-start.1) | copy-done | bytes 294936
  1.7 0.0 copy-start.5
  1.7 0.8 %copy-done.5 = s32[1,1,1,128,128]{4,3,2,1,0:T(8,128)S(1)} copy-done((s32[1,1,1,128,128]{4,3,2,1,0:T(8,128)S(1)}, s32[1,1,1,128,128]{4,3,2,1,0:T(8,128)}, u32[]{:S(2)}) %copy-start.5) | copy-done | bytes 65560
  2.5 0.0 copy-start.6
  2.5 0.8 %copy-done.6 = f32[1,1,1,128,128]{4,3,2,1,0:T(8,128)S(1)} copy-done((f32[1,1,1,128,128]{4,3,2,1,0:T(8,128)S(1)}, f32[1,1,1,128,128]{4,3,2,1,0:T(8,128)}, u32[]{:S(2)}) %copy-start.6) | copy-done | bytes 65560
  3.3 0.0 copy-start.2
  3.3 7.0 %couple_gather.1 = bf16[128,4,128]{2,1,0:T(4,128)(2,1)S(1)} custom-call(s32[128]{0:T(128)S(1)} %bitcast.20, f32[1,8,24,384]{3,2,1,0:T(8,128)S(1)} %copy-done.1, s32[128,128]{1,0:T(8,128)S(1)} %bitcast.17, f32[128,128]{1,0:T(8,128)S(1)} %bitcast.18), custom_call_target="tpu_custom_call" | custom-call | tf_op jit(solution)/shard_map/couple_gather/pallas_call | solution.py:187
  10.4 0.0 copy-start.7
  10.4 0.1 collective-permute-start
  10.5 1.3 %collective-permute-done = bf16[128,4,128]{2,1,0:T(4,128)(2,1)S(1)} collective-permute-done((bf16[128,4,128]{2,1,0:T(4,128)(2,1)S(1)}, bf16[128,4,128]{2,1,0:T(4,128)(2,1)S(1)}, u32[]{:S(2)}, u32[]{:S(2)}) %collective-permute-start) | collective-permute-done | bytes 131104 | tf_op jit(solution)/shard_map/ppermute | solution.py:195
  11.8 26.6 %all_to_all.15.arrived_ref = bf16[128,4,128]{2,1,0:T(4,128)(2,1)S(1)} all-to-all(bf16[128,4,128]{2,1,0:T(4,128)(2,1)S(1)} %collective-permute-done), channel_id=1, replica_groups=mesh['comp'=2,'gx'=16,'gy'=8] {'gx','gy'}, dimensions={0} | all-to-all | bytes 262144 | tf_op jit(solution)/shard_map/all_to_all | solution.py:196
  38.5 0.0 copy-done.2
  38.5 0.0 copy-done.7
  38.5 0.0 copy-start.8
  38.5 6.7 %couple_scatter.1 = (f32[4,24,384]{2,1,0:T(8,128)S(1)}, bf16[8,24,384]{2,1,0:T(8,128)(2,1)}) custom-call(f32[1,8,24,384]{3,2,1,0:T(8,128)S(1)} %copy-done.2, bf16[128,4,128]{2,1,0:T(4,128)(2,1)S(1)} %all_to_all.15.arrived_ref, s32[128,128]{1,0:T(8,128)S(1)} %bitcast.19), custom_call_target="tpu_custom_call" | custom-call | tf_op jit(solution)/shard_map/couple_scatter/pallas_call | solution.py:198
  45.2 0.0 copy-start.3
  45.2 0.0 copy-start.4
  45.2 3.5 %all-to-all-start.1 = ((bf16[8,24,384]{2,1,0:T(8,128)(2,1)}), bf16[8,24,384]{2,1,0:T(8,128)(2,1)S(1)}, u32[]{:S(2)}, u32[]{:S(2)}) async-start(bf16[8,24,384]{2,1,0:T(8,128)(2,1)} %get-tuple-element.8), calls=%async_computation.1 | async-start | bytes 294912 | tf_op jit(solution)/shard_map/all_to_all | solution.py:210
  48.8 0.0 copy-done
  48.8 0.1 reshape.32
  48.9 0.1 copy.14
  49.0 8.9 %all-to-all-done.1.x_ref = bf16[8,24,384]{2,1,0:T(8,128)(2,1)S(1)} async-done(((bf16[8,24,384]{2,1,0:T(8,128)(2,1)}), bf16[8,24,384]{2,1,0:T(8,128)(2,1)S(1)}, u32[]{:S(2)}, u32[]{:S(2)}) %all-to-all-start.1) | async-done | bytes 147488 | tf_op jit(solution)/shard_map/all_to_all | solution.py:210
  57.9 0.0 copy-done.8
  57.9 0.0 copy-done.3
  57.9 0.0 copy-done.4
  57.9 1.4 %zonal_filter.1 = bf16[8,24,384]{2,1,0:T(8,128)(2,1)} custom-call(bf16[8,24,384]{2,1,0:T(8,128)(2,1)S(1)} %all-to-all-done.1.x_ref, f32[2,8,256]{2,1,0:T(8,128)S(1)} %pad.4.resp_ref, bf16[384,512]{1,0:T(8,128)(2,1)S(1)} %copy-done.3, bf16[256,768]{1,0:T(8,128)(2,1)S(1)} %copy-done.4, f32[2,8,384]{2,1,0:T(8,128)S(1)} %copy-done.8), custom_call_target="tpu_custom_call" | custom-call | tf_op jit(solution)/shard_map/zonal_filter/pallas_call | solution.py:217
  59.4 3.4 %all-to-all-start.2 = ((bf16[8,24,384]{2,1,0:T(8,128)(2,1)}), bf16[8,24,384]{2,1,0:T(8,128)(2,1)S(1)}, u32[]{:S(2)}, u32[]{:S(2)}) async-start(bf16[8,24,384]{2,1,0:T(8,128)(2,1)} %zonal_filter.1), calls=%async_computation.2 | async-start | bytes 294912 | tf_op jit(solution)/shard_map/all_to_all | solution.py:225
  62.8 9.1 %all-to-all-done.2 = bf16[8,24,384]{2,1,0:T(8,128)(2,1)S(1)} async-done(((bf16[8,24,384]{2,1,0:T(8,128)(2,1)}), bf16[8,24,384]{2,1,0:T(8,128)(2,1)S(1)}, u32[]{:S(2)}, u32[]{:S(2)}) %all-to-all-start.2) | async-done | bytes 147488 | tf_op jit(solution)/shard_map/all_to_all | solution.py:225
  71.9 0.0 copy-start.10
  72.0 0.1 copy.18
  72.0 4.1 %collective-permute-start.1 = (bf16[8,384]{1,0:T(8,128)(2,1)S(1)}, bf16[8,384]{1,0:T(8,128)(2,1)S(1)}, u32[]{:S(2)}, u32[]{:S(2)}) collective-permute-start(bf16[8,384]{1,0:T(8,128)(2,1)S(1)} %get-tuple-element.9), channel_id=1, source_target_pairs={{8,16},{16,8},{24,32},{32,24},{40,48},{48,40},{56,64},{64,56},{72,... | collective-permute-start | bytes 18440 | tf_op jit(solution)/shard_map/ppermute | solution.py:168
  76.2 0.1 collective-permute-start.2
  76.3 0.0 copy-done.10
  76.3 0.0 copy-start.11
  76.3 3.3 %collective-permute-done.1 = bf16[8,384]{1,0:T(8,128)(2,1)S(1)} collective-permute-done((bf16[8,384]{1,0:T(8,128)(2,1)S(1)}, bf16[8,384]{1,0:T(8,128)(2,1)S(1)}, u32[]{:S(2)}, u32[]{:S(2)}) %collective-permute-start.1) | collective-permute-done | bytes 6176 | tf_op jit(solution)/shard_map/ppermute | solution.py:168
  79.7 0.2 collective-permute-done.2
  79.9 0.0 copy-done.11
  79.9 0.8 %fusion.5 = f32[1,8,24,384]{3,2,1,0:T(8,128)} fusion(f32[8,24,384]{2,1,0:T(8,128)S(1)} %maximum_add_fusion, f32[8,1,384]{2,1,0:T(1,128)S(1)} %reshape.34, f32[8,1,384]{2,1,0:T(1,128)S(1)} %copy.16, f32[24,384]{1,0:T(8,128)S(1)} %convert_select_fusion, f32[24,384]{1,0:T(8,128)S(1)} %bitcast.22), kind=kLoop, calls=%fused_computation.6 | loop fusion | flops 589824 | bytes 688128 | tf_op jit(solution)/shard_map/broadcast_in_dim | solution.py:233
  (9 shorter events, 0.1 us)
Async XLA Ops:
  0.0 48.8 %copy-start = (f32[1,8,3072]{2,1,0:T(8,128)S(1)}, f32[1,8,3072]{2,1,0:T(8,128)}, u32[]{:S(2)}) copy-start(f32[1,8,3072]{2,1,0:T(8,128)} %param.12) | copy-start | bytes 294916
  0.0 0.7 copy-start.9
  0.7 1.0 %copy-start.1 = (f32[1,8,24,384]{3,2,1,0:T(8,128)S(1)}, f32[1,8,24,384]{3,2,1,0:T(8,128)}, u32[]{:S(2)}) copy-start(f32[1,8,24,384]{3,2,1,0:T(8,128)} %state_ref.1) | copy-start | bytes 884740
  1.7 0.8 %copy-start.5 = (s32[1,1,1,128,128]{4,3,2,1,0:T(8,128)S(1)}, s32[1,1,1,128,128]{4,3,2,1,0:T(8,128)}, u32[]{:S(2)}) copy-start(s32[1,1,1,128,128]{4,3,2,1,0:T(8,128)} %param.15) | copy-start | bytes 196612
  2.5 0.8 %copy-start.6 = (f32[1,1,1,128,128]{4,3,2,1,0:T(8,128)S(1)}, f32[1,1,1,128,128]{4,3,2,1,0:T(8,128)}, u32[]{:S(2)}) copy-start(f32[1,1,1,128,128]{4,3,2,1,0:T(8,128)} %param.17) | copy-start | bytes 196612
  3.3 35.1 %copy-start.2 = (f32[1,8,24,384]{3,2,1,0:T(8,128)S(1)}, f32[1,8,24,384]{3,2,1,0:T(8,128)}, u32[]{:S(2)}) copy-start(f32[1,8,24,384]{3,2,1,0:T(8,128)} %state_ref.1) | copy-start | bytes 884740
  10.4 28.1 %copy-start.7 = (s32[1,1,1,128,128]{4,3,2,1,0:T(8,128)S(1)}, s32[1,1,1,128,128]{4,3,2,1,0:T(8,128)}, u32[]{:S(2)}) copy-start(s32[1,1,1,128,128]{4,3,2,1,0:T(8,128)} %param.16) | copy-start | bytes 196612
  10.4 1.4 %collective-permute-start = (bf16[128,4,128]{2,1,0:T(4,128)(2,1)S(1)}, bf16[128,4,128]{2,1,0:T(4,128)(2,1)S(1)}, u32[]{:S(2)}, u32[]{:S(2)}) collective-permute-start(bf16[128,4,128]{2,1,0:T(4,128)(2,1)S(1)} %couple_gather.1), channel_id=1, source_target_pairs={{0,128},{128,0},{1,129},{129,1},{2,130},{130,2},{3,131},{131,3},{4... | collective-permute-start | bytes 393224 | tf_op jit(solution)/shard_map/ppermute | solution.py:195
  38.5 19.4 %copy-start.8 = (f32[2,8,384]{2,1,0:T(8,128)S(1)}, f32[2,8,384]{2,1,0:T(8,128)}, u32[]{:S(2)}) copy-start(f32[2,8,384]{2,1,0:T(8,128)} %constant.46.clone.twiddle_ref) | copy-start | bytes 73732
  45.2 12.7 %copy-start.3 = (bf16[384,512]{1,0:T(8,128)(2,1)S(1)}, bf16[384,512]{1,0:T(8,128)(2,1)}, u32[]{:S(2)}) copy-start(bf16[384,512]{1,0:T(8,128)(2,1)} %constant.44.clone.ahead_ref) | copy-start | bytes 1179652
  45.2 12.7 %copy-start.4 = (bf16[256,768]{1,0:T(8,128)(2,1)S(1)}, bf16[256,768]{1,0:T(8,128)(2,1)}, u32[]{:S(2)}) copy-start(bf16[256,768]{1,0:T(8,128)(2,1)} %constant.45.clone.back_ref) | copy-start | bytes 1179652
  45.2 12.7 %all-to-all-start.1 = ((bf16[8,24,384]{2,1,0:T(8,128)(2,1)}), bf16[8,24,384]{2,1,0:T(8,128)(2,1)S(1)}, u32[]{:S(2)}, u32[]{:S(2)}) async-start(bf16[8,24,384]{2,1,0:T(8,128)(2,1)} %get-tuple-element.8), calls=%async_computation.1 | async-start | bytes 294912 | tf_op jit(solution)/shard_map/all_to_all | solution.py:210
  59.4 12.6 %all-to-all-start.2 = ((bf16[8,24,384]{2,1,0:T(8,128)(2,1)}), bf16[8,24,384]{2,1,0:T(8,128)(2,1)S(1)}, u32[]{:S(2)}, u32[]{:S(2)}) async-start(bf16[8,24,384]{2,1,0:T(8,128)(2,1)} %zonal_filter.1), calls=%async_computation.2 | async-start | bytes 294912 | tf_op jit(solution)/shard_map/all_to_all | solution.py:225
  71.9 4.3 %copy-start.10 = (s32[24,384]{1,0:T(8,128)S(1)}, s32[24,384]{1,0:T(8,128)}, u32[]{:S(2)}) copy-start(s32[24,384]{1,0:T(8,128)} %param.14) | copy-start | bytes 110596
  72.0 7.6 %collective-permute-start.1 = (bf16[8,384]{1,0:T(8,128)(2,1)S(1)}, bf16[8,384]{1,0:T(8,128)(2,1)S(1)}, u32[]{:S(2)}, u32[]{:S(2)}) collective-permute-start(bf16[8,384]{1,0:T(8,128)(2,1)S(1)} %get-tuple-element.9), channel_id=1, source_target_pairs={{8,16},{16,8},{24,32},{32,24},{40,48},{48,40},{56,64},{64,56},{72,... | collective-permute-start | bytes 18440 | tf_op jit(solution)/shard_map/ppermute | solution.py:168
  76.2 3.7 %collective-permute-start.2 = (bf16[8,384]{1,0:T(8,128)(2,1)S(1)}, bf16[8,384]{1,0:T(8,128)(2,1)S(1)}, u32[]{:S(2)}, u32[]{:S(2)}) collective-permute-start(bf16[8,384]{1,0:T(8,128)(2,1)S(1)} %get-tuple-element.10), channel_id=1, source_target_pairs={{0,8},{8,0},{16,24},{24,16},{32,40},{40,32},{48,56},{56,48},{64,72... | collective-permute-start | bytes 18440 | tf_op jit(solution)/shard_map/ppermute | solution.py:167
  76.3 3.6 %copy-start.11 = (f32[1,24,384]{2,1,0:T(8,128)S(1)}, f32[1,24,384]{2,1,0:T(8,128)}, u32[]{:S(2)}) copy-start(f32[1,24,384]{2,1,0:T(8,128)} %param.13) | copy-start | bytes 110596

commit v2 on v1

v2 whole, which is shorter than its diff:
```python
import functools
import math

import jax
import jax.numpy as jnp
import numpy as np
from jax import lax
from jax.experimental import pallas as pl
from jax.experimental.pallas import tpu as pltpu
from jax.sharding import PartitionSpec as P

FC = 4
LANES = 128
BF = jnp.bfloat16
F32 = jnp.float32
VMEM = pl.BlockSpec(memory_space=pltpu.VMEM)
SMEM = pl.BlockSpec(memory_space=pltpu.SMEM)
PARAMS = pltpu.CompilerParams(vmem_limit_bytes=32 * 2**20)


def one_hot(rows, index):
    spot = lax.broadcasted_iota(jnp.int32, (rows, index.shape[1]), 0)
    return jnp.where(spot == index, 1.0, 0.0)


def split_cell(idx, cols):
    row = (idx.astype(F32) * (1.0 / cols) + 0.5 / cols).astype(jnp.int32)
    return row, idx - row * cols


def tiles(block):
    return jnp.concatenate([block[:, t : t + LANES] for t in range(0, block.shape[1], LANES)], axis=0)


def untile(block, rows):
    return jnp.concatenate([block[t : t + rows] for t in range(0, block.shape[0], rows)], axis=1)


def pack_kernel(split, state_ref, dst_ref, out_ref):
    _, levels, rows, cols = state_ref.shape
    peers, slots = dst_ref.shape
    groups = peers // levels
    for h in range(levels):
        idx = dst_ref[pl.ds(h, groups, stride=levels), :]
        row, col = split_cell(idx, cols)
        tile = col // LANES
        line = (tile * rows + row).astype(F32).astype(BF)
        lane = (col - tile * LANES).astype(F32).astype(BF)
        u, other = h // split, h % split
        for v in range(split):
            piece = u * split + v
            out_ref[piece, pl.ds(other * groups, groups), :] = line
            out_ref[piece, pl.ds((split + other) * groups, groups), :] = lane
        out_ref[h, pl.ds(2 * split * groups, rows * cols // LANES), :] = tiles(state_ref[0, h]).astype(BF)


def gather_kernel(split, blocks, count_ref, surf_ref, src_ref, weight_ref, pick_ref, out_ref):
    _, _, rows, cols = surf_ref.shape
    peers, slots = src_ref.shape
    fc = split * out_ref.shape[1] // blocks
    each = fc // split * blocks
    surface = surf_ref[0, :fc].reshape(fc * rows, cols).astype(BF)
    lane = lax.broadcasted_iota(jnp.int32, (blocks, slots), 1)
    sub = lax.broadcasted_iota(jnp.int32, (blocks, slots), 0)

    def step(g, carry):
        base = pl.multiple_of(g * blocks, blocks)
        row, col = split_cell(src_ref[pl.ds(base, blocks), :], cols)
        found = []
        for i in range(0, blocks, 2):
            pick = jnp.concatenate([one_hot(cols, col[j : j + 1]) for j in (i, i + 1)], axis=1)
            lines = jnp.dot(surface, pick.astype(BF), preferred_element_type=F32)
            for j in range(2):
                mask = one_hot(rows, row[i + j : i + j + 1])
                own = lines[:, j * slots : (j + 1) * slots].reshape(fc, rows, slots)
                found.append((own * mask[None]).reshape(fc * rows, slots))
        value = jnp.dot(pick_ref[...], jnp.concatenate(found, axis=0).astype(BF), preferred_element_type=F32)
        limit = jnp.zeros((blocks, slots), jnp.int32)
        for i in range(blocks):
            limit = jnp.where(sub == i, count_ref[base + i], limit)
        weight = jnp.where(lane < limit, weight_ref[pl.ds(base, blocks), :], 0.0)
        value = value * jnp.concatenate([weight] * fc, axis=0)
        for v in range(split):
            out_ref[g * split + v] = value[v * each : (v + 1) * each].astype(BF)
        return carry

    lax.fori_loop(0, peers // blocks, step, 0)


def band_kernel(
    split, scale, arrived_ref, early_ref, resp_ref, ahead_ref, back_ref, twiddle_ref, out_ref, value_ref, line_ref, lane_ref, acc_ref
):
    senders, each, slots = arrived_ref.shape
    blocks = early_ref.shape[0]
    fields = each // blocks
    groups = senders // split
    rows, cols = out_ref.shape[2], out_ref.shape[3]
    cell_rows = rows * cols // LANES
    for s in range(senders):
        value_ref[s] = arrived_ref[s].astype(F32)
    for h in range(blocks):
        line_ref[h] = early_ref[h, :senders].astype(F32).astype(jnp.int32)
        lane_ref[h] = early_ref[h, senders : 2 * senders].astype(F32).astype(jnp.int32)
    acc_ref[...] = jnp.zeros_like(acc_ref)

    def step(g, carry):
        for h in range(blocks):
            spread, pick = [], []
            for v in range(split):
                at = v * groups + g
                mask = lax.broadcasted_iota(jnp.int32, (cell_rows, slots), 0) == line_ref[h, pl.ds(at, 1), :]
                vals = [
                    jnp.where(mask, value_ref[g * split + v, c * blocks + h : c * blocks + h + 1, :], 0.0)
                    for c in range(fields)
                ]
                spread.append(jnp.concatenate(vals, axis=0).astype(BF))
                pick.append(one_hot(LANES, lane_ref[h, pl.ds(at, 1), :]).astype(BF))
            acc_ref[h] += lax.dot_general(
                jnp.concatenate(spread, axis=1),
                jnp.concatenate(pick, axis=1),
                (((1,), (1,)), ((), ())),
                preferred_element_type=F32,
            )
        return carry

    lax.fori_loop(0, groups, step, 0)
    for c in range(fields + 1):
        if c < fields:
            x = [untile(acc_ref[h, c * cell_rows : (c + 1) * cell_rows], rows) for h in range(blocks)]
        else:
            x = [untile(early_ref[h, 2 * senders :].astype(F32), rows) for h in range(blocks)]
        incr = zonal_rows(x, resp_ref.at[c], ahead_ref, back_ref, twiddle_ref)
        for h in range(blocks):
            total = incr[h] * scale
            if c < fields:
                total = total + untile(acc_ref[h, c * cell_rows : (c + 1) * cell_rows], rows)
            out_ref[h, c] = total.astype(BF)


def sum_kernel(split, odd_ref, state_ref, back_ref, fields_ref, first_ref, second_ref):
    _, levels, rows, _ = state_ref.shape
    each = back_ref.shape[1] - 1
    tops, bottoms = [], []
    for c in range(levels):
        total = state_ref[0, c] + back_ref[c, each].astype(F32)
        if c < split * each:
            for u in range(levels // split):
                total = total + back_ref[u * split + c // each, c % each].astype(F32)
        fields_ref[c] = total
        tops.append(total[:1])
        bottoms.append(total[rows - 1 :])
    top, bottom = jnp.concatenate(tops, axis=0), jnp.concatenate(bottoms, axis=0)
    odd = odd_ref[0] == 1
    first_ref[...] = jnp.where(odd, top, bottom).astype(BF)
    second_ref[...] = jnp.where(odd, bottom, top).astype(BF)


def diffuse_kernel(flag_ref, fields_ref, first_ref, second_ref, rate_ref, land_ref, out_ref):
    levels, rows, cols = fields_ref.shape
    odd = flag_ref[0] == 1
    first, second = first_ref[...].astype(F32), second_ref[...].astype(F32)
    low, high = jnp.where(odd, first, second), jnp.where(odd, second, first)
    keep = jnp.where(flag_ref[1] == 1, land_ref[...].astype(F32), 1.0)
    rate = rate_ref[0] * keep
    for c in range(levels):
        own = fields_ref[c]
        above = jnp.concatenate([low[c : c + 1], own[: rows - 1]], axis=0)
        below = jnp.concatenate([own[1:], high[c : c + 1]], axis=0)
        out_ref[0, c] = own * keep + rate * (above + below - 2.0 * own)


def zonal_tables(blocks, cols, waves):
    total = blocks * cols
    b = np.arange(cols)
    n = np.arange(total // 2 // blocks)
    angle = 2.0 * np.pi * ((b[:, None] * n[None, :]) % cols) / cols
    pad = ((0, 0), (0, waves - len(n)))
    cos, sin = np.pad(np.cos(angle), pad), np.pad(np.sin(angle), pad)
    ahead = np.concatenate([cos, sin], axis=1)
    back = np.concatenate([cos.T, sin.T], axis=1)
    turn = 2.0 * np.pi * np.arange(blocks)[:, None] * b[None, :] / total
    twiddle = np.stack([np.cos(turn), np.sin(turn)])
    return jnp.asarray(ahead, BF), jnp.asarray(back, BF), jnp.asarray(twiddle, F32)


def zonal_rows(x, resp, ahead_ref, back_ref, twiddle_ref):
    blocks = len(x)
    rows, cols = x[0].shape
    waves = ahead_ref.shape[1] // 2
    half = math.sqrt(0.5)
    a = [x[i] + x[i + 4] for i in range(4)]
    b = [x[i] - x[i + 4] for i in range(4)]
    b13, d13 = half * (b[1] + b[3]), half * (b[1] - b[3])
    a02, a13 = a[0] + a[2], a[1] + a[3]
    z1 = (b[0] + d13, -(b[2] + b13))
    z2 = (a[0] - a[2], a[3] - a[1])
    z3 = (b[0] - d13, b[2] - b13)
    z = [(a02 + a13, None), z1, z2, z3, (a02 - a13, None)]
    z += [(re, -im) for re, im in (z3, z2, z1)]
    real, imag = [], []
    for r in range(blocks):
        re, im = z[r]
        ct, st = twiddle_ref[0, r : r + 1, :], twiddle_ref[1, r : r + 1, :]
        if r == 0:
            real.append(re)
        elif im is None:
            real.append(re * ct)
            imag.append(-re * st)
        else:
            real.append(re * ct + im * st)
            imag.append(im * ct - re * st)
    spec = jnp.dot(jnp.concatenate(real + imag, axis=0).astype(BF), ahead_ref[...], preferred_element_type=F32)
    cosine, sine = [], []
    for r in range(blocks):
        own = spec[r * rows : (r + 1) * rows]
        c, s = own[:, :waves], own[:, waves:]
        if r > 0:
            other = spec[(blocks + r - 1) * rows : (blocks + r) * rows]
            c, s = c + other[:, waves:], s - other[:, :waves]
        cosine.append(c * resp[0, r : r + 1, :])
        sine.append(s * resp[1, r : r + 1, :])
    full = jnp.dot(jnp.concatenate(cosine + sine, axis=0).astype(BF), back_ref[...], preferred_element_type=F32)
    u = []
    for r in range(blocks):
        fc = full[r * rows : (r + 1) * rows]
        fs = full[(blocks + r) * rows : (blocks + r + 1) * rows]
        re, im = fc[:, :cols] + fs[:, cols:], fc[:, cols:] - fs[:, :cols]
        ct, st = twiddle_ref[0, r : r + 1, :], twiddle_ref[1, r : r + 1, :]
        u.append((re, None) if r == 0 else (re * ct - im * st, re * st + im * ct))
    even, odd = u[0][0] + u[4][0], u[0][0] - u[4][0]
    p1, q1 = u[1][0] + u[7][0], u[1][1] - u[7][1]
    p2, q2 = u[2][0] + u[6][0], u[2][1] - u[6][1]
    p3, q3 = u[3][0] + u[5][0], u[3][1] - u[5][1]
    m1, n1 = half * (p1 - q1), half * (p1 + q1)
    m3, n3 = half * (p3 - q3), half * (p3 + q3)
    return [
        even + p1 + p2 + p3,
        odd + m1 - q2 - n3,
        even - q1 - p2 + q3,
        odd - n1 + q2 + m3,
        even - p1 + p2 - p3,
        odd - m1 - q2 + n3,
        even + q1 - p2 - q3,
        odd + n1 + q2 - m3,
    ]


def local(
    state, response, diffusion, land_mask, couple_src, couple_dst, couple_weight, couple_count
):
    levels, rows, cols = (state.shape[1], state.shape[2], state.shape[3])
    groups_x, split = lax.axis_size("gx"), lax.axis_size("gv")
    blocks = lax.axis_size("gu") * split
    peers = groups_x * blocks
    slots = couple_src.shape[4]
    cols_all = cols * blocks
    senders = groups_x * split
    each = FC // split
    cell_rows = rows * cols // LANES
    waves = 256
    gv = lax.axis_index("gv")
    own = lax.axis_index("gu") * split + gv
    src_idx = couple_src.reshape(peers, slots)
    dst_idx = couple_dst.reshape(peers, slots)
    weight = couple_weight.reshape(peers, slots)
    count = couple_count.reshape(peers)

    early = pl.pallas_call(
        functools.partial(pack_kernel, split),
        out_shape=jax.ShapeDtypeStruct((blocks, 2 * senders + cell_rows, LANES), BF),
        in_specs=[VMEM, VMEM],
        out_specs=VMEM,
        compiler_params=PARAMS,
        name="early_pack",
    )(state, dst_idx)
    early = lax.all_to_all(early, ("gu", "gv"), split_axis=0, concat_axis=0, tiled=True)

    spot = np.zeros((FC, blocks, blocks, FC, rows), np.float32)
    for c in range(FC):
        for h in range(blocks):
            spot[c, h, h, c] = 1.0
    outgoing = pl.pallas_call(
        functools.partial(gather_kernel, split, blocks),
        out_shape=jax.ShapeDtypeStruct((senders, each * blocks, slots), BF),
        in_specs=[SMEM, VMEM, VMEM, VMEM, VMEM],
        out_specs=VMEM,
        compiler_params=PARAMS,
        cost_estimate=pl.CostEstimate(flops=4 * 10**9, bytes_accessed=16 * 10**6, transcendentals=0),
        name="couple_gather",
    )(count, state, src_idx, weight, jnp.asarray(spot.reshape(FC * blocks, -1), BF))
    outgoing, early = lax.optimization_barrier((outgoing, early))
    crossed = lax.ppermute(outgoing, "comp", [(0, 1), (1, 0)])
    arrived = lax.all_to_all(crossed, ("gx", "gv"), split_axis=0, concat_axis=0, tiled=True)

    ahead, back, twiddle = zonal_tables(blocks, cols, waves)
    half = cols_all // 2 // blocks
    resp = jnp.concatenate(
        [lax.dynamic_slice_in_dim(response[0], gv * each, each, 0), lax.dynamic_slice_in_dim(response[0], own, 1, 0)], axis=0
    )
    resp = resp.reshape(each + 1, 2, half, blocks).transpose(0, 1, 3, 2)
    resp = jnp.pad(resp, ((0, 0), (0, 0), (0, 0), (0, waves - half)))
    incr = pl.pallas_call(
        functools.partial(band_kernel, split, 2.0 / cols_all),
        out_shape=jax.ShapeDtypeStruct((blocks, each + 1, rows, cols), BF),
        in_specs=[VMEM] * 6,
        out_specs=VMEM,
        scratch_shapes=[
            pltpu.VMEM((senders, each * blocks, slots), F32),
            pltpu.VMEM((blocks, senders, slots), jnp.int32),
            pltpu.VMEM((blocks, senders, slots), jnp.int32),
            pltpu.VMEM((blocks, each * cell_rows, LANES), F32),
        ],
        compiler_params=PARAMS,
        name="band_filter",
    )(arrived, early, resp, ahead, back, twiddle)
    incr = lax.all_to_all(incr, ("gu", "gv"), split_axis=0, concat_axis=0, tiled=True)

    odd = lax.axis_index("gx") % 2
    flag = jnp.stack([odd, lax.axis_index("comp")])
    edge = jax.ShapeDtypeStruct((levels, cols), BF)
    fields, first, second = pl.pallas_call(
        functools.partial(sum_kernel, split),
        out_shape=(jax.ShapeDtypeStruct((levels, rows, cols), F32), edge, edge),
        in_specs=[SMEM, VMEM, VMEM],
        out_specs=(VMEM, VMEM, VMEM),
        compiler_params=PARAMS,
        name="partial_sum",
    )(flag, state, incr)
    pairs = [(i, i ^ 1) for i in range(groups_x)]
    cross = [pair for i in range(1, groups_x - 1, 2) for pair in ((i, i + 1), (i + 1, i))]
    first = lax.ppermute(first, "gx", pairs)
    second = lax.ppermute(second, "gx", cross)
    return pl.pallas_call(
        diffuse_kernel,
        out_shape=jax.ShapeDtypeStruct((1, levels, rows, cols), F32),
        in_specs=[SMEM] + [VMEM] * 5,
        out_specs=VMEM,
        compiler_params=PARAMS,
        name="diffuse",
    )(flag, fields, first, second, diffusion, land_mask)


def solution(mesh):
    shape = mesh.devices.shape
    mesh = jax.sharding.Mesh(mesh.devices.reshape(shape[0], shape[1], shape[2] // 2, 2), ("comp", "gx", "gu", "gv"))
    gy = ("gu", "gv")
    return jax.shard_map(
        local,
        mesh=mesh,
        in_specs=(
            P("comp", None, "gx", gy),
            P("comp", None, None),
            P("comp", "gx", gy),
            P("gx", gy),
            P("comp", "gx", gy, None, None),
            P("comp", "gx", gy, None, None),
            P("comp", "gx", gy, None, None),
            P("comp", "gx", gy, None),
        ),
        out_specs=P("comp", None, "gx", gy),
        check_vma=False,
    )
```

time: 81.3 us -> 78.2 us (0.962)
  blocking collectives: 26.6 us -> 0 us
  starting transfers between devices: 11.2 us -> 26.5 us
  waiting for transfers between devices: 22.9 us -> 27.8 us
  Pallas kernels: 15.2 us -> 20 us
    all_to_all x1 -> x0, blocking collectives: 26.6 us -> none  [local(): lax.all_to_all(crossed, ('gx', 'gy'), split_axis=0, concat_axis=0, tiled=...]
    all_to_all x2 -> x3, starting transfers between devices: 6.89 us -> 21.2 us  [the longest x1 8.61 us: local(): lax.all_to_all(early, ('gu', 'gv'), split_axis=0, concat_axis=0, tiled=True)]
    all_to_all x2 -> x3, waiting for transfers between devices: 18 us -> 23.3 us  [the longest x1 14.6 us: local(): lax.all_to_all(incr, ('gu', 'gv'), split_axis=0, concat_axis=0, tiled=True)]
    pallas_call x3 -> x5, Pallas kernels: 15.2 us -> 20 us  [the longest x1 9.21 us: local(): pl.pallas_call(functools.partial(gather_kernel, split, blocks), out_shape...]
    ppermute x2, starting transfers between devices: 4.23 us -> 5.35 us  [the longest x1 4.64 us: local(): second = lax.ppermute(second, 'gx', cross)]
    unnamed x24 -> x26, local copies, waits for them, and re-layouts: 3.37 us -> 2.49 us
    broadcast_in_dim x1 -> x0, other arithmetic: 0.84 us -> none  [local(): return (fields * keep[None])[None]]
  transfers between devices with their start and end apart: 5 -> 6, of which waited for: 5 -> 5; matrix products, arithmetic and copies ran while one was open for 0% -> 1% of each run, Pallas kernels for 0% -> 12%
where the time goes in v2:
time: 78.2 us; the launch traced here: 77.7 us
  waiting for transfers between devices  27.8 us (36%)
  starting transfers between devices  26.5 us (34%)
  Pallas kernels  20 us (26%)
  local copies, waits for them, and re-layouts  3.17 us (4%)
    all_to_all x1, waiting for transfers between devices, local(): lax.all_to_all(incr, ('gu', 'gv'), split_axis=0, concat_axis=0, tiled=True)  14.6 us
    pallas_call x1, Pallas kernels, local(): pl.pallas_call(functools.partial(gather_kernel, split, blocks), out_shape...  9.21 us
    all_to_all x1, starting transfers between devices, local(): lax.all_to_all(early, ('gu', 'gv'), split_axis=0, concat_axis=0, tiled=True)  8.61 us
    pallas_call x1, Pallas kernels, local(): pl.pallas_call(functools.partial(band_kernel, split, 2.0 / cols_all), out...  8.04 us
    all_to_all x1, starting transfers between devices, local(): lax.all_to_all(crossed, ('gx', 'gv'), split_axis=0, concat_axis=0, tiled=...  7.62 us
    all_to_all x1, waiting for transfers between devices, local(): lax.all_to_all(crossed, ('gx', 'gv'), split_axis=0, concat_axis=0, tiled=...  6.39 us
    all_to_all x1, starting transfers between devices, local(): lax.all_to_all(incr, ('gu', 'gv'), split_axis=0, concat_axis=0, tiled=True)  4.95 us
    ppermute x1, starting transfers between devices, local(): second = lax.ppermute(second, 'gx', cross)  4.64 us
  transfers between devices with their start and end apart: 6, of which 5 were waited for; matrix products, arithmetic and copies ran while one was open for 1% of the time, Pallas kernels for 12%

profile of v2, /device:TPU:2, one launch (start us, length us, event | category | flops | bytes accessed | tf_op | source)
XLA Modules:
  0.0 77.7 jit_solution(931288562397543803)
XLA Ops:
  0.0 0.0 copy-start
  0.0 0.0 copy-start.1
  0.0 1.0 %copy-done.1 = f32[1,8,24,384]{3,2,1,0:T(8,128)S(1)} copy-done((f32[1,8,24,384]{3,2,1,0:T(8,128)S(1)}, f32[1,8,24,384]{3,2,1,0:T(8,128)}, u32[]{:S(2)}) %copy-start.1) | copy-done | bytes 294936
  1.0 0.0 copy-start.5
  1.0 0.8 %copy-done.5 = s32[1,1,1,128,128]{4,3,2,1,0:T(8,128)S(1)} copy-done((s32[1,1,1,128,128]{4,3,2,1,0:T(8,128)S(1)}, s32[1,1,1,128,128]{4,3,2,1,0:T(8,128)}, u32[]{:S(2)}) %copy-start.5) | copy-done | bytes 65560
  1.8 0.8 %early_pack.1 = bf16[8,136,128]{2,1,0:T(8,128)(2,1)} custom-call(f32[1,8,24,384]{3,2,1,0:T(8,128)S(1)} %copy-done.1, s32[128,128]{1,0:T(8,128)S(1)} %bitcast.8), custom_call_target="tpu_custom_call" | custom-call | tf_op jit(solution)/shard_map/early_pack/pallas_call | solution.py:268
  2.6 0.0 copy-start.2
  2.6 0.0 copy-start.9
  2.6 0.0 copy-start.10
  2.6 0.0 copy-start.12
  2.7 8.6 %all-to-all-start = ((bf16[8,136,128]{2,1,0:T(8,128)(2,1)}), bf16[8,136,128]{2,1,0:T(8,128)(2,1)S(1)}, u32[]{:S(2)}, u32[]{:S(2)}) async-start(bf16[8,136,128]{2,1,0:T(8,128)(2,1)} %early_pack.1), calls=%async_computation | async-start | bytes 557056 | tf_op jit(solution)/shard_map/all_to_all | solution.py:276
  11.3 0.0 copy-start.11
  11.3 0.0 copy-done.2
  11.3 0.0 copy-done.9
  11.3 0.0 copy-done.10
  11.3 0.0 copy-done.12
  11.3 0.6 copy-done.11
  11.9 9.2 %couple_gather.1 = bf16[32,16,128]{2,1,0:T(8,128)(2,1)S(1)} custom-call(s32[128]{0:T(128)S(1)} %bitcast.11, f32[1,8,24,384]{3,2,1,0:T(8,128)S(1)} %copy-done.2, s32[128,128]{1,0:T(8,128)S(1)} %bitcast.9, f32[128,128]{1,0:T(8,128)S(1)} %bitcast.10, bf16[32,768]{1,0:T(8,128)(2,1)S(1)} %copy-done.12), custom_call_target="tpu_custom_call" | custom-call | flops 4000000000 | bytes 16000000 | tf_op jit(solution)/shard_map/couple_gather/pallas_call | solution.py:282
  21.1 2.4 %all-to-all-done.early_ref = bf16[8,136,128]{2,1,0:T(8,128)(2,1)S(1)} async-done(((bf16[8,136,128]{2,1,0:T(8,128)(2,1)}), bf16[8,136,128]{2,1,0:T(8,128)(2,1)S(1)}, u32[]{:S(2)}, u32[]{:S(2)}) %all-to-all-start) | async-done | bytes 278560 | tf_op jit(solution)/shard_map/all_to_all | solution.py:276
  23.5 0.0 collective-permute-start
  23.5 1.5 %collective-permute-done = bf16[32,16,128]{2,1,0:T(8,128)(2,1)} collective-permute-done((bf16[32,16,128]{2,1,0:T(8,128)(2,1)S(1)}, bf16[32,16,128]{2,1,0:T(8,128)(2,1)}, u32[]{:S(2)}, u32[]{:S(2)}) %collective-permute-start) | collective-permute-done | bytes 131104 | tf_op jit(solution)/shard_map/ppermute | solution.py:292
  25.0 7.6 %all-to-all-start.1 = ((bf16[32,16,128]{2,1,0:T(8,128)(2,1)}), bf16[32,16,128]{2,1,0:T(8,128)(2,1)S(1)}, u32[]{:S(2)}, u32[]{:S(2)}) async-start(bf16[32,16,128]{2,1,0:T(8,128)(2,1)} %collective-permute-done), calls=%async_computation.1 | async-start | bytes 262144 | tf_op jit(solution)/shard_map/all_to_all | solution.py:293
  32.6 0.0 copy-done
  32.7 0.1 concatenate.9
  32.8 0.1 copy.14
  32.9 0.0 copy-start.4
  32.9 0.2 concatenate.8
  33.2 0.0 copy-start.3
  33.2 0.2 copy.13
  33.3 0.0 copy-start.8
  33.4 6.4 %all-to-all-done.1.arrived_ref = bf16[32,16,128]{2,1,0:T(8,128)(2,1)S(1)} async-done(((bf16[32,16,128]{2,1,0:T(8,128)(2,1)}), bf16[32,16,128]{2,1,0:T(8,128)(2,1)S(1)}, u32[]{:S(2)}, u32[]{:S(2)}) %all-to-all-start.1) | async-done | bytes 131104 | tf_op jit(solution)/shard_map/all_to_all | solution.py:293
  39.8 0.0 copy-done.4
  39.8 0.0 copy-done.3
  39.8 0.0 copy-done.8
  39.8 8.0 %band_filter.1 = bf16[8,3,24,384]{3,2,1,0:T(8,128)(2,1)} custom-call(bf16[32,16,128]{2,1,0:T(8,128)(2,1)S(1)} %all-to-all-done.1.arrived_ref, bf16[8,136,128]{2,1,0:T(8,128)(2,1)S(1)} %all-to-all-done.early_ref, f32[3,2,8,256]{3,2,1,0:T(8,128)S(1)} %pad.4.resp_ref, bf16[384,512]{1,0:T(8,128)(2,1)S(1)} %copy-done.4, bf16[256,768]{1,0:T(8,128)(2,1)S(1)} %copy-done.3, ...), custom_call_target="tpu_custom_call" | custom-call | tf_op jit(solution)/shard_map/band_filter/pallas_call | solution.py:302
  47.8 5.0 %all-to-all-start.2 = ((bf16[8,3,24,384]{3,2,1,0:T(8,128)(2,1)}), bf16[8,3,24,384]{3,2,1,0:T(8,128)(2,1)S(1)}, u32[]{:S(2)}, u32[]{:S(2)}) async-start(bf16[8,3,24,384]{3,2,1,0:T(8,128)(2,1)} %band_filter.1), calls=%async_computation.2 | async-start | bytes 884736 | tf_op jit(solution)/shard_map/all_to_all | solution.py:316
  52.8 0.1 pad_add_fusion.odd_ref.flag_ref
  52.8 0.0 copy-start.6
  52.8 0.0 copy-start.7
  52.8 14.6 %all-to-all-done.2.back_ref = bf16[8,3,24,384]{3,2,1,0:T(8,128)(2,1)S(1)} async-done(((bf16[8,3,24,384]{3,2,1,0:T(8,128)(2,1)}), bf16[8,3,24,384]{3,2,1,0:T(8,128)(2,1)S(1)}, u32[]{:S(2)}, u32[]{:S(2)}) %all-to-all-start.2) | async-done | bytes 442400 | tf_op jit(solution)/shard_map/all_to_all | solution.py:316
  67.4 0.6 partial_sum.1
  68.0 0.7 collective-permute-start.1
  68.7 4.6 %collective-permute-start.2 = (bf16[8,384]{1,0:T(8,128)(2,1)S(1)}, bf16[8,384]{1,0:T(8,128)(2,1)S(1)}, u32[]{:S(2)}, u32[]{:S(2)}) collective-permute-start(bf16[8,384]{1,0:T(8,128)(2,1)S(1)} %get-tuple-element.14), channel_id=1, source_target_pairs={{8,16},{16,8},{24,32},{32,24},{40,48},{48,40},{56,64},{64,56},{72,... | collective-permute-start | bytes 18440 | tf_op jit(solution)/shard_map/ppermute | solution.py:332
  73.4 0.0 collective-permute-done.1.first_ref
  73.4 3.0 %collective-permute-done.2.second_ref = bf16[8,384]{1,0:T(8,128)(2,1)S(1)} collective-permute-done((bf16[8,384]{1,0:T(8,128)(2,1)S(1)}, bf16[8,384]{1,0:T(8,128)(2,1)S(1)}, u32[]{:S(2)}, u32[]{:S(2)}) %collective-permute-start.2) | collective-permute-done | bytes 6176 | tf_op jit(solution)/shard_map/ppermute | solution.py:332
  76.4 0.0 copy-done.6
  76.4 0.0 copy-done.7
  76.4 1.4 %diffuse.1 = f32[1,8,24,384]{3,2,1,0:T(8,128)} custom-call(s32[2]{0:T(128)S(1)} %pad_add_fusion.odd_ref.flag_ref, f32[8,24,384]{2,1,0:T(8,128)S(1)} %get-tuple-element.12.fields_ref, bf16[8,384]{1,0:T(8,128)(2,1)S(1)} %collective-permute-done.1.first_ref, bf16[8,384]{1,0:T(8,128)(2,1)S(1)} %collective-permute-done.2.second_ref, f32[1,24,384]{2,1,0:T(8,128)S(1)} %copy-done.6, ...), custom_call_target="tpu_custom_call" | custom-call | tf_op jit(solution)/shard_map/diffuse/pallas_call | solution.py:333
  (4 shorter events, 0.1 us)
Async XLA Ops:
  0.0 32.6 %copy-start = (f32[1,8,3072]{2,1,0:T(8,128)S(1)}, f32[1,8,3072]{2,1,0:T(8,128)}, u32[]{:S(2)}) copy-start(f32[1,8,3072]{2,1,0:T(8,128)} %param.13) | copy-start | bytes 294916
  0.0 1.0 %copy-start.1 = (f32[1,8,24,384]{3,2,1,0:T(8,128)S(1)}, f32[1,8,24,384]{3,2,1,0:T(8,128)}, u32[]{:S(2)}) copy-start(f32[1,8,24,384]{3,2,1,0:T(8,128)} %state_ref.3) | copy-start | bytes 884740
  1.0 0.8 %copy-start.5 = (s32[1,1,1,128,128]{4,3,2,1,0:T(8,128)S(1)}, s32[1,1,1,128,128]{4,3,2,1,0:T(8,128)}, u32[]{:S(2)}) copy-start(s32[1,1,1,128,128]{4,3,2,1,0:T(8,128)} %param.17) | copy-start | bytes 196612
  2.6 8.6 %copy-start.2 = (f32[1,8,24,384]{3,2,1,0:T(8,128)S(1)}, f32[1,8,24,384]{3,2,1,0:T(8,128)}, u32[]{:S(2)}) copy-start(f32[1,8,24,384]{3,2,1,0:T(8,128)} %state_ref.3) | copy-start | bytes 884740
  2.6 8.6 %copy-start.9 = (s32[1,1,1,128,128]{4,3,2,1,0:T(8,128)S(1)}, s32[1,1,1,128,128]{4,3,2,1,0:T(8,128)}, u32[]{:S(2)}) copy-start(s32[1,1,1,128,128]{4,3,2,1,0:T(8,128)} %param.16) | copy-start | bytes 196612
  2.6 8.6 %copy-start.10 = (f32[1,1,1,128,128]{4,3,2,1,0:T(8,128)S(1)}, f32[1,1,1,128,128]{4,3,2,1,0:T(8,128)}, u32[]{:S(2)}) copy-start(f32[1,1,1,128,128]{4,3,2,1,0:T(8,128)} %param.18) | copy-start | bytes 196612
  2.6 8.7 %copy-start.12 = (bf16[32,768]{1,0:T(8,128)(2,1)S(1)}, bf16[32,768]{1,0:T(8,128)(2,1)}, u32[]{:S(2)}) copy-start(bf16[32,768]{1,0:T(8,128)(2,1)} %constant.45.clone.pick_ref) | copy-start | bytes 147460
  2.7 20.8 %all-to-all-start = ((bf16[8,136,128]{2,1,0:T(8,128)(2,1)}), bf16[8,136,128]{2,1,0:T(8,128)(2,1)S(1)}, u32[]{:S(2)}, u32[]{:S(2)}) async-start(bf16[8,136,128]{2,1,0:T(8,128)(2,1)} %early_pack.1), calls=%async_computation | async-start | bytes 557056 | tf_op jit(solution)/shard_map/all_to_all | solution.py:276
  11.3 0.7 copy-start.11
  23.5 1.5 %collective-permute-start = (bf16[32,16,128]{2,1,0:T(8,128)(2,1)S(1)}, bf16[32,16,128]{2,1,0:T(8,128)(2,1)}, u32[]{:S(2)}, u32[]{:S(2)}) collective-permute-start(bf16[32,16,128]{2,1,0:T(8,128)(2,1)S(1)} %couple_gather.1), channel_id=1, source_target_pairs={{0,128},{128,0},{1,129},{129,1},{2,130},{130,2},{3,131},{131,3},{4... | collective-permute-start | bytes 393224 | tf_op jit(solution)/shard_map/ppermute | solution.py:292
  25.0 14.8 %all-to-all-start.1 = ((bf16[32,16,128]{2,1,0:T(8,128)(2,1)}), bf16[32,16,128]{2,1,0:T(8,128)(2,1)S(1)}, u32[]{:S(2)}, u32[]{:S(2)}) async-start(bf16[32,16,128]{2,1,0:T(8,128)(2,1)} %collective-permute-done), calls=%async_computation.1 | async-start | bytes 262144 | tf_op jit(solution)/shard_map/all_to_all | solution.py:293
  32.9 6.9 %copy-start.4 = (bf16[384,512]{1,0:T(8,128)(2,1)S(1)}, bf16[384,512]{1,0:T(8,128)(2,1)}, u32[]{:S(2)}) copy-start(bf16[384,512]{1,0:T(8,128)(2,1)} %constant.46.clone.ahead_ref) | copy-start | bytes 1179652
  33.2 6.6 %copy-start.3 = (bf16[256,768]{1,0:T(8,128)(2,1)S(1)}, bf16[256,768]{1,0:T(8,128)(2,1)}, u32[]{:S(2)}) copy-start(bf16[256,768]{1,0:T(8,128)(2,1)} %constant.47.clone.back_ref) | copy-start | bytes 1179652
  33.3 6.4 %copy-start.8 = (f32[2,8,384]{2,1,0:T(8,128)S(1)}, f32[2,8,384]{2,1,0:T(8,128)}, u32[]{:S(2)}) copy-start(f32[2,8,384]{2,1,0:T(8,128)} %constant.48.clone.twiddle_ref) | copy-start | bytes 73732
  47.8 19.6 %all-to-all-start.2 = ((bf16[8,3,24,384]{3,2,1,0:T(8,128)(2,1)}), bf16[8,3,24,384]{3,2,1,0:T(8,128)(2,1)S(1)}, u32[]{:S(2)}, u32[]{:S(2)}) async-start(bf16[8,3,24,384]{3,2,1,0:T(8,128)(2,1)} %band_filter.1), calls=%async_computation.2 | async-start | bytes 884736 | tf_op jit(solution)/shard_map/all_to_all | solution.py:316
  52.8 23.5 %copy-start.6 = (f32[1,24,384]{2,1,0:T(8,128)S(1)}, f32[1,24,384]{2,1,0:T(8,128)}, u32[]{:S(2)}) copy-start(f32[1,24,384]{2,1,0:T(8,128)} %rate_ref.1) | copy-start | bytes 110596
  52.8 23.5 %copy-start.7 = (s32[24,384]{1,0:T(8,128)S(1)}, s32[24,384]{1,0:T(8,128)}, u32[]{:S(2)}) copy-start(s32[24,384]{1,0:T(8,128)} %land_ref.1) | copy-start | bytes 110596
  68.0 5.4 %collective-permute-start.1 = (bf16[8,384]{1,0:T(8,128)(2,1)S(1)}, bf16[8,384]{1,0:T(8,128)(2,1)S(1)}, u32[]{:S(2)}, u32[]{:S(2)}) collective-permute-start(bf16[8,384]{1,0:T(8,128)(2,1)S(1)} %get-tuple-element.13), channel_id=1, source_target_pairs={{0,8},{8,0},{16,24},{24,16},{32,40},{40,32},{48,56},{56,48},{64,72... | collective-permute-start | bytes 18440 | tf_op jit(solution)/shard_map/ppermute | solution.py:331
  68.7 7.6 %collective-permute-start.2 = (bf16[8,384]{1,0:T(8,128)(2,1)S(1)}, bf16[8,384]{1,0:T(8,128)(2,1)S(1)}, u32[]{:S(2)}, u32[]{:S(2)}) collective-permute-start(bf16[8,384]{1,0:T(8,128)(2,1)S(1)} %get-tuple-element.14), channel_id=1, source_target_pairs={{8,16},{16,8},{24,32},{32,24},{40,48},{48,40},{56,64},{64,56},{72,... | collective-permute-start | bytes 18440 | tf_op jit(solution)/shard_map/ppermute | solution.py:332

commit v3 on v2

--- a/solution.py
+++ b/solution.py
@@ -28,6 +28,12 @@
     return row, idx - row * cols
 
 
+def split_lines(idx, rows, cols):
+    row, col = split_cell(idx, cols)
+    tile = col // LANES
+    return tile * rows + row, col - tile * LANES
+
+
 def tiles(block):
     return jnp.concatenate([block[:, t : t + LANES] for t in range(0, block.shape[1], LANES)], axis=0)
 
@@ -42,10 +48,8 @@
     groups = peers // levels
     for h in range(levels):
         idx = dst_ref[pl.ds(h, groups, stride=levels), :]
-        row, col = split_cell(idx, cols)
-        tile = col // LANES
-        line = (tile * rows + row).astype(F32).astype(BF)
-        lane = (col - tile * LANES).astype(F32).astype(BF)
+        line, lane = split_lines(idx, rows, cols)
+        line, lane = line.astype(F32).astype(BF), lane.astype(F32).astype(BF)
         u, other = h // split, h % split
         for v in range(split):
             piece = u * split + v
@@ -59,21 +63,29 @@
     peers, slots = src_ref.shape
     fc = split * out_ref.shape[1] // blocks
     each = fc // split * blocks
-    surface = surf_ref[0, :fc].reshape(fc * rows, cols).astype(BF)
+    lines = rows * cols // LANES
+    half = -(-lines // 16) * 8
+    shift = lines - half
+    surface = [tiles(surf_ref[0, c]) for c in range(fc)]
+    surface = jnp.concatenate([jnp.concatenate([x[:half], x[shift:]], axis=1) for x in surface], axis=0).astype(BF)
     lane = lax.broadcasted_iota(jnp.int32, (blocks, slots), 1)
     sub = lax.broadcasted_iota(jnp.int32, (blocks, slots), 0)
+    spot = lax.broadcasted_iota(jnp.int32, (half, slots), 0)
 
     def step(g, carry):
         base = pl.multiple_of(g * blocks, blocks)
-        row, col = split_cell(src_ref[pl.ds(base, blocks), :], cols)
+        line, col = split_lines(src_ref[pl.ds(base, blocks), :], rows, cols)
+        upper = line >= half
+        line = line - jnp.where(upper, shift, 0)
+        col = col + jnp.where(upper, LANES, 0)
         found = []
         for i in range(0, blocks, 2):
-            pick = jnp.concatenate([one_hot(cols, col[j : j + 1]) for j in (i, i + 1)], axis=1)
-            lines = jnp.dot(surface, pick.astype(BF), preferred_element_type=F32)
+            pick = jnp.concatenate([one_hot(2 * LANES, col[j : j + 1]) for j in (i, i + 1)], axis=1)
+            values = jnp.dot(surface, pick.astype(BF), preferred_element_type=F32)
             for j in range(2):
-                mask = one_hot(rows, row[i + j : i + j + 1])
-                own = lines[:, j * slots : (j + 1) * slots].reshape(fc, rows, slots)
-                found.append((own * mask[None]).reshape(fc * rows, slots))
+                own = values[:, j * slots : (j + 1) * slots].reshape(fc, half, slots)
+                own = jnp.where((spot == line[i + j : i + j + 1])[None], own, 0.0)
+                found.append(jnp.sum(own.reshape(fc, half // 8, 8, slots), axis=1).reshape(fc * 8, slots))
         value = jnp.dot(pick_ref[...], jnp.concatenate(found, axis=0).astype(BF), preferred_element_type=F32)
         limit = jnp.zeros((blocks, slots), jnp.int32)
         for i in range(blocks):
@@ -84,31 +96,40 @@
             out_ref[g * split + v] = value[v * each : (v + 1) * each].astype(BF)
         return carry
 
-    lax.fori_loop(0, peers // blocks, step, 0)
-
-
-def band_kernel(
-    split, scale, arrived_ref, early_ref, resp_ref, ahead_ref, back_ref, twiddle_ref, out_ref, value_ref, line_ref, lane_ref, acc_ref
+    lax.fori_loop(0, peers // blocks, step, 0, unroll=16)
+
+
+def circle_kernel(scale, early_ref, resp_ref, ahead_ref, back_ref, twiddle_ref, out_ref):
+    blocks, rows, cols = out_ref.shape
+    start = early_ref.shape[1] - rows * cols // LANES
+    x = [untile(early_ref[h, start:].astype(F32), rows) for h in range(blocks)]
+    incr = zonal_rows(x, resp_ref[0], resp_ref[1], ahead_ref, back_ref, twiddle_ref)
+    for h in range(blocks):
+        out_ref[h] = (incr[h] * scale).astype(BF)
+
+
+def scatter_kernel(
+    split, flag_ref, arrived_ref, early_ref, part_ref, first_ref, second_ref, value_ref, line_ref, lane_ref, acc_ref
 ):
     senders, each, slots = arrived_ref.shape
     blocks = early_ref.shape[0]
-    fields = each // blocks
+    fields, _, rows, cols = part_ref.shape
     groups = senders // split
-    rows, cols = out_ref.shape[2], out_ref.shape[3]
-    cell_rows = rows * cols // LANES
+    lines = rows * cols // LANES
     for s in range(senders):
         value_ref[s] = arrived_ref[s].astype(F32)
     for h in range(blocks):
         line_ref[h] = early_ref[h, :senders].astype(F32).astype(jnp.int32)
         lane_ref[h] = early_ref[h, senders : 2 * senders].astype(F32).astype(jnp.int32)
     acc_ref[...] = jnp.zeros_like(acc_ref)
+    spot = lax.broadcasted_iota(jnp.int32, (lines, slots), 0)
 
     def step(g, carry):
         for h in range(blocks):
             spread, pick = [], []
             for v in range(split):
                 at = v * groups + g
-                mask = lax.broadcasted_iota(jnp.int32, (cell_rows, slots), 0) == line_ref[h, pl.ds(at, 1), :]
+                mask = spot == line_ref[h, pl.ds(at, 1), :]
                 vals = [
                     jnp.where(mask, value_ref[g * split + v, c * blocks + h : c * blocks + h + 1, :], 0.0)
                     for c in range(fields)
@@ -123,49 +144,80 @@
             )
         return carry
 
-    lax.fori_loop(0, groups, step, 0)
+    lax.fori_loop(0, groups, step, 0, unroll=4)
+    tops, bottoms = [], []
     for c in range(fields + 1):
-        if c < fields:
-            x = [untile(acc_ref[h, c * cell_rows : (c + 1) * cell_rows], rows) for h in range(blocks)]
-        else:
-            x = [untile(early_ref[h, 2 * senders :].astype(F32), rows) for h in range(blocks)]
-        incr = zonal_rows(x, resp_ref.at[c], ahead_ref, back_ref, twiddle_ref)
         for h in range(blocks):
-            total = incr[h] * scale
             if c < fields:
-                total = total + untile(acc_ref[h, c * cell_rows : (c + 1) * cell_rows], rows)
-            out_ref[h, c] = total.astype(BF)
-
-
-def sum_kernel(split, odd_ref, state_ref, back_ref, fields_ref, first_ref, second_ref):
-    _, levels, rows, _ = state_ref.shape
-    each = back_ref.shape[1] - 1
-    tops, bottoms = [], []
-    for c in range(levels):
-        total = state_ref[0, c] + back_ref[c, each].astype(F32)
-        if c < split * each:
-            for u in range(levels // split):
-                total = total + back_ref[u * split + c // each, c % each].astype(F32)
-        fields_ref[c] = total
-        tops.append(total[:1])
-        bottoms.append(total[rows - 1 :])
+                x = untile(acc_ref[h, c * lines : (c + 1) * lines], rows)
+                part_ref[c, h] = x
+            else:
+                x = untile(early_ref[h, 2 * senders :].astype(F32), rows)
+            tops.append(x[:1])
+            bottoms.append(x[rows - 1 :])
     top, bottom = jnp.concatenate(tops, axis=0), jnp.concatenate(bottoms, axis=0)
-    odd = odd_ref[0] == 1
+    odd = flag_ref[0] == 1
     first_ref[...] = jnp.where(odd, top, bottom).astype(BF)
     second_ref[...] = jnp.where(odd, bottom, top).astype(BF)
 
 
-def diffuse_kernel(flag_ref, fields_ref, first_ref, second_ref, rate_ref, land_ref, out_ref):
-    levels, rows, cols = fields_ref.shape
+def part_kernel(scale, part_ref, resp_ref, ahead_ref, back_ref, twiddle_ref, out_ref):
+    blocks, fields, rows, cols = out_ref.shape
+    for c in range(fields):
+        x = [part_ref[c, h] for h in range(blocks)]
+        incr = zonal_rows(x, resp_ref[c, 0], resp_ref[c, 1], ahead_ref, back_ref, twiddle_ref)
+        for h in range(blocks):
+            out_ref[h, c] = (incr[h] * scale + x[h]).astype(BF)
+
+
+def edge_kernel(
+    scale, flag_ref, first_ref, second_ref, part_ref, circle_ref, resp_ref, ahead_ref, back_ref, twiddle_ref, out_ref
+):
+    blocks, fields, rows, cols = part_ref.shape
+    sets = fields + 1
     odd = flag_ref[0] == 1
     first, second = first_ref[...].astype(F32), second_ref[...].astype(F32)
     low, high = jnp.where(odd, first, second), jnp.where(odd, second, first)
+    x = []
+    blank = jnp.zeros((8 - 2 * sets, cols), F32)
+    for h in range(blocks):
+        lines = [side[c * blocks + h : c * blocks + h + 1] for c in range(sets) for side in (low, high)]
+        x.append(jnp.concatenate(lines + [blank], axis=0))
+    zero = jnp.zeros((8 - 2 * sets, resp_ref.shape[3]), F32)
+    resp = [
+        [
+            jnp.concatenate([resp_ref[c, k, r : r + 1, :] for c in range(sets) for _ in range(2)] + [zero], axis=0)
+            for r in range(blocks)
+        ]
+        for k in range(2)
+    ]
+    incr = zonal_rows(x, resp[0], resp[1], ahead_ref, back_ref, twiddle_ref)
+    for h in range(blocks):
+        for c in range(fields):
+            out_ref[h, c * rows : (c + 1) * rows] = part_ref[h, c]
+        out_ref[h, fields * rows : sets * rows] = circle_ref[h]
+        out_ref[h, sets * rows :] = (incr[h] * scale + x[h]).astype(BF)
+
+
+def final_kernel(split, flag_ref, state_ref, back_ref, rate_ref, land_ref, out_ref):
+    _, levels, rows, cols = state_ref.shape
+    sets = (back_ref.shape[1] - 8) // rows
+    fields = sets - 1
     keep = jnp.where(flag_ref[1] == 1, land_ref[...].astype(F32), 1.0)
     rate = rate_ref[0] * keep
+    edges = [back_ref[z, sets * rows :].astype(F32) for z in range(levels)]
     for c in range(levels):
-        own = fields_ref[c]
-        above = jnp.concatenate([low[c : c + 1], own[: rows - 1]], axis=0)
-        below = jnp.concatenate([own[1:], high[c : c + 1]], axis=0)
+        own = state_ref[0, c] + back_ref[c, fields * rows : sets * rows].astype(F32)
+        low, high = edges[c][2 * fields : 2 * fields + 1], edges[c][2 * fields + 1 : 2 * fields + 2]
+        if c < split * fields:
+            at = c % fields
+            for u in range(levels // split):
+                z = u * split + c // fields
+                own = own + back_ref[z, at * rows : (at + 1) * rows].astype(F32)
+                low = low + edges[z][2 * at : 2 * at + 1]
+                high = high + edges[z][2 * at + 1 : 2 * at + 2]
+        above = jnp.concatenate([low, own[: rows - 1]], axis=0)
+        below = jnp.concatenate([own[1:], high], axis=0)
         out_ref[0, c] = own * keep + rate * (above + below - 2.0 * own)
 
 
@@ -183,7 +235,11 @@
     return jnp.asarray(ahead, BF), jnp.asarray(back, BF), jnp.asarray(twiddle, F32)
 
 
-def zonal_rows(x, resp, ahead_ref, back_ref, twiddle_ref):
+def response_row(resp, r):
+    return resp[r] if isinstance(resp, list) else resp[r : r + 1, :]
+
+
+def zonal_rows(x, resp_cos, resp_sin, ahead_ref, back_ref, twiddle_ref):
     blocks = len(x)
     rows, cols = x[0].shape
     waves = ahead_ref.shape[1] // 2
@@ -217,8 +273,8 @@
         if r > 0:
             other = spec[(blocks + r - 1) * rows : (blocks + r) * rows]
             c, s = c + other[:, waves:], s - other[:, :waves]
-        cosine.append(c * resp[0, r : r + 1, :])
-        sine.append(s * resp[1, r : r + 1, :])
+        cosine.append(c * response_row(resp_cos, r))
+        sine.append(s * response_row(resp_sin, r))
     full = jnp.dot(jnp.concatenate(cosine + sine, axis=0).astype(BF), back_ref[...], preferred_element_type=F32)
     u = []
     for r in range(blocks):
@@ -245,6 +301,10 @@
     ]
 
 
+def cost(micros):
+    return pl.CostEstimate(flops=micros * 10**9, bytes_accessed=micros * 3 * 10**6, transcendentals=0)
+
+
 def local(
     state, response, diffusion, land_mask, couple_src, couple_dst, couple_weight, couple_count
 ):
@@ -275,7 +335,7 @@
     )(state, dst_idx)
     early = lax.all_to_all(early, ("gu", "gv"), split_axis=0, concat_axis=0, tiled=True)
 
-    spot = np.zeros((FC, blocks, blocks, FC, rows), np.float32)
+    spot = np.zeros((FC, blocks, blocks, FC, 8), np.float32)
     for c in range(FC):
         for h in range(blocks):
             spot[c, h, h, c] = 1.0
@@ -285,11 +345,12 @@
         in_specs=[SMEM, VMEM, VMEM, VMEM, VMEM],
         out_specs=VMEM,
         compiler_params=PARAMS,
-        cost_estimate=pl.CostEstimate(flops=4 * 10**9, bytes_accessed=16 * 10**6, transcendentals=0),
+        cost_estimate=cost(4),
         name="couple_gather",
     )(count, state, src_idx, weight, jnp.asarray(spot.reshape(FC * blocks, -1), BF))
     outgoing, early = lax.optimization_barrier((outgoing, early))
     crossed = lax.ppermute(outgoing, "comp", [(0, 1), (1, 0)])
+    crossed, early = lax.optimization_barrier((crossed, early))
     arrived = lax.all_to_all(crossed, ("gx", "gv"), split_axis=0, concat_axis=0, tiled=True)
 
     ahead, back, twiddle = zonal_tables(blocks, cols, waves)
@@ -299,11 +360,24 @@
     )
     resp = resp.reshape(each + 1, 2, half, blocks).transpose(0, 1, 3, 2)
     resp = jnp.pad(resp, ((0, 0), (0, 0), (0, 0), (0, waves - half)))
-    incr = pl.pallas_call(
-        functools.partial(band_kernel, split, 2.0 / cols_all),
-        out_shape=jax.ShapeDtypeStruct((blocks, each + 1, rows, cols), BF),
-        in_specs=[VMEM] * 6,
-        out_specs=VMEM,
+    scale = 2.0 / cols_all
+    flag = jnp.stack([lax.axis_index("gx") % 2, lax.axis_index("comp")])
+
+    circle = pl.pallas_call(
+        functools.partial(circle_kernel, scale),
+        out_shape=jax.ShapeDtypeStruct((blocks, rows, cols), BF),
+        in_specs=[VMEM] * 5,
+        out_specs=VMEM,
+        compiler_params=PARAMS,
+        cost_estimate=cost(2),
+        name="circle_filter",
+    )(early, resp[each], ahead, back, twiddle)
+    edge = jax.ShapeDtypeStruct(((each + 1) * blocks, cols), BF)
+    part, first, second = pl.pallas_call(
+        functools.partial(scatter_kernel, split),
+        out_shape=(jax.ShapeDtypeStruct((each, blocks, rows, cols), F32), edge, edge),
+        in_specs=[SMEM, VMEM, VMEM],
+        out_specs=(VMEM, VMEM, VMEM),
         scratch_shapes=[
             pltpu.VMEM((senders, each * blocks, slots), F32),
             pltpu.VMEM((blocks, senders, slots), jnp.int32),
@@ -311,33 +385,41 @@
             pltpu.VMEM((blocks, each * cell_rows, LANES), F32),
         ],
         compiler_params=PARAMS,
-        name="band_filter",
-    )(arrived, early, resp, ahead, back, twiddle)
-    incr = lax.all_to_all(incr, ("gu", "gv"), split_axis=0, concat_axis=0, tiled=True)
-
-    odd = lax.axis_index("gx") % 2
-    flag = jnp.stack([odd, lax.axis_index("comp")])
-    edge = jax.ShapeDtypeStruct((levels, cols), BF)
-    fields, first, second = pl.pallas_call(
-        functools.partial(sum_kernel, split),
-        out_shape=(jax.ShapeDtypeStruct((levels, rows, cols), F32), edge, edge),
-        in_specs=[SMEM, VMEM, VMEM],
-        out_specs=(VMEM, VMEM, VMEM),
-        compiler_params=PARAMS,
-        name="partial_sum",
-    )(flag, state, incr)
+        cost_estimate=cost(4),
+        name="couple_scatter",
+    )(flag, arrived, early)
     pairs = [(i, i ^ 1) for i in range(groups_x)]
     cross = [pair for i in range(1, groups_x - 1, 2) for pair in ((i, i + 1), (i + 1, i))]
     first = lax.ppermute(first, "gx", pairs)
     second = lax.ppermute(second, "gx", cross)
+    part = pl.pallas_call(
+        functools.partial(part_kernel, scale),
+        out_shape=jax.ShapeDtypeStruct((blocks, each, rows, cols), BF),
+        in_specs=[VMEM] * 5,
+        out_specs=VMEM,
+        compiler_params=PARAMS,
+        cost_estimate=cost(3),
+        name="part_filter",
+    )(part, resp, ahead, back, twiddle)
+    incr = pl.pallas_call(
+        functools.partial(edge_kernel, scale),
+        out_shape=jax.ShapeDtypeStruct((blocks, (each + 1) * rows + 8, cols), BF),
+        in_specs=[SMEM] + [VMEM] * 8,
+        out_specs=VMEM,
+        compiler_params=PARAMS,
+        cost_estimate=cost(1),
+        name="edge_filter",
+    )(flag, first, second, part, circle, resp, ahead, back, twiddle)
+    incr = lax.all_to_all(incr, ("gu", "gv"), split_axis=0, concat_axis=0, tiled=True)
     return pl.pallas_call(
-        diffuse_kernel,
+        functools.partial(final_kernel, split),
         out_shape=jax.ShapeDtypeStruct((1, levels, rows, cols), F32),
-        in_specs=[SMEM] + [VMEM] * 5,
-        out_specs=VMEM,
-        compiler_params=PARAMS,
-        name="diffuse",
-    )(flag, fields, first, second, diffusion, land_mask)
+        in_specs=[SMEM] + [VMEM] * 4,
+        out_specs=VMEM,
+        compiler_params=PARAMS,
+        cost_estimate=cost(1),
+        name="final_step",
+    )(flag, state, incr, diffusion, land_mask)
 
 
 def solution(mesh):

time: 78.2 us -> 72.3 us (0.925)
  blocking collectives: 0 us -> 17.1 us
  waiting for transfers between devices: 27.8 us -> 15.9 us
  Pallas kernels: 20 us -> 13.9 us
  starting transfers between devices: 26.5 us -> 21.2 us
    all_to_all x0 -> x1, blocking collectives: none -> 17.1 us  [local(): lax.all_to_all(incr, ('gu', 'gv'), split_axis=0, concat_axis=0, tiled=True)]
    all_to_all x1 -> x0, waiting for transfers between devices: 14.6 us -> none  [local(): lax.all_to_all(incr, ('gu', 'gv'), split_axis=0, concat_axis=0, tiled=True)]
    all_to_all x1 -> x0, starting transfers between devices: 4.95 us -> none  [local(): lax.all_to_all(incr, ('gu', 'gv'), split_axis=0, concat_axis=0, tiled=True)]
    pallas_call x1, Pallas kernels: 9.21 us -> 4.58 us  [local(): pl.pallas_call(functools.partial(gather_kernel, split, blocks), out_shape...]
    all_to_all x1, waiting for transfers between devices: 2.36 us -> 6.1 us  [local(): lax.all_to_all(early, ('gu', 'gv'), split_axis=0, concat_axis=0, tiled=True)]
    pallas_call x3 -> x5, Pallas kernels: 10 us -> 8.57 us  [the longest x1 4.12 us: local(): pl.pallas_call(functools.partial(scatter_kernel, split), out_shape=(jax.S...]
    ppermute x1, waiting for transfers between devices: 2.96 us -> 2.07 us  [local(): second = lax.ppermute(second, 'gx', cross)]
  transfers between devices with their start and end apart: 6 -> 5, of which waited for: 5 -> 4; matrix products, arithmetic and copies ran while one was open for 1% -> 1% of each run, Pallas kernels for 12% -> 9%
where the time goes in v3:
time: 72.3 us; the launch traced here: 71.8 us
  starting transfers between devices  21.2 us (29%)
  blocking collectives  17.1 us (24%)
  waiting for transfers between devices  15.9 us (22%)
  Pallas kernels  13.9 us (19%)
  local copies, waits for them, and re-layouts  3.34 us (5%)
    all_to_all x1, blocking collectives, local(): lax.all_to_all(incr, ('gu', 'gv'), split_axis=0, concat_axis=0, tiled=True)  17.1 us
    all_to_all x1, starting transfers between devices, local(): lax.all_to_all(early, ('gu', 'gv'), split_axis=0, concat_axis=0, tiled=True)  8.47 us
    all_to_all x1, starting transfers between devices, local(): lax.all_to_all(crossed, ('gx', 'gv'), split_axis=0, concat_axis=0, tiled=...  7.62 us
    all_to_all x1, waiting for transfers between devices, local(): lax.all_to_all(crossed, ('gx', 'gv'), split_axis=0, concat_axis=0, tiled=...  6.32 us
    all_to_all x1, waiting for transfers between devices, local(): lax.all_to_all(early, ('gu', 'gv'), split_axis=0, concat_axis=0, tiled=True)  6.1 us
    pallas_call x1, Pallas kernels, local(): pl.pallas_call(functools.partial(gather_kernel, split, blocks), out_shape...  4.58 us
    ppermute x1, starting transfers between devices, local(): second = lax.ppermute(second, 'gx', cross)  4.43 us
    pallas_call x1, Pallas kernels, local(): pl.pallas_call(functools.partial(scatter_kernel, split), out_shape=(jax.S...  4.12 us
  transfers between devices with their start and end apart: 5, of which 4 were waited for; matrix products, arithmetic and copies ran while one was open for 1% of the time, Pallas kernels for 9%

profile of v3, /device:TPU:2, one launch (start us, length us, event | category | flops | bytes accessed | tf_op | source)
XLA Modules:
  0.0 71.8 jit_solution(8782812153838643634)
XLA Ops:
  0.0 0.0 copy-start
  0.0 0.0 copy-start.1
  0.0 1.0 %copy-done.1 = f32[1,8,24,384]{3,2,1,0:T(8,128)S(1)} copy-done((f32[1,8,24,384]{3,2,1,0:T(8,128)S(1)}, f32[1,8,24,384]{3,2,1,0:T(8,128)}, u32[]{:S(2)}) %copy-start.1) | copy-done | bytes 294936
  1.0 0.0 copy-start.3
  1.0 0.8 %copy-done.3 = s32[1,1,1,128,128]{4,3,2,1,0:T(8,128)S(1)} copy-done((s32[1,1,1,128,128]{4,3,2,1,0:T(8,128)S(1)}, s32[1,1,1,128,128]{4,3,2,1,0:T(8,128)}, u32[]{:S(2)}) %copy-start.3) | copy-done | bytes 65560
  1.8 0.8 %early_pack.1 = bf16[8,136,128]{2,1,0:T(8,128)(2,1)} custom-call(f32[1,8,24,384]{3,2,1,0:T(8,128)S(1)} %copy-done.1, s32[128,128]{1,0:T(8,128)S(1)} %bitcast.10), custom_call_target="tpu_custom_call" | custom-call | tf_op jit(solution)/shard_map/early_pack/pallas_call | solution.py:328
  2.6 8.5 %all-to-all-start = ((bf16[8,136,128]{2,1,0:T(8,128)(2,1)}), bf16[8,136,128]{2,1,0:T(8,128)(2,1)S(1)}, u32[]{:S(2)}, u32[]{:S(2)}) async-start(bf16[8,136,128]{2,1,0:T(8,128)(2,1)} %early_pack.1), calls=%async_computation | async-start | bytes 557056 | tf_op jit(solution)/shard_map/all_to_all | solution.py:336
  11.1 0.0 copy-done
  11.2 0.1 concatenate.9
  11.3 0.1 copy.14
  11.4 0.0 copy-start.12
  11.4 0.2 concatenate.8
  11.7 0.0 copy-start.2
  11.7 0.0 copy-start.4
  11.7 0.0 copy-start.5
  11.7 0.2 copy.13
  11.9 0.0 copy-start.8
  11.9 0.3 copy-done.12
  12.1 0.5 copy-done.2
  12.6 0.0 copy-done.4
  12.6 0.0 copy-done.5
  12.6 0.0 copy-done.8
  12.6 0.0 copy-start.10
  12.6 4.6 %couple_gather.1 = bf16[32,16,128]{2,1,0:T(8,128)(2,1)S(1)} custom-call(s32[128]{0:T(128)S(1)} %bitcast.13, f32[1,8,24,384]{3,2,1,0:T(8,128)S(1)} %copy-done.2, s32[128,128]{1,0:T(8,128)S(1)} %bitcast.11, f32[128,128]{1,0:T(8,128)S(1)} %bitcast.12, bf16[32,256]{1,0:T(8,128)(2,1)S(1)} %copy-done.12), custom_call_target="tpu_custom_call" | custom-call | flops 4000000000 | bytes 12000000 | tf_op jit(solution)/shard_map/couple_gather/pallas_call | solution.py:342
  17.2 6.1 %all-to-all-done.early_ref = bf16[8,136,128]{2,1,0:T(8,128)(2,1)S(1)} async-done(((bf16[8,136,128]{2,1,0:T(8,128)(2,1)}), bf16[8,136,128]{2,1,0:T(8,128)(2,1)S(1)}, u32[]{:S(2)}, u32[]{:S(2)}) %all-to-all-start) | async-done | bytes 278560 | tf_op jit(solution)/shard_map/all_to_all | solution.py:336
  23.3 0.0 collective-permute-start
  23.4 0.0 copy-start.11
  23.4 1.4 %collective-permute-done = bf16[32,16,128]{2,1,0:T(8,128)(2,1)} collective-permute-done((bf16[32,16,128]{2,1,0:T(8,128)(2,1)S(1)}, bf16[32,16,128]{2,1,0:T(8,128)(2,1)}, u32[]{:S(2)}, u32[]{:S(2)}) %collective-permute-start) | collective-permute-done | bytes 131104 | tf_op jit(solution)/shard_map/ppermute | solution.py:352
  24.8 7.6 %all-to-all-start.1 = ((bf16[32,16,128]{2,1,0:T(8,128)(2,1)}), bf16[32,16,128]{2,1,0:T(8,128)(2,1)S(1)}, u32[]{:S(2)}, u32[]{:S(2)}) async-start(bf16[32,16,128]{2,1,0:T(8,128)(2,1)} %collective-permute-done), calls=%async_computation.1 | async-start | bytes 262144 | tf_op jit(solution)/shard_map/all_to_all | solution.py:354
  32.4 0.1 pad_add_fusion.flag_ref
  32.5 0.0 copy-done.10
  32.5 0.0 copy-done.9
  32.5 0.0 copy-done.11
  32.5 0.7 %circle_filter.1.circle_ref = bf16[8,24,384]{2,1,0:T(8,128)(2,1)S(1)} custom-call(bf16[8,136,128]{2,1,0:T(8,128)(2,1)S(1)} %all-to-all-done.early_ref, f32[2,8,256]{2,1,0:T(8,128)S(1)} %slice_bitcast_fusion.resp_ref, bf16[384,512]{1,0:T(8,128)(2,1)S(1)} %copy-done.10, bf16[256,768]{1,0:T(8,128)(2,1)S(1)} %copy-done.9, f32[2,8,384]{2,1,0:T(8,128)S(1)} %copy-done.11), custom_call_target="tpu_custom_call" | custom-call | flops 2000000000 | bytes 6000000 | tf_op jit(solution)/shard_map/circle_filter/pallas_call | solution.py:366
  33.3 6.3 %all-to-all-done.1.arrived_ref = bf16[32,16,128]{2,1,0:T(8,128)(2,1)S(1)} async-done(((bf16[32,16,128]{2,1,0:T(8,128)(2,1)}), bf16[32,16,128]{2,1,0:T(8,128)(2,1)S(1)}, u32[]{:S(2)}, u32[]{:S(2)}) %all-to-all-start.1) | async-done | bytes 131104 | tf_op jit(solution)/shard_map/all_to_all | solution.py:354
  39.6 4.1 %couple_scatter.1 = (f32[2,8,24,384]{3,2,1,0:T(8,128)S(1)}, bf16[24,384]{1,0:T(8,128)(2,1)S(1)}, bf16[24,384]{1,0:T(8,128)(2,1)S(1)}) custom-call(s32[2]{0:T(128)S(1)} %pad_add_fusion.flag_ref, bf16[32,16,128]{2,1,0:T(8,128)(2,1)S(1)} %all-to-all-done.1.arrived_ref, bf16[8,136,128]{2,1,0:T(8,128)(2,1)S(1)} %all-to-all-done.early_ref), custom_call_target="tpu_custom_call" | custom-call | flops 4000000000 | bytes 12000000 | tf_op jit(solution)/shard_map/couple_scatter/pallas_call | solution.py:376
  43.7 0.7 collective-permute-start.1
  44.4 4.4 %collective-permute-start.2 = (bf16[24,384]{1,0:T(8,128)(2,1)S(1)}, bf16[24,384]{1,0:T(8,128)(2,1)S(1)}, u32[]{:S(2)}, u32[]{:S(2)}) collective-permute-start(bf16[24,384]{1,0:T(8,128)(2,1)S(1)} %get-tuple-element.17), channel_id=1, source_target_pairs={{8,16},{16,8},{24,32},{32,24},{40,48},{48,40},{56,64},{64,56},{72,... | collective-permute-start | bytes 55304 | tf_op jit(solution)/shard_map/ppermute | solution.py:394
  48.9 1.2 %part_filter.1.part_ref = bf16[8,2,24,384]{3,2,1,0:T(8,128)(2,1)S(1)} custom-call(f32[2,8,24,384]{3,2,1,0:T(8,128)S(1)} %get-tuple-element.18.part_ref, f32[3,2,8,256]{3,2,1,0:T(8,128)S(1)} %pad.4.resp_ref, bf16[384,512]{1,0:T(8,128)(2,1)S(1)} %copy-done.10, bf16[256,768]{1,0:T(8,128)(2,1)S(1)} %copy-done.9, f32[2,8,384]{2,1,0:T(8,128)S(1)} %copy-done.11), custom_call_target="tpu_custom_call" | custom-call | flops 3000000000 | bytes 9000000 | tf_op jit(solution)/shard_map/part_filter/pallas_call | solution.py:395
  50.1 0.0 collective-permute-done.1.first_ref
  50.1 2.1 %collective-permute-done.2.second_ref = bf16[24,384]{1,0:T(8,128)(2,1)S(1)} collective-permute-done((bf16[24,384]{1,0:T(8,128)(2,1)S(1)}, bf16[24,384]{1,0:T(8,128)(2,1)S(1)}, u32[]{:S(2)}, u32[]{:S(2)}) %collective-permute-start.2) | collective-permute-done | bytes 18464 | tf_op jit(solution)/shard_map/ppermute | solution.py:394
  52.2 1.0 %edge_filter.1 = bf16[8,80,384]{2,1,0:T(8,128)(2,1)S(1)} custom-call(s32[2]{0:T(128)S(1)} %pad_add_fusion.flag_ref, bf16[24,384]{1,0:T(8,128)(2,1)S(1)} %collective-permute-done.1.first_ref, bf16[24,384]{1,0:T(8,128)(2,1)S(1)} %collective-permute-done.2.second_ref, bf16[8,2,24,384]{3,2,1,0:T(8,128)(2,1)S(1)} %part_filter.1.part_ref, ...), custom_call_target="tpu_custom_call" | custom-call | flops 1000000000 | bytes 3000000 | tf_op jit(solution)/shard_map/edge_filter/pallas_call | solution.py:404
  53.2 0.0 copy-start.6
  53.2 0.0 copy-start.7
  53.2 17.1 %all_to_all.15.back_ref = bf16[8,80,384]{2,1,0:T(8,128)(2,1)S(1)} all-to-all(bf16[8,80,384]{2,1,0:T(8,128)(2,1)S(1)} %edge_filter.1), channel_id=1, replica_groups=mesh['comp'=2,'gx'=16,'gu'=4,'gv'=2] {'gu','gv'}, dimensions={0} | all-to-all | bytes 983040 | tf_op jit(solution)/shard_map/all_to_all | solution.py:413
  70.4 0.0 copy-done.6
  70.4 0.0 copy-done.7
  70.4 1.4 %final_step.1 = f32[1,8,24,384]{3,2,1,0:T(8,128)} custom-call(s32[2]{0:T(128)S(1)} %pad_add_fusion.flag_ref, f32[1,8,24,384]{3,2,1,0:T(8,128)S(1)} %copy-done.2, bf16[8,80,384]{2,1,0:T(8,128)(2,1)S(1)} %all_to_all.15.back_ref, f32[1,24,384]{2,1,0:T(8,128)S(1)} %copy-done.6, s32[24,384]{1,0:T(8,128)S(1)} %copy-done.7), custom_call_target="tpu_custom_call" | custom-call | flops 1000000000 | bytes 3000000 | tf_op jit(solution)/shard_map/final_step/pallas_call | solution.py:414
  (6 shorter events, 0.1 us)
Async XLA Ops:
  0.0 11.1 %copy-start = (f32[1,8,3072]{2,1,0:T(8,128)S(1)}, f32[1,8,3072]{2,1,0:T(8,128)}, u32[]{:S(2)}) copy-start(f32[1,8,3072]{2,1,0:T(8,128)} %param.13) | copy-start | bytes 294916
  0.0 1.0 %copy-start.1 = (f32[1,8,24,384]{3,2,1,0:T(8,128)S(1)}, f32[1,8,24,384]{3,2,1,0:T(8,128)}, u32[]{:S(2)}) copy-start(f32[1,8,24,384]{3,2,1,0:T(8,128)} %state_ref.3) | copy-start | bytes 884740
  1.0 0.8 %copy-start.3 = (s32[1,1,1,128,128]{4,3,2,1,0:T(8,128)S(1)}, s32[1,1,1,128,128]{4,3,2,1,0:T(8,128)}, u32[]{:S(2)}) copy-start(s32[1,1,1,128,128]{4,3,2,1,0:T(8,128)} %param.17) | copy-start | bytes 196612
  2.6 20.7 %all-to-all-start = ((bf16[8,136,128]{2,1,0:T(8,128)(2,1)}), bf16[8,136,128]{2,1,0:T(8,128)(2,1)S(1)}, u32[]{:S(2)}, u32[]{:S(2)}) async-start(bf16[8,136,128]{2,1,0:T(8,128)(2,1)} %early_pack.1), calls=%async_computation | async-start | bytes 557056 | tf_op jit(solution)/shard_map/all_to_all | solution.py:336
  11.4 0.7 %copy-start.12 = (bf16[32,256]{1,0:T(8,128)(2,1)S(1)}, bf16[32,256]{1,0:T(8,128)(2,1)}, u32[]{:S(2)}) copy-start(bf16[32,256]{1,0:T(8,128)(2,1)} %constant.45.clone.pick_ref) | copy-start | bytes 49156
  11.7 1.0 %copy-start.2 = (f32[1,8,24,384]{3,2,1,0:T(8,128)S(1)}, f32[1,8,24,384]{3,2,1,0:T(8,128)}, u32[]{:S(2)}) copy-start(f32[1,8,24,384]{3,2,1,0:T(8,128)} %state_ref.3) | copy-start | bytes 884740
  11.7 1.0 %copy-start.4 = (s32[1,1,1,128,128]{4,3,2,1,0:T(8,128)S(1)}, s32[1,1,1,128,128]{4,3,2,1,0:T(8,128)}, u32[]{:S(2)}) copy-start(s32[1,1,1,128,128]{4,3,2,1,0:T(8,128)} %param.16) | copy-start | bytes 196612
  11.7 0.9 %copy-start.5 = (f32[1,1,1,128,128]{4,3,2,1,0:T(8,128)S(1)}, f32[1,1,1,128,128]{4,3,2,1,0:T(8,128)}, u32[]{:S(2)}) copy-start(f32[1,1,1,128,128]{4,3,2,1,0:T(8,128)} %param.18) | copy-start | bytes 196612
  11.9 0.8 %copy-start.8 = (s32[1,1,1,128]{3,2,1,0:T(1,128)S(1)}, s32[1,1,1,128]{3,2,1,0:T(1,128)}, u32[]{:S(2)}) copy-start(s32[1,1,1,128]{3,2,1,0:T(1,128)} %param.19) | copy-start | bytes 1540
  12.6 19.9 %copy-start.10 = (bf16[384,512]{1,0:T(8,128)(2,1)S(1)}, bf16[384,512]{1,0:T(8,128)(2,1)}, u32[]{:S(2)}) copy-start(bf16[384,512]{1,0:T(8,128)(2,1)} %constant.46.clone.ahead_ref) | copy-start | bytes 1179652
  17.2 15.3 %copy-start.9 = (bf16[256,768]{1,0:T(8,128)(2,1)S(1)}, bf16[256,768]{1,0:T(8,128)(2,1)}, u32[]{:S(2)}) copy-start(bf16[256,768]{1,0:T(8,128)(2,1)} %constant.47.clone.back_ref) | copy-start | bytes 1179652
  23.3 1.5 %collective-permute-start = (bf16[32,16,128]{2,1,0:T(8,128)(2,1)S(1)}, bf16[32,16,128]{2,1,0:T(8,128)(2,1)}, u32[]{:S(2)}, u32[]{:S(2)}) collective-permute-start(bf16[32,16,128]{2,1,0:T(8,128)(2,1)S(1)} %couple_gather.1), channel_id=1, source_target_pairs={{0,128},{128,0},{1,129},{129,1},{2,130},{130,2},{3,131},{131,3},{4... | collective-permute-start | bytes 393224 | tf_op jit(solution)/shard_map/ppermute | solution.py:352
  23.4 9.1 %copy-start.11 = (f32[2,8,384]{2,1,0:T(8,128)S(1)}, f32[2,8,384]{2,1,0:T(8,128)}, u32[]{:S(2)}) copy-start(f32[2,8,384]{2,1,0:T(8,128)} %constant.48.clone.twiddle_ref) | copy-start | bytes 73732
  24.8 14.8 %all-to-all-start.1 = ((bf16[32,16,128]{2,1,0:T(8,128)(2,1)}), bf16[32,16,128]{2,1,0:T(8,128)(2,1)S(1)}, u32[]{:S(2)}, u32[]{:S(2)}) async-start(bf16[32,16,128]{2,1,0:T(8,128)(2,1)} %collective-permute-done), calls=%async_computation.1 | async-start | bytes 262144 | tf_op jit(solution)/shard_map/all_to_all | solution.py:354
  43.7 6.3 %collective-permute-start.1 = (bf16[24,384]{1,0:T(8,128)(2,1)S(1)}, bf16[24,384]{1,0:T(8,128)(2,1)S(1)}, u32[]{:S(2)}, u32[]{:S(2)}) collective-permute-start(bf16[24,384]{1,0:T(8,128)(2,1)S(1)} %get-tuple-element.16), channel_id=1, source_target_pairs={{0,8},{8,0},{16,24},{24,16},{32,40},{40,32},{48,56},{56,48},{64,72... | collective-permute-start | bytes 55304 | tf_op jit(solution)/shard_map/ppermute | solution.py:393
  44.4 7.8 %collective-permute-start.2 = (bf16[24,384]{1,0:T(8,128)(2,1)S(1)}, bf16[24,384]{1,0:T(8,128)(2,1)S(1)}, u32[]{:S(2)}, u32[]{:S(2)}) collective-permute-start(bf16[24,384]{1,0:T(8,128)(2,1)S(1)} %get-tuple-element.17), channel_id=1, source_target_pairs={{8,16},{16,8},{24,32},{32,24},{40,48},{48,40},{56,64},{64,56},{72,... | collective-permute-start | bytes 55304 | tf_op jit(solution)/shard_map/ppermute | solution.py:394
  53.2 17.2 %copy-start.6 = (f32[1,24,384]{2,1,0:T(8,128)S(1)}, f32[1,24,384]{2,1,0:T(8,128)}, u32[]{:S(2)}) copy-start(f32[1,24,384]{2,1,0:T(8,128)} %rate_ref.1) | copy-start | bytes 110596
  53.2 17.1 %copy-start.7 = (s32[24,384]{1,0:T(8,128)S(1)}, s32[24,384]{1,0:T(8,128)}, u32[]{:S(2)}) copy-start(s32[24,384]{1,0:T(8,128)} %land_ref.1) | copy-start | bytes 110596

commit v4 on v3

--- a/solution.py
+++ b/solution.py
@@ -15,12 +15,14 @@
 F32 = jnp.float32
 VMEM = pl.BlockSpec(memory_space=pltpu.VMEM)
 SMEM = pl.BlockSpec(memory_space=pltpu.SMEM)
+HBM = pl.BlockSpec(memory_space=pltpu.HBM)
+LARGE = pltpu.CompilerParams(vmem_limit_bytes=60 * 2**20)
 PARAMS = pltpu.CompilerParams(vmem_limit_bytes=32 * 2**20)
 
 
 def one_hot(rows, index):
-    spot = lax.broadcasted_iota(jnp.int32, (rows, index.shape[1]), 0)
-    return jnp.where(spot == index, 1.0, 0.0)
+    spot = lax.broadcasted_iota(jnp.int16, (rows, index.shape[1]), 0)
+    return jnp.where(spot == index.astype(jnp.int16), jnp.asarray(1, BF), jnp.asarray(0, BF))
 
 
 def split_cell(idx, cols):
@@ -42,56 +44,88 @@
     return jnp.concatenate([block[t : t + rows] for t in range(0, block.shape[0], rows)], axis=1)
 
 
-def pack_kernel(split, state_ref, dst_ref, out_ref):
+def give_kernel(count_ref, state_hbm, src_hbm, weight_hbm, give_ref, state_ref, src_ref, weight_ref, sems):
+    copies = [
+        pltpu.make_async_copy(state_hbm.at[0, :FC], state_ref, sems.at[0]),
+        pltpu.make_async_copy(src_hbm, src_ref, sems.at[1]),
+        pltpu.make_async_copy(weight_hbm, weight_ref, sems.at[2]),
+    ]
+    for copy in copies:
+        copy.start()
+    for copy in copies:
+        copy.wait()
+    _, rows, cols = state_ref.shape
+    peers, slots = src_ref.shape
+    start = FC * rows * cols // LANES
+    give_ref[:start] = jnp.concatenate([tiles(state_ref[c]) for c in range(FC)], axis=0).astype(BF)
+    line, lane = split_lines(src_ref[...], rows, cols)
+    give_ref[start : start + peers] = line.astype(F32).astype(BF)
+    give_ref[start + peers : start + 2 * peers] = lane.astype(F32).astype(BF)
+    slot = lax.broadcasted_iota(jnp.int32, (8, slots), 1)
+    sub = lax.broadcasted_iota(jnp.int32, (8, slots), 0)
+    weights = []
+    for base in range(0, peers, 8):
+        limit = jnp.zeros((8, slots), jnp.int32)
+        for i in range(8):
+            limit = jnp.where(sub == i, count_ref[base + i], limit)
+        weights.append(jnp.where(slot < limit, weight_ref[base : base + 8, :], 0.0))
+    give_ref[start + 2 * peers :] = jnp.concatenate(weights, axis=0).astype(BF)
+
+
+def pack_kernel(split, state_hbm, dst_hbm, early_ref, state_ref, dst_ref, sems):
+    copies = [
+        pltpu.make_async_copy(dst_hbm, dst_ref, sems.at[0]),
+        pltpu.make_async_copy(state_hbm, state_ref, sems.at[1]),
+    ]
+    for copy in copies:
+        copy.start()
+    for copy in copies:
+        copy.wait()
     _, levels, rows, cols = state_ref.shape
-    peers, slots = dst_ref.shape
-    groups = peers // levels
-    for h in range(levels):
-        idx = dst_ref[pl.ds(h, groups, stride=levels), :]
-        line, lane = split_lines(idx, rows, cols)
+    groups, blocks, slots = dst_ref.shape
+    for h in range(blocks):
+        line, lane = split_lines(dst_ref[:, h, :], rows, cols)
         line, lane = line.astype(F32).astype(BF), lane.astype(F32).astype(BF)
         u, other = h // split, h % split
         for v in range(split):
             piece = u * split + v
-            out_ref[piece, pl.ds(other * groups, groups), :] = line
-            out_ref[piece, pl.ds((split + other) * groups, groups), :] = lane
-        out_ref[h, pl.ds(2 * split * groups, rows * cols // LANES), :] = tiles(state_ref[0, h]).astype(BF)
-
-
-def gather_kernel(split, blocks, count_ref, surf_ref, src_ref, weight_ref, pick_ref, out_ref):
-    _, _, rows, cols = surf_ref.shape
-    peers, slots = src_ref.shape
+            early_ref[piece, other * groups : (other + 1) * groups, :] = line
+            early_ref[piece, (split + other) * groups : (split + other + 1) * groups, :] = lane
+        early_ref[h, 2 * split * groups :, :] = tiles(state_ref[0, h]).astype(BF)
+
+
+def gather_kernel(split, blocks, lines, got_ref, pick_ref, out_ref, line_ref, lane_ref, weight_ref):
+    peers, slots = line_ref.shape
     fc = split * out_ref.shape[1] // blocks
     each = fc // split * blocks
-    lines = rows * cols // LANES
+    start = fc * lines
     half = -(-lines // 16) * 8
     shift = lines - half
-    surface = [tiles(surf_ref[0, c]) for c in range(fc)]
+    surface = got_ref[:start].astype(F32)
+    surface = [surface[c * lines : (c + 1) * lines] for c in range(fc)]
     surface = jnp.concatenate([jnp.concatenate([x[:half], x[shift:]], axis=1) for x in surface], axis=0).astype(BF)
-    lane = lax.broadcasted_iota(jnp.int32, (blocks, slots), 1)
-    sub = lax.broadcasted_iota(jnp.int32, (blocks, slots), 0)
+    line = got_ref[start : start + peers].astype(F32).astype(jnp.int32)
+    lane = got_ref[start + peers : start + 2 * peers].astype(F32).astype(jnp.int32)
+    upper = line >= half
+    line_ref[...] = line - jnp.where(upper, shift, 0)
+    lane_ref[...] = lane + jnp.where(upper, LANES, 0)
+    weight_ref[...] = got_ref[start + 2 * peers :].astype(F32)
     spot = lax.broadcasted_iota(jnp.int32, (half, slots), 0)
 
     def step(g, carry):
         base = pl.multiple_of(g * blocks, blocks)
-        line, col = split_lines(src_ref[pl.ds(base, blocks), :], rows, cols)
-        upper = line >= half
-        line = line - jnp.where(upper, shift, 0)
-        col = col + jnp.where(upper, LANES, 0)
+        line = line_ref[pl.ds(base, blocks), :]
+        lane = lane_ref[pl.ds(base, blocks), :]
         found = []
         for i in range(0, blocks, 2):
-            pick = jnp.concatenate([one_hot(2 * LANES, col[j : j + 1]) for j in (i, i + 1)], axis=1)
-            values = jnp.dot(surface, pick.astype(BF), preferred_element_type=F32)
+            pick = jnp.concatenate([one_hot(2 * LANES, lane[j : j + 1]) for j in (i, i + 1)], axis=1)
+            values = jnp.dot(surface, pick, preferred_element_type=F32)
             for j in range(2):
                 own = values[:, j * slots : (j + 1) * slots].reshape(fc, half, slots)
                 own = jnp.where((spot == line[i + j : i + j + 1])[None], own, 0.0)
                 found.append(jnp.sum(own.reshape(fc, half // 8, 8, slots), axis=1).reshape(fc * 8, slots))
         value = jnp.dot(pick_ref[...], jnp.concatenate(found, axis=0).astype(BF), preferred_element_type=F32)
-        limit = jnp.zeros((blocks, slots), jnp.int32)
-        for i in range(blocks):
-            limit = jnp.where(sub == i, count_ref[base + i], limit)
-        weight = jnp.where(lane < limit, weight_ref[pl.ds(base, blocks), :], 0.0)
-        value = value * jnp.concatenate([weight] * fc, axis=0)
+        value = value * jnp.concatenate([weight_ref[pl.ds(base, blocks), :]] * fc, axis=0)
         for v in range(split):
             out_ref[g * split + v] = value[v * each : (v + 1) * each].astype(BF)
         return carry
@@ -124,18 +158,19 @@
     acc_ref[...] = jnp.zeros_like(acc_ref)
     spot = lax.broadcasted_iota(jnp.int32, (lines, slots), 0)
 
-    def step(g, carry):
+    def step(pair, carry):
         for h in range(blocks):
             spread, pick = [], []
-            for v in range(split):
-                at = v * groups + g
-                mask = spot == line_ref[h, pl.ds(at, 1), :]
-                vals = [
-                    jnp.where(mask, value_ref[g * split + v, c * blocks + h : c * blocks + h + 1, :], 0.0)
-                    for c in range(fields)
-                ]
-                spread.append(jnp.concatenate(vals, axis=0).astype(BF))
-                pick.append(one_hot(LANES, lane_ref[h, pl.ds(at, 1), :]).astype(BF))
+            for g in (2 * pair, 2 * pair + 1):
+                for v in range(split):
+                    at = v * groups + g
+                    mask = spot == line_ref[h, pl.ds(at, 1), :]
+                    vals = [
+                        jnp.where(mask, value_ref[g * split + v, c * blocks + h : c * blocks + h + 1, :], 0.0)
+                        for c in range(fields)
+                    ]
+                    spread.append(jnp.concatenate(vals, axis=0).astype(BF))
+                    pick.append(one_hot(LANES, lane_ref[h, pl.ds(at, 1), :]))
             acc_ref[h] += lax.dot_general(
                 jnp.concatenate(spread, axis=1),
                 jnp.concatenate(pick, axis=1),
@@ -144,7 +179,7 @@
             )
         return carry
 
-    lax.fori_loop(0, groups, step, 0, unroll=4)
+    lax.fori_loop(0, groups // 2, step, 0, unroll=4)
     tops, bottoms = [], []
     for c in range(fields + 1):
         for h in range(blocks):
@@ -321,18 +356,39 @@
     gv = lax.axis_index("gv")
     own = lax.axis_index("gu") * split + gv
     src_idx = couple_src.reshape(peers, slots)
-    dst_idx = couple_dst.reshape(peers, slots)
     weight = couple_weight.reshape(peers, slots)
     count = couple_count.reshape(peers)
 
+    give = pl.pallas_call(
+        give_kernel,
+        out_shape=jax.ShapeDtypeStruct((FC * cell_rows + 3 * peers, LANES), BF),
+        in_specs=[SMEM] + [HBM] * 3,
+        out_specs=VMEM,
+        scratch_shapes=[
+            pltpu.VMEM((FC, rows, cols), F32),
+            pltpu.VMEM((peers, slots), jnp.int32),
+            pltpu.VMEM((peers, slots), F32),
+            pltpu.SemaphoreType.DMA((3,)),
+        ],
+        compiler_params=LARGE,
+        cost_estimate=cost(1),
+        name="give_pack",
+    )(count, state, src_idx, weight)
+    got = lax.ppermute(give, "comp", [(0, 1), (1, 0)])
     early = pl.pallas_call(
         functools.partial(pack_kernel, split),
         out_shape=jax.ShapeDtypeStruct((blocks, 2 * senders + cell_rows, LANES), BF),
-        in_specs=[VMEM, VMEM],
-        out_specs=VMEM,
-        compiler_params=PARAMS,
+        in_specs=[HBM] * 2,
+        out_specs=VMEM,
+        scratch_shapes=[
+            pltpu.VMEM(state.shape, F32),
+            pltpu.VMEM((groups_x, blocks, slots), jnp.int32),
+            pltpu.SemaphoreType.DMA((2,)),
+        ],
+        compiler_params=LARGE,
+        cost_estimate=cost(1),
         name="early_pack",
-    )(state, dst_idx)
+    )(state, couple_dst.reshape(groups_x, blocks, slots))
     early = lax.all_to_all(early, ("gu", "gv"), split_axis=0, concat_axis=0, tiled=True)
 
     spot = np.zeros((FC, blocks, blocks, FC, 8), np.float32)
@@ -340,18 +396,21 @@
         for h in range(blocks):
             spot[c, h, h, c] = 1.0
     outgoing = pl.pallas_call(
-        functools.partial(gather_kernel, split, blocks),
+        functools.partial(gather_kernel, split, blocks, cell_rows),
         out_shape=jax.ShapeDtypeStruct((senders, each * blocks, slots), BF),
-        in_specs=[SMEM, VMEM, VMEM, VMEM, VMEM],
-        out_specs=VMEM,
+        in_specs=[VMEM, VMEM],
+        out_specs=VMEM,
+        scratch_shapes=[
+            pltpu.VMEM((peers, slots), jnp.int32),
+            pltpu.VMEM((peers, slots), jnp.int32),
+            pltpu.VMEM((peers, slots), F32),
+        ],
         compiler_params=PARAMS,
         cost_estimate=cost(4),
         name="couple_gather",
-    )(count, state, src_idx, weight, jnp.asarray(spot.reshape(FC * blocks, -1), BF))
+    )(got, jnp.asarray(spot.reshape(FC * blocks, -1), BF))
     outgoing, early = lax.optimization_barrier((outgoing, early))
-    crossed = lax.ppermute(outgoing, "comp", [(0, 1), (1, 0)])
-    crossed, early = lax.optimization_barrier((crossed, early))
-    arrived = lax.all_to_all(crossed, ("gx", "gv"), split_axis=0, concat_axis=0, tiled=True)
+    arrived = lax.all_to_all(outgoing, ("gx", "gv"), split_axis=0, concat_axis=0, tiled=True)
 
     ahead, back, twiddle = zonal_tables(blocks, cols, waves)
     half = cols_all // 2 // blocks
@@ -391,7 +450,6 @@
     pairs = [(i, i ^ 1) for i in range(groups_x)]
     cross = [pair for i in range(1, groups_x - 1, 2) for pair in ((i, i + 1), (i + 1, i))]
     first = lax.ppermute(first, "gx", pairs)
-    second = lax.ppermute(second, "gx", cross)
     part = pl.pallas_call(
         functools.partial(part_kernel, scale),
         out_shape=jax.ShapeDtypeStruct((blocks, each, rows, cols), BF),
@@ -401,6 +459,8 @@
         cost_estimate=cost(3),
         name="part_filter",
     )(part, resp, ahead, back, twiddle)
+    second, part = lax.optimization_barrier((second, part))
+    second = lax.ppermute(second, "gx", cross)
     incr = pl.pallas_call(
         functools.partial(edge_kernel, scale),
         out_shape=jax.ShapeDtypeStruct((blocks, (each + 1) * rows + 8, cols), BF),

time: 72.3 us -> 74.5 us (1.030)
  Pallas kernels: 13.9 us -> 17.6 us
  local copies, waits for them, and re-layouts: 3.34 us -> 1.27 us
    pallas_call x1 -> x2, Pallas kernels: 4.58 us -> 7.22 us  [the longest x1 4.68 us: local(): pl.pallas_call(functools.partial(gather_kernel, split, blocks, cell_rows)...]
    unnamed x26 -> x16, local copies, waits for them, and re-layouts: 2.66 us -> 0.59 us
    pallas_call x1, Pallas kernels: 0.8 us -> 2.43 us  [local(): pl.pallas_call(functools.partial(pack_kernel, split), out_shape=jax.Shape...]
    ppermute x1, waiting for transfers between devices: 1.41 us -> 0.01 us  [local(): got = lax.ppermute(give, 'comp', [(0, 1), (1, 0)])]
    all_to_all x1, waiting for transfers between devices: 6.1 us -> 6.93 us  [local(): lax.all_to_all(early, ('gu', 'gv'), split_axis=0, concat_axis=0, tiled=True)]
  transfers between devices with their start and end apart: 5 -> 5, of which waited for: 4 -> 3; matrix products, arithmetic and copies ran while one was open for 1% -> 1% of each run, Pallas kernels for 9% -> 12%
where the time goes in v4:
time: 74.5 us; the launch traced here: 74.1 us
  starting transfers between devices  21.3 us (29%)
  Pallas kernels  17.6 us (24%)
  blocking collectives  17.1 us (23%)
  waiting for transfers between devices  16.5 us (22%)
  local copies, waits for them, and re-layouts  1.27 us (2%)
    all_to_all x1, blocking collectives, local(): lax.all_to_all(incr, ('gu', 'gv'), split_axis=0, concat_axis=0, tiled=True)  17.1 us
    all_to_all x1, starting transfers between devices, local(): lax.all_to_all(early, ('gu', 'gv'), split_axis=0, concat_axis=0, tiled=True)  8.48 us
    all_to_all x1, starting transfers between devices, local(): lax.all_to_all(outgoing, ('gx', 'gv'), split_axis=0, concat_axis=0, tiled...  7.62 us
    all_to_all x1, waiting for transfers between devices, local(): lax.all_to_all(outgoing, ('gx', 'gv'), split_axis=0, concat_axis=0, tiled...  7.02 us
    all_to_all x1, waiting for transfers between devices, local(): lax.all_to_all(early, ('gu', 'gv'), split_axis=0, concat_axis=0, tiled=True)  6.93 us
    pallas_call x1, Pallas kernels, local(): pl.pallas_call(functools.partial(gather_kernel, split, blocks, cell_rows)...  4.68 us
    ppermute x1, starting transfers between devices, local(): second = lax.ppermute(second, 'gx', cross)  4.44 us
    pallas_call x1, Pallas kernels, local(): pl.pallas_call(functools.partial(scatter_kernel, split), out_shape=(jax.S...  3.45 us
  transfers between devices with their start and end apart: 5, of which 3 were waited for; matrix products, arithmetic and copies ran while one was open for 1% of the time, Pallas kernels for 12%

profile of v4, /device:TPU:2, one launch (start us, length us, event | category | flops | bytes accessed | tf_op | source)
XLA Modules:
  0.0 74.1 jit_solution(10674856095539083532)
XLA Ops:
  0.0 0.0 copy-start
  0.0 2.5 %give_pack.1 = bf16[672,128]{1,0:T(8,128)(2,1)} custom-call(s32[128]{0:T(128)} %bitcast.13, f32[1,8,24,384]{3,2,1,0:T(8,128)} %state_ref.1, s32[128,128]{1,0:T(8,128)} %bitcast.10, f32[128,128]{1,0:T(8,128)} %bitcast.11), custom_call_target="tpu_custom_call" | custom-call | flops 1000000000 | bytes 3000000 | tf_op jit(solution)/shard_map/give_pack/pallas_call | solution.py:362
  2.6 0.1 collective-permute-start
  2.7 2.4 %early_pack.1 = bf16[8,136,128]{2,1,0:T(8,128)(2,1)} custom-call(f32[1,8,24,384]{3,2,1,0:T(8,128)} %state_ref.1, s32[16,8,128]{2,1,0:T(8,128)} %bitcast.12), custom_call_target="tpu_custom_call" | custom-call | flops 1000000000 | bytes 3000000 | tf_op jit(solution)/shard_map/early_pack/pallas_call | solution.py:378
  5.1 8.5 %all-to-all-start = ((bf16[8,136,128]{2,1,0:T(8,128)(2,1)}), bf16[8,136,128]{2,1,0:T(8,128)(2,1)S(1)}, u32[]{:S(2)}, u32[]{:S(2)}) async-start(bf16[8,136,128]{2,1,0:T(8,128)(2,1)} %early_pack.1), calls=%async_computation | async-start | bytes 557056 | tf_op jit(solution)/shard_map/all_to_all | solution.py:392
  13.6 0.0 copy-done
  13.7 0.1 concatenate.9
  13.8 0.1 copy.14
  13.9 0.2 concatenate.8
  14.1 0.0 copy-start.7
  14.1 0.2 copy.13
  14.3 0.0 collective-permute-done.got_ref
  14.3 0.5 copy-done.7
  14.9 4.7 %couple_gather.1 = bf16[32,16,128]{2,1,0:T(8,128)(2,1)} custom-call(bf16[672,128]{1,0:T(8,128)(2,1)S(1)} %collective-permute-done.got_ref, bf16[32,256]{1,0:T(8,128)(2,1)S(1)} %copy-done.7), custom_call_target="tpu_custom_call" | custom-call | flops 4000000000 | bytes 12000000 | tf_op jit(solution)/shard_map/couple_gather/pallas_call | solution.py:398
  19.5 6.9 %all-to-all-done.early_ref = bf16[8,136,128]{2,1,0:T(8,128)(2,1)S(1)} async-done(((bf16[8,136,128]{2,1,0:T(8,128)(2,1)}), bf16[8,136,128]{2,1,0:T(8,128)(2,1)S(1)}, u32[]{:S(2)}, u32[]{:S(2)}) %all-to-all-start) | async-done | bytes 278560 | tf_op jit(solution)/shard_map/all_to_all | solution.py:392
  26.5 7.6 %all-to-all-start.1 = ((bf16[32,16,128]{2,1,0:T(8,128)(2,1)}), bf16[32,16,128]{2,1,0:T(8,128)(2,1)S(1)}, u32[]{:S(2)}, u32[]{:S(2)}) async-start(bf16[32,16,128]{2,1,0:T(8,128)(2,1)} %couple_gather.1), calls=%async_computation.1 | async-start | bytes 262144 | tf_op jit(solution)/shard_map/all_to_all | solution.py:413
  34.1 0.1 pad_add_fusion.flag_ref
  34.2 0.0 copy-start.4
  34.2 0.0 copy-start.5
  34.2 0.0 copy-start.6
  34.2 7.0 %all-to-all-done.1.arrived_ref = bf16[32,16,128]{2,1,0:T(8,128)(2,1)S(1)} async-done(((bf16[32,16,128]{2,1,0:T(8,128)(2,1)}), bf16[32,16,128]{2,1,0:T(8,128)(2,1)S(1)}, u32[]{:S(2)}, u32[]{:S(2)}) %all-to-all-start.1) | async-done | bytes 131104 | tf_op jit(solution)/shard_map/all_to_all | solution.py:413
  41.3 3.4 %couple_scatter.1 = (f32[2,8,24,384]{3,2,1,0:T(8,128)S(1)}, bf16[24,384]{1,0:T(8,128)(2,1)S(1)}, bf16[24,384]{1,0:T(8,128)(2,1)S(1)}) custom-call(s32[2]{0:T(128)S(1)} %pad_add_fusion.flag_ref, bf16[32,16,128]{2,1,0:T(8,128)(2,1)S(1)} %all-to-all-done.1.arrived_ref, bf16[8,136,128]{2,1,0:T(8,128)(2,1)S(1)} %all-to-all-done.early_ref), custom_call_target="tpu_custom_call" | custom-call | flops 4000000000 | bytes 12000000 | tf_op jit(solution)/shard_map/couple_scatter/pallas_call | solution.py:435
  44.7 0.7 collective-permute-start.1
  45.4 0.0 copy-done.4
  45.4 0.0 copy-done.5
  45.4 0.0 copy-done.6
  45.4 1.3 %part_filter.1.part_ref = bf16[8,2,24,384]{3,2,1,0:T(8,128)(2,1)S(1)} custom-call(f32[2,8,24,384]{3,2,1,0:T(8,128)S(1)} %get-tuple-element.16.part_ref, f32[3,2,8,256]{3,2,1,0:T(8,128)S(1)} %pad.4.resp_ref, bf16[384,512]{1,0:T(8,128)(2,1)S(1)} %copy-done.5, bf16[256,768]{1,0:T(8,128)(2,1)S(1)} %copy-done.4, f32[2,8,384]{2,1,0:T(8,128)S(1)} %copy-done.6), custom_call_target="tpu_custom_call" | custom-call | flops 3000000000 | bytes 9000000 | tf_op jit(solution)/shard_map/part_filter/pallas_call | solution.py:453
  46.7 4.4 %collective-permute-start.2 = (bf16[24,384]{1,0:T(8,128)(2,1)S(1)}, bf16[24,384]{1,0:T(8,128)(2,1)S(1)}, u32[]{:S(2)}, u32[]{:S(2)}) collective-permute-start(bf16[24,384]{1,0:T(8,128)(2,1)S(1)} %get-tuple-element.17), channel_id=1, source_target_pairs={{8,16},{16,8},{24,32},{32,24},{40,48},{48,40},{56,64},{64,56},{72,... | collective-permute-start | bytes 55304 | tf_op jit(solution)/shard_map/ppermute | solution.py:463
  51.1 0.8 %circle_filter.1.circle_ref = bf16[8,24,384]{2,1,0:T(8,128)(2,1)S(1)} custom-call(bf16[8,136,128]{2,1,0:T(8,128)(2,1)S(1)} %all-to-all-done.early_ref, f32[2,8,256]{2,1,0:T(8,128)S(1)} %slice_bitcast_fusion.resp_ref, bf16[384,512]{1,0:T(8,128)(2,1)S(1)} %copy-done.5, bf16[256,768]{1,0:T(8,128)(2,1)S(1)} %copy-done.4, f32[2,8,384]{2,1,0:T(8,128)S(1)} %copy-done.6), custom_call_target="tpu_custom_call" | custom-call | flops 2000000000 | bytes 6000000 | tf_op jit(solution)/shard_map/circle_filter/pallas_call | solution.py:425
  51.9 0.0 collective-permute-done.1.first_ref
  51.9 2.5 %collective-permute-done.2.second_ref = bf16[24,384]{1,0:T(8,128)(2,1)S(1)} collective-permute-done((bf16[24,384]{1,0:T(8,128)(2,1)S(1)}, bf16[24,384]{1,0:T(8,128)(2,1)S(1)}, u32[]{:S(2)}, u32[]{:S(2)}) %collective-permute-start.2) | collective-permute-done | bytes 18464 | tf_op jit(solution)/shard_map/ppermute | solution.py:463
  54.4 1.0 %edge_filter.1 = bf16[8,80,384]{2,1,0:T(8,128)(2,1)S(1)} custom-call(s32[2]{0:T(128)S(1)} %pad_add_fusion.flag_ref, bf16[24,384]{1,0:T(8,128)(2,1)S(1)} %collective-permute-done.1.first_ref, bf16[24,384]{1,0:T(8,128)(2,1)S(1)} %collective-permute-done.2.second_ref, bf16[8,2,24,384]{3,2,1,0:T(8,128)(2,1)S(1)} %part_filter.1.part_ref, ...), custom_call_target="tpu_custom_call" | custom-call | flops 1000000000 | bytes 3000000 | tf_op jit(solution)/shard_map/edge_filter/pallas_call | solution.py:464
  55.5 0.0 copy-start.1
  55.5 0.0 copy-start.2
  55.5 0.0 copy-start.3
  55.5 17.1 %all_to_all.15.back_ref = bf16[8,80,384]{2,1,0:T(8,128)(2,1)S(1)} all-to-all(bf16[8,80,384]{2,1,0:T(8,128)(2,1)S(1)} %edge_filter.1), channel_id=1, replica_groups=mesh['comp'=2,'gx'=16,'gu'=4,'gv'=2] {'gu','gv'}, dimensions={0} | all-to-all | bytes 983040 | tf_op jit(solution)/shard_map/all_to_all | solution.py:473
  72.6 0.0 copy-done.1
  72.6 0.0 copy-done.2
  72.6 0.0 copy-done.3
  72.6 1.4 %final_step.1 = f32[1,8,24,384]{3,2,1,0:T(8,128)} custom-call(s32[2]{0:T(128)S(1)} %pad_add_fusion.flag_ref, f32[1,8,24,384]{3,2,1,0:T(8,128)S(1)} %copy-done.1, bf16[8,80,384]{2,1,0:T(8,128)(2,1)S(1)} %all_to_all.15.back_ref, f32[1,24,384]{2,1,0:T(8,128)S(1)} %copy-done.2, s32[24,384]{1,0:T(8,128)S(1)} %copy-done.3), custom_call_target="tpu_custom_call" | custom-call | flops 1000000000 | bytes 3000000 | tf_op jit(solution)/shard_map/final_step/pallas_call | solution.py:474
  (5 shorter events, 0.1 us)
Async XLA Ops:
  0.0 13.6 %copy-start = (f32[1,8,3072]{2,1,0:T(8,128)S(1)}, f32[1,8,3072]{2,1,0:T(8,128)}, u32[]{:S(2)}) copy-start(f32[1,8,3072]{2,1,0:T(8,128)} %param.13) | copy-start | bytes 294916
  2.6 11.7 %collective-permute-start = (bf16[672,128]{1,0:T(8,128)(2,1)}, bf16[672,128]{1,0:T(8,128)(2,1)S(1)}, u32[]{:S(2)}, u32[]{:S(2)}) collective-permute-start(bf16[672,128]{1,0:T(8,128)(2,1)} %give_pack.1), channel_id=1, source_target_pairs={{0,128},{128,0},{1,129},{129,1},{2,130},{130,2},{3,131},{131,3},{4... | collective-permute-start | bytes 516104 | tf_op jit(solution)/shard_map/ppermute | solution.py:377
  5.1 21.4 %all-to-all-start = ((bf16[8,136,128]{2,1,0:T(8,128)(2,1)}), bf16[8,136,128]{2,1,0:T(8,128)(2,1)S(1)}, u32[]{:S(2)}, u32[]{:S(2)}) async-start(bf16[8,136,128]{2,1,0:T(8,128)(2,1)} %early_pack.1), calls=%async_computation | async-start | bytes 557056 | tf_op jit(solution)/shard_map/all_to_all | solution.py:392
  14.1 0.7 copy-start.7
  26.5 14.8 %all-to-all-start.1 = ((bf16[32,16,128]{2,1,0:T(8,128)(2,1)}), bf16[32,16,128]{2,1,0:T(8,128)(2,1)S(1)}, u32[]{:S(2)}, u32[]{:S(2)}) async-start(bf16[32,16,128]{2,1,0:T(8,128)(2,1)} %couple_gather.1), calls=%async_computation.1 | async-start | bytes 262144 | tf_op jit(solution)/shard_map/all_to_all | solution.py:413
  34.2 11.2 %copy-start.4 = (bf16[256,768]{1,0:T(8,128)(2,1)S(1)}, bf16[256,768]{1,0:T(8,128)(2,1)}, u32[]{:S(2)}) copy-start(bf16[256,768]{1,0:T(8,128)(2,1)} %constant.47.clone.back_ref) | copy-start | bytes 1179652
  34.2 11.2 %copy-start.5 = (bf16[384,512]{1,0:T(8,128)(2,1)S(1)}, bf16[384,512]{1,0:T(8,128)(2,1)}, u32[]{:S(2)}) copy-start(bf16[384,512]{1,0:T(8,128)(2,1)} %constant.46.clone.ahead_ref) | copy-start | bytes 1179652
  34.2 11.2 %copy-start.6 = (f32[2,8,384]{2,1,0:T(8,128)S(1)}, f32[2,8,384]{2,1,0:T(8,128)}, u32[]{:S(2)}) copy-start(f32[2,8,384]{2,1,0:T(8,128)} %constant.48.clone.twiddle_ref) | copy-start | bytes 73732
  44.7 7.2 %collective-permute-start.1 = (bf16[24,384]{1,0:T(8,128)(2,1)S(1)}, bf16[24,384]{1,0:T(8,128)(2,1)S(1)}, u32[]{:S(2)}, u32[]{:S(2)}) collective-permute-start(bf16[24,384]{1,0:T(8,128)(2,1)S(1)} %get-tuple-element.14), channel_id=1, source_target_pairs={{0,8},{8,0},{16,24},{24,16},{32,40},{40,32},{48,56},{56,48},{64,72... | collective-permute-start | bytes 55304 | tf_op jit(solution)/shard_map/ppermute | solution.py:452
  46.7 7.8 %collective-permute-start.2 = (bf16[24,384]{1,0:T(8,128)(2,1)S(1)}, bf16[24,384]{1,0:T(8,128)(2,1)S(1)}, u32[]{:S(2)}, u32[]{:S(2)}) collective-permute-start(bf16[24,384]{1,0:T(8,128)(2,1)S(1)} %get-tuple-element.17), channel_id=1, source_target_pairs={{8,16},{16,8},{24,32},{32,24},{40,48},{48,40},{56,64},{64,56},{72,... | collective-permute-start | bytes 55304 | tf_op jit(solution)/shard_map/ppermute | solution.py:463
  55.5 17.2 %copy-start.1 = (f32[1,8,24,384]{3,2,1,0:T(8,128)S(1)}, f32[1,8,24,384]{3,2,1,0:T(8,128)}, u32[]{:S(2)}) copy-start(f32[1,8,24,384]{3,2,1,0:T(8,128)} %state_ref.1) | copy-start | bytes 884740
  55.5 17.1 %copy-start.2 = (f32[1,24,384]{2,1,0:T(8,128)S(1)}, f32[1,24,384]{2,1,0:T(8,128)}, u32[]{:S(2)}) copy-start(f32[1,24,384]{2,1,0:T(8,128)} %rate_ref.1) | copy-start | bytes 110596
  55.5 17.1 %copy-start.3 = (s32[24,384]{1,0:T(8,128)S(1)}, s32[24,384]{1,0:T(8,128)}, u32[]{:S(2)}) copy-start(s32[24,384]{1,0:T(8,128)} %land_ref.1) | copy-start | bytes 110596

commit v5 on v3

--- a/solution.py
+++ b/solution.py
@@ -15,12 +15,14 @@
 F32 = jnp.float32
 VMEM = pl.BlockSpec(memory_space=pltpu.VMEM)
 SMEM = pl.BlockSpec(memory_space=pltpu.SMEM)
+HBM = pl.BlockSpec(memory_space=pltpu.HBM)
+LARGE = pltpu.CompilerParams(vmem_limit_bytes=60 * 2**20)
 PARAMS = pltpu.CompilerParams(vmem_limit_bytes=32 * 2**20)
 
 
 def one_hot(rows, index):
-    spot = lax.broadcasted_iota(jnp.int32, (rows, index.shape[1]), 0)
-    return jnp.where(spot == index, 1.0, 0.0)
+    spot = lax.broadcasted_iota(jnp.int16, (rows, index.shape[1]), 0)
+    return jnp.where(spot == index.astype(jnp.int16), jnp.asarray(1, BF), jnp.asarray(0, BF))
 
 
 def split_cell(idx, cols):
@@ -34,6 +36,17 @@
     return tile * rows + row, col - tile * LANES
 
 
+def encode_cell(idx, rows, cols):
+    line, lane = split_lines(idx, rows, cols)
+    return (lane + LANES).astype(F32) * jnp.exp2((line - 36).astype(F32))
+
+
+def decode_cell(code):
+    top = jnp.floor(jnp.log2(code) + 0.003)
+    lane = code * jnp.exp2(-top) * LANES - LANES + 0.5
+    return (top + 29.0).astype(jnp.int32), lane.astype(jnp.int32)
+
+
 def tiles(block):
     return jnp.concatenate([block[:, t : t + LANES] for t in range(0, block.shape[1], LANES)], axis=0)
 
@@ -42,20 +55,24 @@
     return jnp.concatenate([block[t : t + rows] for t in range(0, block.shape[0], rows)], axis=1)
 
 
-def pack_kernel(split, state_ref, dst_ref, out_ref):
+def pack_kernel(split, state_hbm, dst_hbm, early_ref, state_ref, dst_ref, sems):
+    copies = [
+        pltpu.make_async_copy(dst_hbm, dst_ref, sems.at[0]),
+        pltpu.make_async_copy(state_hbm, state_ref, sems.at[1]),
+    ]
+    for copy in copies:
+        copy.start()
+    copies[0].wait()
     _, levels, rows, cols = state_ref.shape
-    peers, slots = dst_ref.shape
-    groups = peers // levels
-    for h in range(levels):
-        idx = dst_ref[pl.ds(h, groups, stride=levels), :]
-        line, lane = split_lines(idx, rows, cols)
-        line, lane = line.astype(F32).astype(BF), lane.astype(F32).astype(BF)
+    groups, blocks, slots = dst_ref.shape
+    for h in range(blocks):
+        code = encode_cell(dst_ref[:, h, :], rows, cols).astype(BF)
         u, other = h // split, h % split
         for v in range(split):
-            piece = u * split + v
-            out_ref[piece, pl.ds(other * groups, groups), :] = line
-            out_ref[piece, pl.ds((split + other) * groups, groups), :] = lane
-        out_ref[h, pl.ds(2 * split * groups, rows * cols // LANES), :] = tiles(state_ref[0, h]).astype(BF)
+            early_ref[u * split + v, other * groups : (other + 1) * groups, :] = code
+    copies[1].wait()
+    for h in range(blocks):
+        early_ref[h, split * groups :, :] = tiles(state_ref[0, h]).astype(BF)
 
 
 def gather_kernel(split, blocks, count_ref, surf_ref, src_ref, weight_ref, pick_ref, out_ref):
@@ -81,7 +98,7 @@
         found = []
         for i in range(0, blocks, 2):
             pick = jnp.concatenate([one_hot(2 * LANES, col[j : j + 1]) for j in (i, i + 1)], axis=1)
-            values = jnp.dot(surface, pick.astype(BF), preferred_element_type=F32)
+            values = jnp.dot(surface, pick, preferred_element_type=F32)
             for j in range(2):
                 own = values[:, j * slots : (j + 1) * slots].reshape(fc, half, slots)
                 own = jnp.where((spot == line[i + j : i + j + 1])[None], own, 0.0)
@@ -99,9 +116,11 @@
     lax.fori_loop(0, peers // blocks, step, 0, unroll=16)
 
 
-def circle_kernel(scale, early_ref, resp_ref, ahead_ref, back_ref, twiddle_ref, out_ref):
+def circle_kernel(scale, early_ref, resp_ref, ahead_ref, back_ref, twiddle_ref, out_ref, line_ref, lane_ref):
     blocks, rows, cols = out_ref.shape
     start = early_ref.shape[1] - rows * cols // LANES
+    for h in range(blocks):
+        line_ref[h], lane_ref[h] = decode_cell(early_ref[h, :start].astype(F32))
     x = [untile(early_ref[h, start:].astype(F32), rows) for h in range(blocks)]
     incr = zonal_rows(x, resp_ref[0], resp_ref[1], ahead_ref, back_ref, twiddle_ref)
     for h in range(blocks):
@@ -109,7 +128,7 @@
 
 
 def scatter_kernel(
-    split, flag_ref, arrived_ref, early_ref, part_ref, first_ref, second_ref, value_ref, line_ref, lane_ref, acc_ref
+    split, flag_ref, arrived_ref, early_ref, line_ref, lane_ref, part_ref, first_ref, second_ref, value_ref, acc_ref
 ):
     senders, each, slots = arrived_ref.shape
     blocks = early_ref.shape[0]
@@ -118,24 +137,22 @@
     lines = rows * cols // LANES
     for s in range(senders):
         value_ref[s] = arrived_ref[s].astype(F32)
-    for h in range(blocks):
-        line_ref[h] = early_ref[h, :senders].astype(F32).astype(jnp.int32)
-        lane_ref[h] = early_ref[h, senders : 2 * senders].astype(F32).astype(jnp.int32)
     acc_ref[...] = jnp.zeros_like(acc_ref)
     spot = lax.broadcasted_iota(jnp.int32, (lines, slots), 0)
 
-    def step(g, carry):
+    def step(pair, carry):
         for h in range(blocks):
             spread, pick = [], []
-            for v in range(split):
-                at = v * groups + g
-                mask = spot == line_ref[h, pl.ds(at, 1), :]
-                vals = [
-                    jnp.where(mask, value_ref[g * split + v, c * blocks + h : c * blocks + h + 1, :], 0.0)
-                    for c in range(fields)
-                ]
-                spread.append(jnp.concatenate(vals, axis=0).astype(BF))
-                pick.append(one_hot(LANES, lane_ref[h, pl.ds(at, 1), :]).astype(BF))
+            for g in (2 * pair, 2 * pair + 1):
+                for v in range(split):
+                    at = v * groups + g
+                    mask = spot == line_ref[h, pl.ds(at, 1), :]
+                    vals = [
+                        jnp.where(mask, value_ref[g * split + v, c * blocks + h : c * blocks + h + 1, :], 0.0)
+                        for c in range(fields)
+                    ]
+                    spread.append(jnp.concatenate(vals, axis=0).astype(BF))
+                    pick.append(one_hot(LANES, lane_ref[h, pl.ds(at, 1), :]))
             acc_ref[h] += lax.dot_general(
                 jnp.concatenate(spread, axis=1),
                 jnp.concatenate(pick, axis=1),
@@ -144,7 +161,7 @@
             )
         return carry
 
-    lax.fori_loop(0, groups, step, 0, unroll=4)
+    lax.fori_loop(0, groups // 2, step, 0, unroll=4)
     tops, bottoms = [], []
     for c in range(fields + 1):
         for h in range(blocks):
@@ -152,7 +169,7 @@
                 x = untile(acc_ref[h, c * lines : (c + 1) * lines], rows)
                 part_ref[c, h] = x
             else:
-                x = untile(early_ref[h, 2 * senders :].astype(F32), rows)
+                x = untile(early_ref[h, senders:].astype(F32), rows)
             tops.append(x[:1])
             bottoms.append(x[rows - 1 :])
     top, bottom = jnp.concatenate(tops, axis=0), jnp.concatenate(bottoms, axis=0)
@@ -321,18 +338,24 @@
     gv = lax.axis_index("gv")
     own = lax.axis_index("gu") * split + gv
     src_idx = couple_src.reshape(peers, slots)
-    dst_idx = couple_dst.reshape(peers, slots)
     weight = couple_weight.reshape(peers, slots)
     count = couple_count.reshape(peers)
 
     early = pl.pallas_call(
         functools.partial(pack_kernel, split),
-        out_shape=jax.ShapeDtypeStruct((blocks, 2 * senders + cell_rows, LANES), BF),
-        in_specs=[VMEM, VMEM],
+        out_shape=jax.ShapeDtypeStruct((blocks, senders + cell_rows, LANES), BF),
+        in_specs=[HBM] * 2,
         out_specs=VMEM,
-        compiler_params=PARAMS,
+        scratch_shapes=[
+            pltpu.VMEM(state.shape, F32),
+            pltpu.VMEM((groups_x, blocks, slots), jnp.int32),
+            pltpu.SemaphoreType.DMA((2,)),
+        ],
+        compiler_params=LARGE,
+        cost_estimate=cost(1),
         name="early_pack",
-    )(state, dst_idx)
+    )(state, couple_dst.reshape(groups_x, blocks, slots))
+    src_idx, early = lax.optimization_barrier((src_idx, early))
     early = lax.all_to_all(early, ("gu", "gv"), split_axis=0, concat_axis=0, tiled=True)
 
     spot = np.zeros((FC, blocks, blocks, FC, 8), np.float32)
@@ -348,7 +371,6 @@
         cost_estimate=cost(4),
         name="couple_gather",
     )(count, state, src_idx, weight, jnp.asarray(spot.reshape(FC * blocks, -1), BF))
-    outgoing, early = lax.optimization_barrier((outgoing, early))
     crossed = lax.ppermute(outgoing, "comp", [(0, 1), (1, 0)])
     crossed, early = lax.optimization_barrier((crossed, early))
     arrived = lax.all_to_all(crossed, ("gx", "gv"), split_axis=0, concat_axis=0, tiled=True)
@@ -363,11 +385,12 @@
     scale = 2.0 / cols_all
     flag = jnp.stack([lax.axis_index("gx") % 2, lax.axis_index("comp")])
 
-    circle = pl.pallas_call(
+    index = jax.ShapeDtypeStruct((blocks, senders, slots), jnp.int32)
+    circle, line, lane = pl.pallas_call(
         functools.partial(circle_kernel, scale),
-        out_shape=jax.ShapeDtypeStruct((blocks, rows, cols), BF),
+        out_shape=(jax.ShapeDtypeStruct((blocks, rows, cols), BF), index, index),
         in_specs=[VMEM] * 5,
-        out_specs=VMEM,
+        out_specs=(VMEM, VMEM, VMEM),
         compiler_params=PARAMS,
         cost_estimate=cost(2),
         name="circle_filter",
@@ -376,18 +399,16 @@
     part, first, second = pl.pallas_call(
         functools.partial(scatter_kernel, split),
         out_shape=(jax.ShapeDtypeStruct((each, blocks, rows, cols), F32), edge, edge),
-        in_specs=[SMEM, VMEM, VMEM],
+        in_specs=[SMEM] + [VMEM] * 4,
         out_specs=(VMEM, VMEM, VMEM),
         scratch_shapes=[
             pltpu.VMEM((senders, each * blocks, slots), F32),
-            pltpu.VMEM((blocks, senders, slots), jnp.int32),
-            pltpu.VMEM((blocks, senders, slots), jnp.int32),
             pltpu.VMEM((blocks, each * cell_rows, LANES), F32),
         ],
         compiler_params=PARAMS,
         cost_estimate=cost(4),
         name="couple_scatter",
-    )(flag, arrived, early)
+    )(flag, arrived, early, line, lane)
     pairs = [(i, i ^ 1) for i in range(groups_x)]
     cross = [pair for i in range(1, groups_x - 1, 2) for pair in ((i, i + 1), (i + 1, i))]
     first = lax.ppermute(first, "gx", pairs)

time: 72.3 us -> 68.7 us (0.950)
  waiting for transfers between devices: 15.9 us -> 13.1 us
  local copies, waits for them, and re-layouts: 3.34 us -> 1.36 us
  Pallas kernels: 13.9 us -> 14.8 us
    unnamed x26 -> x22, local copies, waits for them, and re-layouts: 2.66 us -> 0.67 us
    all_to_all x1, waiting for transfers between devices: 6.1 us -> 4.12 us  [local(): lax.all_to_all(early, ('gu', 'gv'), split_axis=0, concat_axis=0, tiled=True)]
    pallas_call x1, Pallas kernels: 0.8 us -> 2.3 us  [local(): pl.pallas_call(functools.partial(pack_kernel, split), out_shape=jax.Shape...]
    ppermute x1, waiting for transfers between devices: 1.41 us -> 0.66 us  [local(): crossed = lax.ppermute(outgoing, 'comp', [(0, 1), (1, 0)])]
  transfers between devices with their start and end apart: 5 -> 5, of which waited for: 4 -> 4; matrix products, arithmetic and copies ran while one was open for 1% -> 1% of each run, Pallas kernels for 9% -> 10%
where the time goes in v5:
time: 68.7 us; the launch traced here: 68.3 us
  starting transfers between devices  21.3 us (31%)
  blocking collectives  17.4 us (25%)
  Pallas kernels  14.8 us (22%)
  waiting for transfers between devices  13.1 us (19%)
  local copies, waits for them, and re-layouts  1.36 us (2%)
    all_to_all x1, blocking collectives, local(): lax.all_to_all(incr, ('gu', 'gv'), split_axis=0, concat_axis=0, tiled=True)  17.4 us
    all_to_all x1, starting transfers between devices, local(): lax.all_to_all(early, ('gu', 'gv'), split_axis=0, concat_axis=0, tiled=True)  8.61 us
    all_to_all x1, starting transfers between devices, local(): lax.all_to_all(crossed, ('gx', 'gv'), split_axis=0, concat_axis=0, tiled=...  7.62 us
    all_to_all x1, waiting for transfers between devices, local(): lax.all_to_all(crossed, ('gx', 'gv'), split_axis=0, concat_axis=0, tiled=...  6.25 us
    pallas_call x1, Pallas kernels, local(): pl.pallas_call(functools.partial(gather_kernel, split, blocks), out_shape...  4.56 us
    ppermute x1, starting transfers between devices, local(): second = lax.ppermute(second, 'gx', cross)  4.44 us
    all_to_all x1, waiting for transfers between devices, local(): lax.all_to_all(early, ('gu', 'gv'), split_axis=0, concat_axis=0, tiled=True)  4.12 us
    pallas_call x1, Pallas kernels, local(): pl.pallas_call(functools.partial(scatter_kernel, split), out_shape=(jax.S...  3.42 us
  transfers between devices with their start and end apart: 5, of which 4 were waited for; matrix products, arithmetic and copies ran while one was open for 1% of the time, Pallas kernels for 10%

profile of v5, /device:TPU:2, one launch (start us, length us, event | category | flops | bytes accessed | tf_op | source)
XLA Modules:
  0.0 68.3 jit_solution(2758372105328030092)
XLA Ops:
  0.0 0.0 copy-start
  0.0 0.0 copy-start.10
  0.0 2.3 %early_pack.1 = bf16[8,104,128]{2,1,0:T(8,128)(2,1)} custom-call(f32[1,8,24,384]{3,2,1,0:T(8,128)} %state_ref.1, s32[16,8,128]{2,1,0:T(8,128)} %bitcast.13), custom_call_target="tpu_custom_call" | custom-call | flops 1000000000 | bytes 3000000 | tf_op jit(solution)/shard_map/early_pack/pallas_call | solution.py:344
  2.3 0.0 copy-start.1
  2.3 0.0 copy-start.2
  2.3 0.0 copy-start.3
  2.3 8.6 %all-to-all-start = ((bf16[8,104,128]{2,1,0:T(8,128)(2,1)}), bf16[8,104,128]{2,1,0:T(8,128)(2,1)S(1)}, u32[]{:S(2)}, u32[]{:S(2)}) async-start(bf16[8,104,128]{2,1,0:T(8,128)(2,1)} %early_pack.1), calls=%async_computation | async-start | bytes 425984 | tf_op jit(solution)/shard_map/all_to_all | solution.py:359
  11.0 0.0 copy-start.6
  11.0 0.0 copy-done.10
  11.0 0.0 copy-done.1
  11.0 0.0 copy-done.2
  11.0 0.0 copy-done.3
  11.0 0.6 copy-done.6
  11.6 4.6 %couple_gather.1 = bf16[32,16,128]{2,1,0:T(8,128)(2,1)S(1)} custom-call(s32[128]{0:T(128)S(1)} %bitcast.12, f32[1,8,24,384]{3,2,1,0:T(8,128)S(1)} %copy-done.1, s32[128,128]{1,0:T(8,128)S(1)} %bitcast.10, f32[128,128]{1,0:T(8,128)S(1)} %bitcast.11, bf16[32,256]{1,0:T(8,128)(2,1)S(1)} %copy-done.10), custom_call_target="tpu_custom_call" | custom-call | flops 4000000000 | bytes 12000000 | tf_op jit(solution)/shard_map/couple_gather/pallas_call | solution.py:365
  16.2 0.0 collective-permute-start
  16.2 0.0 copy-done
  16.3 0.1 concatenate.9
  16.4 0.1 copy.14
  16.5 0.2 concatenate.8
  16.8 0.0 copy-start.7
  16.8 0.0 copy-start.8
  16.8 0.2 copy.13
  17.0 0.0 copy-start.9
  17.0 0.7 collective-permute-done
  17.7 4.1 %all-to-all-done.early_ref = bf16[8,104,128]{2,1,0:T(8,128)(2,1)S(1)} async-done(((bf16[8,104,128]{2,1,0:T(8,128)(2,1)}), bf16[8,104,128]{2,1,0:T(8,128)(2,1)S(1)}, u32[]{:S(2)}, u32[]{:S(2)}) %all-to-all-start) | async-done | bytes 213024 | tf_op jit(solution)/shard_map/all_to_all | solution.py:359
  21.8 7.6 %all-to-all-start.1 = ((bf16[32,16,128]{2,1,0:T(8,128)(2,1)}), bf16[32,16,128]{2,1,0:T(8,128)(2,1)S(1)}, u32[]{:S(2)}, u32[]{:S(2)}) async-start(bf16[32,16,128]{2,1,0:T(8,128)(2,1)} %collective-permute-done), calls=%async_computation.1 | async-start | bytes 262144 | tf_op jit(solution)/shard_map/all_to_all | solution.py:376
  29.4 0.1 pad_add_fusion.flag_ref
  29.5 0.0 copy-done.7
  29.5 0.0 copy-done.8
  29.5 0.0 copy-done.9
  29.5 0.8 %circle_filter.1 = (bf16[8,24,384]{2,1,0:T(8,128)(2,1)S(1)}, s32[8,32,128]{2,1,0:T(8,128)S(1)}, s32[8,32,128]{2,1,0:T(8,128)S(1)}) custom-call(bf16[8,104,128]{2,1,0:T(8,128)(2,1)S(1)} %all-to-all-done.early_ref, f32[2,8,256]{2,1,0:T(8,128)S(1)} %slice_bitcast_fusion.resp_ref, bf16[384,512]{1,0:T(8,128)(2,1)S(1)} %copy-done.8, ...), custom_call_target="tpu_custom_call" | custom-call | flops 2000000000 | bytes 6000000 | tf_op jit(solution)/shard_map/circle_filter/pallas_call | solution.py:389
  30.3 6.2 %all-to-all-done.1.arrived_ref = bf16[32,16,128]{2,1,0:T(8,128)(2,1)S(1)} async-done(((bf16[32,16,128]{2,1,0:T(8,128)(2,1)}), bf16[32,16,128]{2,1,0:T(8,128)(2,1)S(1)}, u32[]{:S(2)}, u32[]{:S(2)}) %all-to-all-start.1) | async-done | bytes 131104 | tf_op jit(solution)/shard_map/all_to_all | solution.py:376
  36.6 3.4 %couple_scatter.1 = (f32[2,8,24,384]{3,2,1,0:T(8,128)S(1)}, bf16[24,384]{1,0:T(8,128)(2,1)S(1)}, bf16[24,384]{1,0:T(8,128)(2,1)S(1)}) custom-call(s32[2]{0:T(128)S(1)} %pad_add_fusion.flag_ref, bf16[32,16,128]{2,1,0:T(8,128)(2,1)S(1)} %all-to-all-done.1.arrived_ref, bf16[8,104,128]{2,1,0:T(8,128)(2,1)S(1)} %all-to-all-done.early_ref, ...), custom_call_target="tpu_custom_call" | custom-call | flops 4000000000 | bytes 12000000 | tf_op jit(solution)/shard_map/couple_scatter/pallas_call | solution.py:399
  40.0 0.7 collective-permute-start.1
  40.7 4.4 %collective-permute-start.2 = (bf16[24,384]{1,0:T(8,128)(2,1)S(1)}, bf16[24,384]{1,0:T(8,128)(2,1)S(1)}, u32[]{:S(2)}, u32[]{:S(2)}) collective-permute-start(bf16[24,384]{1,0:T(8,128)(2,1)S(1)} %get-tuple-element.22), channel_id=1, source_target_pairs={{8,16},{16,8},{24,32},{32,24},{40,48},{48,40},{56,64},{64,56},{72,... | collective-permute-start | bytes 55304 | tf_op jit(solution)/shard_map/ppermute | solution.py:415
  45.1 1.2 %part_filter.1.part_ref = bf16[8,2,24,384]{3,2,1,0:T(8,128)(2,1)S(1)} custom-call(f32[2,8,24,384]{3,2,1,0:T(8,128)S(1)} %get-tuple-element.23.part_ref, f32[3,2,8,256]{3,2,1,0:T(8,128)S(1)} %pad.4.resp_ref, bf16[384,512]{1,0:T(8,128)(2,1)S(1)} %copy-done.8, bf16[256,768]{1,0:T(8,128)(2,1)S(1)} %copy-done.7, f32[2,8,384]{2,1,0:T(8,128)S(1)} %copy-done.9), custom_call_target="tpu_custom_call" | custom-call | flops 3000000000 | bytes 9000000 | tf_op jit(solution)/shard_map/part_filter/pallas_call | solution.py:416
  46.4 0.0 collective-permute-done.1.first_ref
  46.4 2.1 %collective-permute-done.2.second_ref = bf16[24,384]{1,0:T(8,128)(2,1)S(1)} collective-permute-done((bf16[24,384]{1,0:T(8,128)(2,1)S(1)}, bf16[24,384]{1,0:T(8,128)(2,1)S(1)}, u32[]{:S(2)}, u32[]{:S(2)}) %collective-permute-start.2) | collective-permute-done | bytes 18464 | tf_op jit(solution)/shard_map/ppermute | solution.py:415
  48.4 1.0 %edge_filter.1 = bf16[8,80,384]{2,1,0:T(8,128)(2,1)S(1)} custom-call(s32[2]{0:T(128)S(1)} %pad_add_fusion.flag_ref, bf16[24,384]{1,0:T(8,128)(2,1)S(1)} %collective-permute-done.1.first_ref, bf16[24,384]{1,0:T(8,128)(2,1)S(1)} %collective-permute-done.2.second_ref, bf16[8,2,24,384]{3,2,1,0:T(8,128)(2,1)S(1)} %part_filter.1.part_ref, ...), custom_call_target="tpu_custom_call" | custom-call | flops 1000000000 | bytes 3000000 | tf_op jit(solution)/shard_map/edge_filter/pallas_call | solution.py:425
  49.5 0.0 copy-start.4
  49.5 0.0 copy-start.5
  49.5 17.4 %all_to_all.15.back_ref = bf16[8,80,384]{2,1,0:T(8,128)(2,1)S(1)} all-to-all(bf16[8,80,384]{2,1,0:T(8,128)(2,1)S(1)} %edge_filter.1), channel_id=1, replica_groups=mesh['comp'=2,'gx'=16,'gu'=4,'gv'=2] {'gu','gv'}, dimensions={0} | all-to-all | bytes 983040 | tf_op jit(solution)/shard_map/all_to_all | solution.py:434
  66.8 0.0 copy-done.4
  66.8 0.0 copy-done.5
  66.8 1.4 %final_step.1 = f32[1,8,24,384]{3,2,1,0:T(8,128)} custom-call(s32[2]{0:T(128)S(1)} %pad_add_fusion.flag_ref, f32[1,8,24,384]{3,2,1,0:T(8,128)S(1)} %copy-done.1, bf16[8,80,384]{2,1,0:T(8,128)(2,1)S(1)} %all_to_all.15.back_ref, f32[1,24,384]{2,1,0:T(8,128)S(1)} %copy-done.4, s32[24,384]{1,0:T(8,128)S(1)} %copy-done.5), custom_call_target="tpu_custom_call" | custom-call | flops 1000000000 | bytes 3000000 | tf_op jit(solution)/shard_map/final_step/pallas_call | solution.py:435
  (5 shorter events, 0.1 us)
Async XLA Ops:
  0.0 16.2 %copy-start = (f32[1,8,3072]{2,1,0:T(8,128)S(1)}, f32[1,8,3072]{2,1,0:T(8,128)}, u32[]{:S(2)}) copy-start(f32[1,8,3072]{2,1,0:T(8,128)} %param.13) | copy-start | bytes 294916
  0.0 11.0 %copy-start.10 = (bf16[32,256]{1,0:T(8,128)(2,1)S(1)}, bf16[32,256]{1,0:T(8,128)(2,1)}, u32[]{:S(2)}) copy-start(bf16[32,256]{1,0:T(8,128)(2,1)} %constant.45.clone.pick_ref) | copy-start | bytes 49156
  2.3 8.7 %copy-start.1 = (f32[1,8,24,384]{3,2,1,0:T(8,128)S(1)}, f32[1,8,24,384]{3,2,1,0:T(8,128)}, u32[]{:S(2)}) copy-start(f32[1,8,24,384]{3,2,1,0:T(8,128)} %state_ref.1) | copy-start | bytes 884740
  2.3 8.7 %copy-start.2 = (s32[1,1,1,128,128]{4,3,2,1,0:T(8,128)S(1)}, s32[1,1,1,128,128]{4,3,2,1,0:T(8,128)}, u32[]{:S(2)}) copy-start(s32[1,1,1,128,128]{4,3,2,1,0:T(8,128)} %param.16) | copy-start | bytes 196612
  2.3 8.7 %copy-start.3 = (f32[1,1,1,128,128]{4,3,2,1,0:T(8,128)S(1)}, f32[1,1,1,128,128]{4,3,2,1,0:T(8,128)}, u32[]{:S(2)}) copy-start(f32[1,1,1,128,128]{4,3,2,1,0:T(8,128)} %param.18) | copy-start | bytes 196612
  2.3 19.4 %all-to-all-start = ((bf16[8,104,128]{2,1,0:T(8,128)(2,1)}), bf16[8,104,128]{2,1,0:T(8,128)(2,1)S(1)}, u32[]{:S(2)}, u32[]{:S(2)}) async-start(bf16[8,104,128]{2,1,0:T(8,128)(2,1)} %early_pack.1), calls=%async_computation | async-start | bytes 425984 | tf_op jit(solution)/shard_map/all_to_all | solution.py:359
  11.0 0.7 copy-start.6
  16.2 1.5 %collective-permute-start = (bf16[32,16,128]{2,1,0:T(8,128)(2,1)S(1)}, bf16[32,16,128]{2,1,0:T(8,128)(2,1)}, u32[]{:S(2)}, u32[]{:S(2)}) collective-permute-start(bf16[32,16,128]{2,1,0:T(8,128)(2,1)S(1)} %couple_gather.1), channel_id=1, source_target_pairs={{0,128},{128,0},{1,129},{129,1},{2,130},{130,2},{3,131},{131,3},{4... | collective-permute-start | bytes 393224 | tf_op jit(solution)/shard_map/ppermute | solution.py:374
  16.8 12.7 %copy-start.7 = (bf16[256,768]{1,0:T(8,128)(2,1)S(1)}, bf16[256,768]{1,0:T(8,128)(2,1)}, u32[]{:S(2)}) copy-start(bf16[256,768]{1,0:T(8,128)(2,1)} %constant.47.clone.back_ref) | copy-start | bytes 1179652
  16.8 12.7 %copy-start.8 = (bf16[384,512]{1,0:T(8,128)(2,1)S(1)}, bf16[384,512]{1,0:T(8,128)(2,1)}, u32[]{:S(2)}) copy-start(bf16[384,512]{1,0:T(8,128)(2,1)} %constant.46.clone.ahead_ref) | copy-start | bytes 1179652
  17.0 12.5 %copy-start.9 = (f32[2,8,384]{2,1,0:T(8,128)S(1)}, f32[2,8,384]{2,1,0:T(8,128)}, u32[]{:S(2)}) copy-start(f32[2,8,384]{2,1,0:T(8,128)} %constant.48.clone.twiddle_ref) | copy-start | bytes 73732
  21.8 14.8 %all-to-all-start.1 = ((bf16[32,16,128]{2,1,0:T(8,128)(2,1)}), bf16[32,16,128]{2,1,0:T(8,128)(2,1)S(1)}, u32[]{:S(2)}, u32[]{:S(2)}) async-start(bf16[32,16,128]{2,1,0:T(8,128)(2,1)} %collective-permute-done), calls=%async_computation.1 | async-start | bytes 262144 | tf_op jit(solution)/shard_map/all_to_all | solution.py:376
  40.0 6.4 %collective-permute-start.1 = (bf16[24,384]{1,0:T(8,128)(2,1)S(1)}, bf16[24,384]{1,0:T(8,128)(2,1)S(1)}, u32[]{:S(2)}, u32[]{:S(2)}) collective-permute-start(bf16[24,384]{1,0:T(8,128)(2,1)S(1)} %get-tuple-element.21), channel_id=1, source_target_pairs={{0,8},{8,0},{16,24},{24,16},{32,40},{40,32},{48,56},{56,48},{64,72... | collective-permute-start | bytes 55304 | tf_op jit(solution)/shard_map/ppermute | solution.py:414
  40.7 7.8 %collective-permute-start.2 = (bf16[24,384]{1,0:T(8,128)(2,1)S(1)}, bf16[24,384]{1,0:T(8,128)(2,1)S(1)}, u32[]{:S(2)}, u32[]{:S(2)}) collective-permute-start(bf16[24,384]{1,0:T(8,128)(2,1)S(1)} %get-tuple-element.22), channel_id=1, source_target_pairs={{8,16},{16,8},{24,32},{32,24},{40,48},{48,40},{56,64},{64,56},{72,... | collective-permute-start | bytes 55304 | tf_op jit(solution)/shard_map/ppermute | solution.py:415
  49.5 17.4 %copy-start.4 = (f32[1,24,384]{2,1,0:T(8,128)S(1)}, f32[1,24,384]{2,1,0:T(8,128)}, u32[]{:S(2)}) copy-start(f32[1,24,384]{2,1,0:T(8,128)} %rate_ref.1) | copy-start | bytes 110596
  49.5 17.4 %copy-start.5 = (s32[24,384]{1,0:T(8,128)S(1)}, s32[24,384]{1,0:T(8,128)}, u32[]{:S(2)}) copy-start(s32[24,384]{1,0:T(8,128)} %land_ref.1) | copy-start | bytes 110596

commit v6 on v5

--- a/solution.py
+++ b/solution.py
@@ -58,24 +58,26 @@
 def pack_kernel(split, state_hbm, dst_hbm, early_ref, state_ref, dst_ref, sems):
     copies = [
         pltpu.make_async_copy(dst_hbm, dst_ref, sems.at[0]),
-        pltpu.make_async_copy(state_hbm, state_ref, sems.at[1]),
+        pltpu.make_async_copy(state_hbm.at[0, FC:], state_ref, sems.at[1]),
     ]
     for copy in copies:
         copy.start()
     copies[0].wait()
-    _, levels, rows, cols = state_ref.shape
+    levels, rows, cols = state_ref.shape
     groups, blocks, slots = dst_ref.shape
+    senders, own_rows = split * groups, rows * levels // blocks
     for h in range(blocks):
         code = encode_cell(dst_ref[:, h, :], rows, cols).astype(BF)
         u, other = h // split, h % split
         for v in range(split):
             early_ref[u * split + v, other * groups : (other + 1) * groups, :] = code
     copies[1].wait()
-    for h in range(blocks):
-        early_ref[h, split * groups :, :] = tiles(state_ref[0, h]).astype(BF)
-
-
-def gather_kernel(split, blocks, count_ref, surf_ref, src_ref, weight_ref, pick_ref, out_ref):
+    for z in range(blocks):
+        u, v = z // split, z % split
+        early_ref[z, senders:, :] = tiles(state_ref[u, v * own_rows : (v + 1) * own_rows, :]).astype(BF)
+
+
+def gather_kernel(split, blocks, surf_ref, src_ref, weight_ref, pick_ref, out_ref):
     _, _, rows, cols = surf_ref.shape
     peers, slots = src_ref.shape
     fc = split * out_ref.shape[1] // blocks
@@ -85,8 +87,6 @@
     shift = lines - half
     surface = [tiles(surf_ref[0, c]) for c in range(fc)]
     surface = jnp.concatenate([jnp.concatenate([x[:half], x[shift:]], axis=1) for x in surface], axis=0).astype(BF)
-    lane = lax.broadcasted_iota(jnp.int32, (blocks, slots), 1)
-    sub = lax.broadcasted_iota(jnp.int32, (blocks, slots), 0)
     spot = lax.broadcasted_iota(jnp.int32, (half, slots), 0)
 
     def step(g, carry):
@@ -104,10 +104,7 @@
                 own = jnp.where((spot == line[i + j : i + j + 1])[None], own, 0.0)
                 found.append(jnp.sum(own.reshape(fc, half // 8, 8, slots), axis=1).reshape(fc * 8, slots))
         value = jnp.dot(pick_ref[...], jnp.concatenate(found, axis=0).astype(BF), preferred_element_type=F32)
-        limit = jnp.zeros((blocks, slots), jnp.int32)
-        for i in range(blocks):
-            limit = jnp.where(sub == i, count_ref[base + i], limit)
-        weight = jnp.where(lane < limit, weight_ref[pl.ds(base, blocks), :], 0.0)
+        weight = weight_ref[pl.ds(base, blocks), :]
         value = value * jnp.concatenate([weight] * fc, axis=0)
         for v in range(split):
             out_ref[g * split + v] = value[v * each : (v + 1) * each].astype(BF)
@@ -116,23 +113,29 @@
     lax.fori_loop(0, peers // blocks, step, 0, unroll=16)
 
 
-def circle_kernel(scale, early_ref, resp_ref, ahead_ref, back_ref, twiddle_ref, out_ref, line_ref, lane_ref):
-    blocks, rows, cols = out_ref.shape
-    start = early_ref.shape[1] - rows * cols // LANES
-    for h in range(blocks):
-        line_ref[h], lane_ref[h] = decode_cell(early_ref[h, :start].astype(F32))
-    x = [untile(early_ref[h, start:].astype(F32), rows) for h in range(blocks)]
+def circle_kernel(scale, early_ref, resp_ref, ahead_ref, back_ref, twiddle_ref, x_ref, incr_ref, line_ref, lane_ref):
+    blocks, frame, cols = x_ref.shape
+    senders = line_ref.shape[1]
+    rows = (early_ref.shape[1] - senders) * LANES // cols
+    blank = jnp.zeros((frame - rows, cols), F32)
+    x = []
+    for h in range(blocks):
+        code = early_ref[h].astype(F32)
+        line_ref[h], lane_ref[h] = decode_cell(code[:senders])
+        x.append(jnp.concatenate([untile(code[senders:], rows), blank], axis=0))
+        x_ref[h] = x[h]
     incr = zonal_rows(x, resp_ref[0], resp_ref[1], ahead_ref, back_ref, twiddle_ref)
     for h in range(blocks):
-        out_ref[h] = (incr[h] * scale).astype(BF)
+        incr_ref[h] = incr[h] * scale
 
 
 def scatter_kernel(
-    split, flag_ref, arrived_ref, early_ref, line_ref, lane_ref, part_ref, first_ref, second_ref, value_ref, acc_ref
+    split, flag_ref, arrived_ref, circle_ref, line_ref, lane_ref, state_ref, mate_ref, part_ref, x_ref, first_ref, second_ref, value_ref, acc_ref
 ):
     senders, each, slots = arrived_ref.shape
-    blocks = early_ref.shape[0]
+    blocks = circle_ref.shape[0]
     fields, _, rows, cols = part_ref.shape
+    last = rows * (state_ref.shape[1] - split * fields) // blocks - 1
     groups = senders // split
     lines = rows * cols // LANES
     for s in range(senders):
@@ -162,29 +165,36 @@
         return carry
 
     lax.fori_loop(0, groups // 2, step, 0, unroll=4)
+    own = flag_ref[2]
+    first_level = lax.rem(own, split) * fields
+    for c in range(fields):
+        for h in range(blocks):
+            x = untile(acc_ref[h, c * lines : (c + 1) * lines], rows)
+            part_ref[c, h] = x
+            x_ref[c, h] = x
+        x_ref[c, own] += state_ref[0, first_level + c]
+        x_ref[c, flag_ref[3]] += mate_ref[c].astype(F32)
     tops, bottoms = [], []
-    for c in range(fields + 1):
+    for c in range(fields):
         for h in range(blocks):
-            if c < fields:
-                x = untile(acc_ref[h, c * lines : (c + 1) * lines], rows)
-                part_ref[c, h] = x
-            else:
-                x = untile(early_ref[h, senders:].astype(F32), rows)
-            tops.append(x[:1])
-            bottoms.append(x[rows - 1 :])
+            tops.append(x_ref[c, h, :1, :])
+            bottoms.append(x_ref[c, h, rows - 1 :, :])
+    for h in range(blocks):
+        tops.append(circle_ref[h, :1, :])
+        bottoms.append(circle_ref[h, last : last + 1, :])
     top, bottom = jnp.concatenate(tops, axis=0), jnp.concatenate(bottoms, axis=0)
     odd = flag_ref[0] == 1
     first_ref[...] = jnp.where(odd, top, bottom).astype(BF)
     second_ref[...] = jnp.where(odd, bottom, top).astype(BF)
 
 
-def part_kernel(scale, part_ref, resp_ref, ahead_ref, back_ref, twiddle_ref, out_ref):
+def part_kernel(scale, part_ref, x_ref, resp_ref, ahead_ref, back_ref, twiddle_ref, out_ref):
     blocks, fields, rows, cols = out_ref.shape
     for c in range(fields):
-        x = [part_ref[c, h] for h in range(blocks)]
+        x = [x_ref[c, h] for h in range(blocks)]
         incr = zonal_rows(x, resp_ref[c, 0], resp_ref[c, 1], ahead_ref, back_ref, twiddle_ref)
         for h in range(blocks):
-            out_ref[h, c] = (incr[h] * scale + x[h]).astype(BF)
+            out_ref[h, c] = (incr[h] * scale + part_ref[c, h]).astype(BF)
 
 
 def edge_kernel(
@@ -209,30 +219,37 @@
         for k in range(2)
     ]
     incr = zonal_rows(x, resp[0], resp[1], ahead_ref, back_ref, twiddle_ref)
+    more = out_ref.shape[1] - fields * rows
     for h in range(blocks):
         for c in range(fields):
             out_ref[h, c * rows : (c + 1) * rows] = part_ref[h, c]
-        out_ref[h, fields * rows : sets * rows] = circle_ref[h]
-        out_ref[h, sets * rows :] = (incr[h] * scale + x[h]).astype(BF)
-
-
-def final_kernel(split, flag_ref, state_ref, back_ref, rate_ref, land_ref, out_ref):
+        tail = [circle_ref[h, : more - 2 * sets], (incr[h] * scale + x[h])[: 2 * sets]]
+        out_ref[h, fields * rows :] = jnp.concatenate(tail, axis=0).astype(BF)
+
+
+def final_kernel(split, fields, flag_ref, state_ref, back_ref, rate_ref, land_ref, out_ref):
     _, levels, rows, cols = state_ref.shape
-    sets = (back_ref.shape[1] - 8) // rows
-    fields = sets - 1
+    blocks = back_ref.shape[0]
+    coupled = split * fields
+    start = fields * rows
+    more = rows * (levels - coupled) // blocks
     keep = jnp.where(flag_ref[1] == 1, land_ref[...].astype(F32), 1.0)
     rate = rate_ref[0] * keep
-    edges = [back_ref[z, sets * rows :].astype(F32) for z in range(levels)]
+    tail = [back_ref[z, start:].astype(F32) for z in range(blocks)]
+    edge = lambda z, k: tail[z][more + k : more + k + 1]
     for c in range(levels):
-        own = state_ref[0, c] + back_ref[c, fields * rows : sets * rows].astype(F32)
-        low, high = edges[c][2 * fields : 2 * fields + 1], edges[c][2 * fields + 1 : 2 * fields + 2]
-        if c < split * fields:
+        own = state_ref[0, c]
+        if c < coupled:
             at = c % fields
-            for u in range(levels // split):
-                z = u * split + c // fields
+            zs = [u * split + c // fields for u in range(blocks // split)]
+            for z in zs:
                 own = own + back_ref[z, at * rows : (at + 1) * rows].astype(F32)
-                low = low + edges[z][2 * at : 2 * at + 1]
-                high = high + edges[z][2 * at + 1 : 2 * at + 2]
+            low = sum(edge(z, 2 * at) for z in zs)
+            high = sum(edge(z, 2 * at + 1) for z in zs)
+        else:
+            zs = [(c - coupled) * split + v for v in range(split)]
+            own = own + jnp.concatenate([tail[z][:more] for z in zs], axis=0)
+            low, high = edge(zs[-1], 2 * fields), edge(zs[0], 2 * fields + 1)
         above = jnp.concatenate([low, own[: rows - 1]], axis=0)
         below = jnp.concatenate([own[1:], high], axis=0)
         out_ref[0, c] = own * keep + rate * (above + below - 2.0 * own)
@@ -338,16 +355,18 @@
     gv = lax.axis_index("gv")
     own = lax.axis_index("gu") * split + gv
     src_idx = couple_src.reshape(peers, slots)
-    weight = couple_weight.reshape(peers, slots)
-    count = couple_count.reshape(peers)
+    live = jnp.arange(slots, dtype=jnp.int32)[None, :] < couple_count.reshape(peers, 1)
+    weight = jnp.where(live, couple_weight.reshape(peers, slots), jnp.float32(0.0))
+    more = rows * (levels - FC) // blocks
+    frame = -(-more // 8) * 8
 
     early = pl.pallas_call(
         functools.partial(pack_kernel, split),
-        out_shape=jax.ShapeDtypeStruct((blocks, senders + cell_rows, LANES), BF),
+        out_shape=jax.ShapeDtypeStruct((blocks, senders + more * cols // LANES, LANES), BF),
         in_specs=[HBM] * 2,
         out_specs=VMEM,
         scratch_shapes=[
-            pltpu.VMEM(state.shape, F32),
+            pltpu.VMEM((levels - FC, rows, cols), F32),
             pltpu.VMEM((groups_x, blocks, slots), jnp.int32),
             pltpu.SemaphoreType.DMA((2,)),
         ],
@@ -365,42 +384,47 @@
     outgoing = pl.pallas_call(
         functools.partial(gather_kernel, split, blocks),
         out_shape=jax.ShapeDtypeStruct((senders, each * blocks, slots), BF),
-        in_specs=[SMEM, VMEM, VMEM, VMEM, VMEM],
+        in_specs=[VMEM] * 4,
         out_specs=VMEM,
         compiler_params=PARAMS,
         cost_estimate=cost(4),
         name="couple_gather",
-    )(count, state, src_idx, weight, jnp.asarray(spot.reshape(FC * blocks, -1), BF))
+    )(state, src_idx, weight, jnp.asarray(spot.reshape(FC * blocks, -1), BF))
     crossed = lax.ppermute(outgoing, "comp", [(0, 1), (1, 0)])
-    crossed, early = lax.optimization_barrier((crossed, early))
+    mate = lax.dynamic_slice_in_dim(state[0], (1 - gv) * each, each, 0).astype(BF)
+    crossed, early, mate, response = lax.optimization_barrier((crossed, early, mate, response))
+    mate = lax.ppermute(mate, "gv", [(0, 1), (1, 0)])
     arrived = lax.all_to_all(crossed, ("gx", "gv"), split_axis=0, concat_axis=0, tiled=True)
 
     ahead, back, twiddle = zonal_tables(blocks, cols, waves)
     half = cols_all // 2 // blocks
     resp = jnp.concatenate(
-        [lax.dynamic_slice_in_dim(response[0], gv * each, each, 0), lax.dynamic_slice_in_dim(response[0], own, 1, 0)], axis=0
+        [lax.dynamic_slice_in_dim(response[0], gv * each, each, 0), lax.dynamic_slice_in_dim(response[0], FC + lax.axis_index("gu"), 1, 0)], axis=0
     )
     resp = resp.reshape(each + 1, 2, half, blocks).transpose(0, 1, 3, 2)
     resp = jnp.pad(resp, ((0, 0), (0, 0), (0, 0), (0, waves - half)))
     scale = 2.0 / cols_all
-    flag = jnp.stack([lax.axis_index("gx") % 2, lax.axis_index("comp")])
+    mate_block = own + 1 - 2 * gv
+    flag = jnp.stack([lax.axis_index("gx") % 2, lax.axis_index("comp"), own, mate_block])
 
     index = jax.ShapeDtypeStruct((blocks, senders, slots), jnp.int32)
-    circle, line, lane = pl.pallas_call(
+    framed = jax.ShapeDtypeStruct((blocks, frame, cols), F32)
+    circle, circle_incr, line, lane = pl.pallas_call(
         functools.partial(circle_kernel, scale),
-        out_shape=(jax.ShapeDtypeStruct((blocks, rows, cols), BF), index, index),
+        out_shape=(framed, framed, index, index),
         in_specs=[VMEM] * 5,
-        out_specs=(VMEM, VMEM, VMEM),
+        out_specs=(VMEM,) * 4,
         compiler_params=PARAMS,
         cost_estimate=cost(2),
         name="circle_filter",
     )(early, resp[each], ahead, back, twiddle)
     edge = jax.ShapeDtypeStruct(((each + 1) * blocks, cols), BF)
-    part, first, second = pl.pallas_call(
+    part_shape = jax.ShapeDtypeStruct((each, blocks, rows, cols), F32)
+    part, x, first, second = pl.pallas_call(
         functools.partial(scatter_kernel, split),
-        out_shape=(jax.ShapeDtypeStruct((each, blocks, rows, cols), F32), edge, edge),
-        in_specs=[SMEM] + [VMEM] * 4,
-        out_specs=(VMEM, VMEM, VMEM),
+        out_shape=(part_shape, part_shape, edge, edge),
+        in_specs=[SMEM] + [VMEM] * 6,
+        out_specs=(VMEM,) * 4,
         scratch_shapes=[
             pltpu.VMEM((senders, each * blocks, slots), F32),
             pltpu.VMEM((blocks, each * cell_rows, LANES), F32),
@@ -408,7 +432,7 @@
         compiler_params=PARAMS,
         cost_estimate=cost(4),
         name="couple_scatter",
-    )(flag, arrived, early, line, lane)
+    )(flag, arrived, circle, line, lane, state, mate)
     pairs = [(i, i ^ 1) for i in range(groups_x)]
     cross = [pair for i in range(1, groups_x - 1, 2) for pair in ((i, i + 1), (i + 1, i))]
     first = lax.ppermute(first, "gx", pairs)
@@ -416,24 +440,24 @@
     part = pl.pallas_call(
         functools.partial(part_kernel, scale),
         out_shape=jax.ShapeDtypeStruct((blocks, each, rows, cols), BF),
-        in_specs=[VMEM] * 5,
+        in_specs=[VMEM] * 6,
         out_specs=VMEM,
         compiler_params=PARAMS,
         cost_estimate=cost(3),
         name="part_filter",
-    )(part, resp, ahead, back, twiddle)
+    )(part, x, resp, ahead, back, twiddle)
     incr = pl.pallas_call(
         functools.partial(edge_kernel, scale),
-        out_shape=jax.ShapeDtypeStruct((blocks, (each + 1) * rows + 8, cols), BF),
+        out_shape=jax.ShapeDtypeStruct((blocks, each * rows + more + 2 * (each + 1), cols), BF),
         in_specs=[SMEM] + [VMEM] * 8,
         out_specs=VMEM,
         compiler_params=PARAMS,
         cost_estimate=cost(1),
         name="edge_filter",
-    )(flag, first, second, part, circle, resp, ahead, back, twiddle)
+    )(flag, first, second, part, circle_incr, resp, ahead, back, twiddle)
     incr = lax.all_to_all(incr, ("gu", "gv"), split_axis=0, concat_axis=0, tiled=True)
     return pl.pallas_call(
-        functools.partial(final_kernel, split),
+        functools.partial(final_kernel, split, each),
         out_shape=jax.ShapeDtypeStruct((1, levels, rows, cols), F32),
         in_specs=[SMEM] + [VMEM] * 4,
         out_specs=VMEM,

time: 68.7 us -> 68 us (0.990)
  waiting for transfers between devices: 13.1 us -> 9.09 us
  starting transfers between devices: 21.3 us -> 22.9 us
  local copies, waits for them, and re-layouts: 1.36 us -> 2.94 us
    all_to_all x1, waiting for transfers between devices: 6.25 us -> 2.97 us  [local(): lax.all_to_all(crossed, ('gx', 'gv'), split_axis=0, concat_axis=0, tiled=...]
    all_to_all x1, waiting for transfers between devices: 4.12 us -> 2.41 us  [local(): lax.all_to_all(early, ('gu', 'gv'), split_axis=0, concat_axis=0, tiled=True)]
    unnamed x22, local copies, waits for them, and re-layouts: 0.67 us -> 2.25 us
    ppermute x0 -> x1, starting transfers between devices: none -> 1.55 us  [local(): mate = lax.ppermute(mate, 'gv', [(0, 1), (1, 0)])]
    ppermute x1, waiting for transfers between devices: 0.66 us -> 1.37 us  [local(): crossed = lax.ppermute(outgoing, 'comp', [(0, 1), (1, 0)])]
  transfers between devices with their start and end apart: 5 -> 6, of which waited for: 4 -> 5; matrix products, arithmetic and copies ran while one was open for 1% -> 1% of each run, Pallas kernels for 10% -> 9%
where the time goes in v6:
time: 68 us; the launch traced here: 67.5 us
  starting transfers between devices  22.9 us (34%)
  blocking collectives  18 us (26%)
  Pallas kernels  14.2 us (21%)
  waiting for transfers between devices  9.09 us (13%)
  local copies, waits for them, and re-layouts  2.94 us (4%)
    all_to_all x1, blocking collectives, local(): lax.all_to_all(incr, ('gu', 'gv'), split_axis=0, concat_axis=0, tiled=True)  18 us
    all_to_all x1, starting transfers between devices, local(): lax.all_to_all(early, ('gu', 'gv'), split_axis=0, concat_axis=0, tiled=True)  8.61 us
    all_to_all x1, starting transfers between devices, local(): lax.all_to_all(crossed, ('gx', 'gv'), split_axis=0, concat_axis=0, tiled=...  7.62 us
    ppermute x1, starting transfers between devices, local(): second = lax.ppermute(second, 'gx', cross)  4.44 us
    pallas_call x1, Pallas kernels, local(): pl.pallas_call(functools.partial(gather_kernel, split, blocks), out_shape...  4.01 us
    pallas_call x1, Pallas kernels, local(): pl.pallas_call(functools.partial(scatter_kernel, split), out_shape=(part_...  3.48 us
    all_to_all x1, waiting for transfers between devices, local(): lax.all_to_all(crossed, ('gx', 'gv'), split_axis=0, concat_axis=0, tiled=...  2.97 us
    all_to_all x1, waiting for transfers between devices, local(): lax.all_to_all(early, ('gu', 'gv'), split_axis=0, concat_axis=0, tiled=True)  2.41 us
  transfers between devices with their start and end apart: 6, of which 5 were waited for; matrix products, arithmetic and copies ran while one was open for 1% of the time, Pallas kernels for 9%

profile of v6, /device:TPU:2, one launch (start us, length us, event | category | flops | bytes accessed | tf_op | source)
XLA Modules:
  0.0 67.5 jit_solution(10444029832288194472)
XLA Ops:
  0.0 0.0 copy-start
  0.0 0.0 copy-start.9
  0.0 2.3 %early_pack.1 = bf16[8,68,128]{2,1,0:T(8,128)(2,1)} custom-call(f32[1,8,24,384]{3,2,1,0:T(8,128)} %state_ref.3, s32[16,8,128]{2,1,0:T(8,128)} %bitcast.17), custom_call_target="tpu_custom_call" | custom-call | flops 1000000000 | bytes 3000000 | tf_op jit(solution)/shard_map/early_pack/pallas_call | solution.py:363
  2.3 0.0 copy-start.1
  2.3 8.6 %all-to-all-start = ((bf16[8,68,128]{2,1,0:T(8,128)(2,1)}), bf16[8,68,128]{2,1,0:T(8,128)(2,1)S(1)}, u32[]{:S(2)}, u32[]{:S(2)}) async-start(bf16[8,68,128]{2,1,0:T(8,128)(2,1)} %early_pack.1), calls=%async_computation | async-start | bytes 294912 | tf_op jit(solution)/shard_map/all_to_all | solution.py:378
  10.9 0.0 copy-start.10
  10.9 0.0 copy-done.9
  10.9 0.6 copy-done.10
  11.6 0.0 copy-start.2
  11.6 0.0 copy-start.8
  11.6 0.1 bitcast_select_fusion.weight_ref
  11.7 0.0 copy-done.1
  11.7 0.7 %copy-done.2 = s32[1,1,1,128,128]{4,3,2,1,0:T(8,128)S(1)} copy-done((s32[1,1,1,128,128]{4,3,2,1,0:T(8,128)S(1)}, s32[1,1,1,128,128]{4,3,2,1,0:T(8,128)}, u32[]{:S(2)}) %copy-start.2) | copy-done | bytes 65560
  12.4 0.0 copy-done.8
  12.4 4.0 %couple_gather.1 = bf16[32,16,128]{2,1,0:T(8,128)(2,1)S(1)} custom-call(f32[1,8,24,384]{3,2,1,0:T(8,128)S(1)} %copy-done.1, s32[128,128]{1,0:T(8,128)S(1)} %bitcast.15, f32[128,128]{1,0:T(8,128)S(1)} %bitcast_select_fusion.weight_ref, bf16[32,256]{1,0:T(8,128)(2,1)S(1)} %copy-done.8), custom_call_target="tpu_custom_call" | custom-call | flops 4000000000 | bytes 12000000 | tf_op jit(solution)/shard_map/couple_gather/pallas_call | solution.py:384
  16.4 0.0 collective-permute-start
  16.5 0.1 pad_add_fusion.flag_ref
  16.5 1.4 %collective-permute-done = bf16[32,16,128]{2,1,0:T(8,128)(2,1)} collective-permute-done((bf16[32,16,128]{2,1,0:T(8,128)(2,1)S(1)}, bf16[32,16,128]{2,1,0:T(8,128)(2,1)}, u32[]{:S(2)}, u32[]{:S(2)}) %collective-permute-start) | collective-permute-done | bytes 131104 | tf_op jit(solution)/shard_map/ppermute | solution.py:393
  17.9 2.4 %all-to-all-done.early_ref = bf16[8,68,128]{2,1,0:T(8,128)(2,1)S(1)} async-done(((bf16[8,68,128]{2,1,0:T(8,128)(2,1)}), bf16[8,68,128]{2,1,0:T(8,128)(2,1)S(1)}, u32[]{:S(2)}, u32[]{:S(2)}) %all-to-all-start) | async-done | bytes 139296 | tf_op jit(solution)/shard_map/all_to_all | solution.py:378
  20.3 7.6 %all-to-all-start.1 = ((bf16[32,16,128]{2,1,0:T(8,128)(2,1)}), bf16[32,16,128]{2,1,0:T(8,128)(2,1)S(1)}, u32[]{:S(2)}, u32[]{:S(2)}) async-start(bf16[32,16,128]{2,1,0:T(8,128)(2,1)} %collective-permute-done), calls=%async_computation.1 | async-start | bytes 262144 | tf_op jit(solution)/shard_map/all_to_all | solution.py:397
  28.0 0.0 copy-done
  28.0 1.6 %collective-permute-start.1 = (bf16[2,24,384]{2,1,0:T(8,128)(2,1)S(1)}, bf16[2,24,384]{2,1,0:T(8,128)(2,1)S(1)}, u32[]{:S(2)}, u32[]{:S(2)}) collective-permute-start(bf16[2,24,384]{2,1,0:T(8,128)(2,1)S(1)} %fusion), channel_id=1, source_target_pairs={{0,1},{1,0},{2,3},{3,2},{4,5},{5,4},{6,7},{7,6},{8,9},{9,8},{10,11... | collective-permute-start | bytes 110600 | tf_op jit(solution)/shard_map/ppermute | solution.py:396
  29.6 0.1 concatenate.9
  29.7 0.1 copy.14
  29.8 0.0 copy-start.6
  29.8 0.2 concatenate.8
  30.1 0.0 copy-start.5
  30.1 0.2 copy.13
  30.3 0.0 copy-start.7
  30.3 0.5 copy-done.6
  30.8 0.3 copy-done.5
  31.1 0.0 copy-done.7
  31.1 0.7 %circle_filter.1 = (f32[8,16,384]{2,1,0:T(8,128)S(1)}, f32[8,16,384]{2,1,0:T(8,128)S(1)}, s32[8,32,128]{2,1,0:T(8,128)S(1)}, s32[8,32,128]{2,1,0:T(8,128)S(1)}) custom-call(bf16[8,68,128]{2,1,0:T(8,128)(2,1)S(1)} %all-to-all-done.early_ref, f32[2,8,256]{2,1,0:T(8,128)S(1)} %slice_bitcast_fusion.resp_ref, bf16[384,512]{1,0:T(8,128)(2,1)S(1)} %copy-done.6, ...), custom_call_target="tpu_custom_call" | custom-call | flops 2000000000 | bytes 6000000 | tf_op jit(solution)/shard_map/circle_filter/pallas_call | solution.py:412
  31.9 0.3 collective-permute-done.1.mate_ref
  32.2 3.0 %all-to-all-done.1.arrived_ref = bf16[32,16,128]{2,1,0:T(8,128)(2,1)S(1)} async-done(((bf16[32,16,128]{2,1,0:T(8,128)(2,1)}), bf16[32,16,128]{2,1,0:T(8,128)(2,1)S(1)}, u32[]{:S(2)}, u32[]{:S(2)}) %all-to-all-start.1) | async-done | bytes 131104 | tf_op jit(solution)/shard_map/all_to_all | solution.py:397
  35.1 3.5 %couple_scatter.1 = (f32[2,8,24,384]{3,2,1,0:T(8,128)S(1)}, f32[2,8,24,384]{3,2,1,0:T(8,128)S(1)}, bf16[24,384]{1,0:T(8,128)(2,1)S(1)}, bf16[24,384]{1,0:T(8,128)(2,1)S(1)}) custom-call(s32[4]{0:T(128)S(1)} %pad_add_fusion.flag_ref, bf16[32,16,128]{2,1,0:T(8,128)(2,1)S(1)} %all-to-all-done.1.arrived_ref, f32[8,16,384]{2,1,0:T(8,128)S(1)} %get-tuple-element.24.circle_ref, ...), custom_call_target="tpu_custom_call" | custom-call | flops 4000000000 | bytes 12000000 | tf_op jit(solution)/shard_map/couple_scatter/pallas_call | solution.py:423
  38.6 0.7 collective-permute-start.2
  39.3 4.4 %collective-permute-start.3 = (bf16[24,384]{1,0:T(8,128)(2,1)S(1)}, bf16[24,384]{1,0:T(8,128)(2,1)S(1)}, u32[]{:S(2)}, u32[]{:S(2)}) collective-permute-start(bf16[24,384]{1,0:T(8,128)(2,1)S(1)} %get-tuple-element.29), channel_id=1, source_target_pairs={{8,16},{16,8},{24,32},{32,24},{40,48},{48,40},{56,64},{64,56},{72,... | collective-permute-start | bytes 55304 | tf_op jit(solution)/shard_map/ppermute | solution.py:439
  43.7 1.3 %part_filter.1.part_ref = bf16[8,2,24,384]{3,2,1,0:T(8,128)(2,1)S(1)} custom-call(f32[2,8,24,384]{3,2,1,0:T(8,128)S(1)} %get-tuple-element.30.part_ref, f32[2,8,24,384]{3,2,1,0:T(8,128)S(1)} %get-tuple-element.31.x_ref, f32[3,2,8,256]{3,2,1,0:T(8,128)S(1)} %pad.4.resp_ref, bf16[384,512]{1,0:T(8,128)(2,1)S(1)} %copy-done.6, bf16[256,768]{1,0:T(8,128)(2,1)S(1)} %copy-done.5, ...), custom_call_target="tpu_custom_call" | custom-call | flops 3000000000 | bytes 9000000 | tf_op jit(solution)/shard_map/part_filter/pallas_call | solution.py:440
  45.0 0.0 collective-permute-done.2.first_ref
  45.0 2.0 %collective-permute-done.3.second_ref = bf16[24,384]{1,0:T(8,128)(2,1)S(1)} collective-permute-done((bf16[24,384]{1,0:T(8,128)(2,1)S(1)}, bf16[24,384]{1,0:T(8,128)(2,1)S(1)}, u32[]{:S(2)}, u32[]{:S(2)}) %collective-permute-start.3) | collective-permute-done | bytes 18464 | tf_op jit(solution)/shard_map/ppermute | solution.py:439
  47.0 1.0 %edge_filter.1 = bf16[8,66,384]{2,1,0:T(8,128)(2,1)S(1)} custom-call(s32[4]{0:T(128)S(1)} %pad_add_fusion.flag_ref, bf16[24,384]{1,0:T(8,128)(2,1)S(1)} %collective-permute-done.2.first_ref, bf16[24,384]{1,0:T(8,128)(2,1)S(1)} %collective-permute-done.3.second_ref, bf16[8,2,24,384]{3,2,1,0:T(8,128)(2,1)S(1)} %part_filter.1.part_ref, ...), custom_call_target="tpu_custom_call" | custom-call | flops 1000000000 | bytes 3000000 | tf_op jit(solution)/shard_map/edge_filter/pallas_call | solution.py:449
  48.1 0.0 copy-start.3
  48.1 0.0 copy-start.4
  48.1 18.0 %all_to_all.15.back_ref = bf16[8,66,384]{2,1,0:T(8,128)(2,1)S(1)} all-to-all(bf16[8,66,384]{2,1,0:T(8,128)(2,1)S(1)} %edge_filter.1), channel_id=1, replica_groups=mesh['comp'=2,'gx'=16,'gu'=4,'gv'=2] {'gu','gv'}, dimensions={0} | all-to-all | bytes 811008 | tf_op jit(solution)/shard_map/all_to_all | solution.py:458
  66.1 0.0 copy-done.3
  66.1 0.0 copy-done.4
  66.1 1.4 %final_step.1 = f32[1,8,24,384]{3,2,1,0:T(8,128)} custom-call(s32[4]{0:T(128)S(1)} %pad_add_fusion.flag_ref, f32[1,8,24,384]{3,2,1,0:T(8,128)S(1)} %copy-done.1, bf16[8,66,384]{2,1,0:T(8,128)(2,1)S(1)} %all_to_all.15.back_ref, f32[1,24,384]{2,1,0:T(8,128)S(1)} %copy-done.3, s32[24,384]{1,0:T(8,128)S(1)} %copy-done.4), custom_call_target="tpu_custom_call" | custom-call | flops 1000000000 | bytes 3000000 | tf_op jit(solution)/shard_map/final_step/pallas_call | solution.py:459
  (6 shorter events, 0.1 us)
Async XLA Ops:
  0.0 28.0 %copy-start = (f32[1,8,3072]{2,1,0:T(8,128)S(1)}, f32[1,8,3072]{2,1,0:T(8,128)}, u32[]{:S(2)}) copy-start(f32[1,8,3072]{2,1,0:T(8,128)} %param.13) | copy-start | bytes 294916
  0.0 10.9 %copy-start.9 = (f32[1,1,1,128,128]{4,3,2,1,0:T(8,128)S(1)}, f32[1,1,1,128,128]{4,3,2,1,0:T(8,128)}, u32[]{:S(2)}) copy-start(f32[1,1,1,128,128]{4,3,2,1,0:T(8,128)} %param.18) | copy-start | bytes 196612
  2.3 9.4 %copy-start.1 = (f32[1,8,24,384]{3,2,1,0:T(8,128)S(1)}, f32[1,8,24,384]{3,2,1,0:T(8,128)}, u32[]{:S(2)}) copy-start(f32[1,8,24,384]{3,2,1,0:T(8,128)} %state_ref.3) | copy-start | bytes 884740
  2.3 18.0 %all-to-all-start = ((bf16[8,68,128]{2,1,0:T(8,128)(2,1)}), bf16[8,68,128]{2,1,0:T(8,128)(2,1)S(1)}, u32[]{:S(2)}, u32[]{:S(2)}) async-start(bf16[8,68,128]{2,1,0:T(8,128)(2,1)} %early_pack.1), calls=%async_computation | async-start | bytes 294912 | tf_op jit(solution)/shard_map/all_to_all | solution.py:378
  10.9 0.7 copy-start.10
  11.6 0.8 %copy-start.2 = (s32[1,1,1,128,128]{4,3,2,1,0:T(8,128)S(1)}, s32[1,1,1,128,128]{4,3,2,1,0:T(8,128)}, u32[]{:S(2)}) copy-start(s32[1,1,1,128,128]{4,3,2,1,0:T(8,128)} %param.16) | copy-start | bytes 196612
  11.6 0.8 %copy-start.8 = (bf16[32,256]{1,0:T(8,128)(2,1)S(1)}, bf16[32,256]{1,0:T(8,128)(2,1)}, u32[]{:S(2)}) copy-start(bf16[32,256]{1,0:T(8,128)(2,1)} %constant.52.clone.pick_ref) | copy-start | bytes 49156
  16.4 1.5 %collective-permute-start = (bf16[32,16,128]{2,1,0:T(8,128)(2,1)S(1)}, bf16[32,16,128]{2,1,0:T(8,128)(2,1)}, u32[]{:S(2)}, u32[]{:S(2)}) collective-permute-start(bf16[32,16,128]{2,1,0:T(8,128)(2,1)S(1)} %couple_gather.1), channel_id=1, source_target_pairs={{0,128},{128,0},{1,129},{129,1},{2,130},{130,2},{3,131},{131,3},{4... | collective-permute-start | bytes 393224 | tf_op jit(solution)/shard_map/ppermute | solution.py:393
  20.3 14.8 %all-to-all-start.1 = ((bf16[32,16,128]{2,1,0:T(8,128)(2,1)}), bf16[32,16,128]{2,1,0:T(8,128)(2,1)S(1)}, u32[]{:S(2)}, u32[]{:S(2)}) async-start(bf16[32,16,128]{2,1,0:T(8,128)(2,1)} %collective-permute-done), calls=%async_computation.1 | async-start | bytes 262144 | tf_op jit(solution)/shard_map/all_to_all | solution.py:397
  28.0 4.1 %collective-permute-start.1 = (bf16[2,24,384]{2,1,0:T(8,128)(2,1)S(1)}, bf16[2,24,384]{2,1,0:T(8,128)(2,1)S(1)}, u32[]{:S(2)}, u32[]{:S(2)}) collective-permute-start(bf16[2,24,384]{2,1,0:T(8,128)(2,1)S(1)} %fusion), channel_id=1, source_target_pairs={{0,1},{1,0},{2,3},{3,2},{4,5},{5,4},{6,7},{7,6},{8,9},{9,8},{10,11... | collective-permute-start | bytes 110600 | tf_op jit(solution)/shard_map/ppermute | solution.py:396
  29.8 1.0 %copy-start.6 = (bf16[384,512]{1,0:T(8,128)(2,1)S(1)}, bf16[384,512]{1,0:T(8,128)(2,1)}, u32[]{:S(2)}) copy-start(bf16[384,512]{1,0:T(8,128)(2,1)} %constant.53.clone.ahead_ref) | copy-start | bytes 1179652
  30.1 1.0 %copy-start.5 = (bf16[256,768]{1,0:T(8,128)(2,1)S(1)}, bf16[256,768]{1,0:T(8,128)(2,1)}, u32[]{:S(2)}) copy-start(bf16[256,768]{1,0:T(8,128)(2,1)} %constant.54.clone.back_ref) | copy-start | bytes 1179652
  30.3 0.9 %copy-start.7 = (f32[2,8,384]{2,1,0:T(8,128)S(1)}, f32[2,8,384]{2,1,0:T(8,128)}, u32[]{:S(2)}) copy-start(f32[2,8,384]{2,1,0:T(8,128)} %constant.55.clone.twiddle_ref) | copy-start | bytes 73732
  38.6 6.4 %collective-permute-start.2 = (bf16[24,384]{1,0:T(8,128)(2,1)S(1)}, bf16[24,384]{1,0:T(8,128)(2,1)S(1)}, u32[]{:S(2)}, u32[]{:S(2)}) collective-permute-start(bf16[24,384]{1,0:T(8,128)(2,1)S(1)} %get-tuple-element.28), channel_id=1, source_target_pairs={{0,8},{8,0},{16,24},{24,16},{32,40},{40,32},{48,56},{56,48},{64,72... | collective-permute-start | bytes 55304 | tf_op jit(solution)/shard_map/ppermute | solution.py:438
  39.3 7.8 %collective-permute-start.3 = (bf16[24,384]{1,0:T(8,128)(2,1)S(1)}, bf16[24,384]{1,0:T(8,128)(2,1)S(1)}, u32[]{:S(2)}, u32[]{:S(2)}) collective-permute-start(bf16[24,384]{1,0:T(8,128)(2,1)S(1)} %get-tuple-element.29), channel_id=1, source_target_pairs={{8,16},{16,8},{24,32},{32,24},{40,48},{48,40},{56,64},{64,56},{72,... | collective-permute-start | bytes 55304 | tf_op jit(solution)/shard_map/ppermute | solution.py:439
  48.1 18.0 %copy-start.3 = (f32[1,24,384]{2,1,0:T(8,128)S(1)}, f32[1,24,384]{2,1,0:T(8,128)}, u32[]{:S(2)}) copy-start(f32[1,24,384]{2,1,0:T(8,128)} %rate_ref.1) | copy-start | bytes 110596
  48.1 18.0 %copy-start.4 = (s32[24,384]{1,0:T(8,128)S(1)}, s32[24,384]{1,0:T(8,128)}, u32[]{:S(2)}) copy-start(s32[24,384]{1,0:T(8,128)} %land_ref.1) | copy-start | bytes 110596

commit v7 on v6

--- a/solution.py
+++ b/solution.py
@@ -14,7 +14,6 @@
 BF = jnp.bfloat16
 F32 = jnp.float32
 VMEM = pl.BlockSpec(memory_space=pltpu.VMEM)
-SMEM = pl.BlockSpec(memory_space=pltpu.SMEM)
 HBM = pl.BlockSpec(memory_space=pltpu.HBM)
 LARGE = pltpu.CompilerParams(vmem_limit_bytes=60 * 2**20)
 PARAMS = pltpu.CompilerParams(vmem_limit_bytes=32 * 2**20)
@@ -130,7 +129,7 @@
 
 
 def scatter_kernel(
-    split, flag_ref, arrived_ref, circle_ref, line_ref, lane_ref, state_ref, mate_ref, part_ref, x_ref, first_ref, second_ref, value_ref, acc_ref
+    split, arrived_ref, circle_ref, line_ref, lane_ref, state_ref, mate_ref, part_ref, x_ref, first_ref, second_ref, value_ref, acc_ref
 ):
     senders, each, slots = arrived_ref.shape
     blocks = circle_ref.shape[0]
@@ -165,15 +164,16 @@
         return carry
 
     lax.fori_loop(0, groups // 2, step, 0, unroll=4)
-    own = flag_ref[2]
-    first_level = lax.rem(own, split) * fields
+    gv = lax.axis_index("gv")
+    own = lax.axis_index("gu") * split + gv
+    first_level = gv * fields
     for c in range(fields):
         for h in range(blocks):
             x = untile(acc_ref[h, c * lines : (c + 1) * lines], rows)
             part_ref[c, h] = x
             x_ref[c, h] = x
         x_ref[c, own] += state_ref[0, first_level + c]
-        x_ref[c, flag_ref[3]] += mate_ref[c].astype(F32)
+        x_ref[c, own + 1 - 2 * gv] += mate_ref[c].astype(F32)
     tops, bottoms = [], []
     for c in range(fields):
         for h in range(blocks):
@@ -183,7 +183,7 @@
         tops.append(circle_ref[h, :1, :])
         bottoms.append(circle_ref[h, last : last + 1, :])
     top, bottom = jnp.concatenate(tops, axis=0), jnp.concatenate(bottoms, axis=0)
-    odd = flag_ref[0] == 1
+    odd = lax.axis_index("gx") % 2 == 1
     first_ref[...] = jnp.where(odd, top, bottom).astype(BF)
     second_ref[...] = jnp.where(odd, bottom, top).astype(BF)
 
@@ -198,11 +198,11 @@
 
 
 def edge_kernel(
-    scale, flag_ref, first_ref, second_ref, part_ref, circle_ref, resp_ref, ahead_ref, back_ref, twiddle_ref, out_ref
+    scale, second_ref, first_ref, part_ref, circle_ref, resp_ref, ahead_ref, back_ref, twiddle_ref, out_ref
 ):
     blocks, fields, rows, cols = part_ref.shape
     sets = fields + 1
-    odd = flag_ref[0] == 1
+    odd = lax.axis_index("gx") % 2 == 1
     first, second = first_ref[...].astype(F32), second_ref[...].astype(F32)
     low, high = jnp.where(odd, first, second), jnp.where(odd, second, first)
     x = []
@@ -227,16 +227,17 @@
         out_ref[h, fields * rows :] = jnp.concatenate(tail, axis=0).astype(BF)
 
 
-def final_kernel(split, fields, flag_ref, state_ref, back_ref, rate_ref, land_ref, out_ref):
+def final_kernel(split, fields, state_ref, back_ref, rate_ref, land_ref, out_hbm, out_ref, sems):
     _, levels, rows, cols = state_ref.shape
     blocks = back_ref.shape[0]
     coupled = split * fields
     start = fields * rows
     more = rows * (levels - coupled) // blocks
-    keep = jnp.where(flag_ref[1] == 1, land_ref[...].astype(F32), 1.0)
+    keep = jnp.where(lax.axis_index("comp") == 1, land_ref[...].astype(F32), 1.0)
     rate = rate_ref[0] * keep
     tail = [back_ref[z, start:].astype(F32) for z in range(blocks)]
     edge = lambda z, k: tail[z][more + k : more + k + 1]
+    copies = []
     for c in range(levels):
         own = state_ref[0, c]
         if c < coupled:
@@ -252,7 +253,11 @@
             low, high = edge(zs[-1], 2 * fields), edge(zs[0], 2 * fields + 1)
         above = jnp.concatenate([low, own[: rows - 1]], axis=0)
         below = jnp.concatenate([own[1:], high], axis=0)
-        out_ref[0, c] = own * keep + rate * (above + below - 2.0 * own)
+        out_ref[c] = own * keep + rate * (above + below - 2.0 * own)
+        copies.append(pltpu.make_async_copy(out_ref.at[c], out_hbm.at[0, c], sems.at[c]))
+        copies[c].start()
+    for copy in copies:
+        copy.wait()
 
 
 def zonal_tables(blocks, cols, waves):
@@ -353,10 +358,7 @@
     cell_rows = rows * cols // LANES
     waves = 256
     gv = lax.axis_index("gv")
-    own = lax.axis_index("gu") * split + gv
     src_idx = couple_src.reshape(peers, slots)
-    live = jnp.arange(slots, dtype=jnp.int32)[None, :] < couple_count.reshape(peers, 1)
-    weight = jnp.where(live, couple_weight.reshape(peers, slots), jnp.float32(0.0))
     more = rows * (levels - FC) // blocks
     frame = -(-more // 8) * 8
 
@@ -374,7 +376,9 @@
         cost_estimate=cost(1),
         name="early_pack",
     )(state, couple_dst.reshape(groups_x, blocks, slots))
-    src_idx, early = lax.optimization_barrier((src_idx, early))
+    after_pack, early = lax.optimization_barrier((lax.axis_index("gx"), early))
+    live = jnp.arange(slots, dtype=jnp.int32)[None, :] + jnp.minimum(after_pack, 0) < couple_count.reshape(peers, 1)
+    weight = jnp.where(live, couple_weight.reshape(peers, slots), jnp.float32(0.0))
     early = lax.all_to_all(early, ("gu", "gv"), split_axis=0, concat_axis=0, tiled=True)
 
     spot = np.zeros((FC, blocks, blocks, FC, 8), np.float32)
@@ -404,8 +408,6 @@
     resp = resp.reshape(each + 1, 2, half, blocks).transpose(0, 1, 3, 2)
     resp = jnp.pad(resp, ((0, 0), (0, 0), (0, 0), (0, waves - half)))
     scale = 2.0 / cols_all
-    mate_block = own + 1 - 2 * gv
-    flag = jnp.stack([lax.axis_index("gx") % 2, lax.axis_index("comp"), own, mate_block])
 
     index = jax.ShapeDtypeStruct((blocks, senders, slots), jnp.int32)
     framed = jax.ShapeDtypeStruct((blocks, frame, cols), F32)
@@ -423,7 +425,7 @@
     part, x, first, second = pl.pallas_call(
         functools.partial(scatter_kernel, split),
         out_shape=(part_shape, part_shape, edge, edge),
-        in_specs=[SMEM] + [VMEM] * 6,
+        in_specs=[VMEM] * 6,
         out_specs=(VMEM,) * 4,
         scratch_shapes=[
             pltpu.VMEM((senders, each * blocks, slots), F32),
@@ -432,11 +434,11 @@
         compiler_params=PARAMS,
         cost_estimate=cost(4),
         name="couple_scatter",
-    )(flag, arrived, circle, line, lane, state, mate)
+    )(arrived, circle, line, lane, state, mate)
     pairs = [(i, i ^ 1) for i in range(groups_x)]
     cross = [pair for i in range(1, groups_x - 1, 2) for pair in ((i, i + 1), (i + 1, i))]
+    second = lax.ppermute(second, "gx", cross)
     first = lax.ppermute(first, "gx", pairs)
-    second = lax.ppermute(second, "gx", cross)
     part = pl.pallas_call(
         functools.partial(part_kernel, scale),
         out_shape=jax.ShapeDtypeStruct((blocks, each, rows, cols), BF),
@@ -449,22 +451,23 @@
     incr = pl.pallas_call(
         functools.partial(edge_kernel, scale),
         out_shape=jax.ShapeDtypeStruct((blocks, each * rows + more + 2 * (each + 1), cols), BF),
-        in_specs=[SMEM] + [VMEM] * 8,
+        in_specs=[VMEM] * 8,
         out_specs=VMEM,
         compiler_params=PARAMS,
         cost_estimate=cost(1),
         name="edge_filter",
-    )(flag, first, second, part, circle_incr, resp, ahead, back, twiddle)
+    )(second, first, part, circle_incr, resp, ahead, back, twiddle)
     incr = lax.all_to_all(incr, ("gu", "gv"), split_axis=0, concat_axis=0, tiled=True)
     return pl.pallas_call(
         functools.partial(final_kernel, split, each),
         out_shape=jax.ShapeDtypeStruct((1, levels, rows, cols), F32),
-        in_specs=[SMEM] + [VMEM] * 4,
-        out_specs=VMEM,
+        in_specs=[VMEM] * 4,
+        out_specs=HBM,
+        scratch_shapes=[pltpu.VMEM((levels, rows, cols), F32), pltpu.SemaphoreType.DMA((levels,))],
         compiler_params=PARAMS,
         cost_estimate=cost(1),
         name="final_step",
-    )(flag, state, incr, diffusion, land_mask)
+    )(state, incr, diffusion, land_mask)
 
 
 def solution(mesh):

time: 68 us -> 65.9 us (0.969)
  Pallas kernels: 14.2 us -> 12.5 us
  starting transfers between devices: 22.9 us -> 21.9 us
  transfers between devices with their start and end apart: 6 -> 6, of which waited for: 5 -> 6; matrix products, arithmetic and copies ran while one was open for 1% -> 1% of each run, Pallas kernels for 9% -> 9%
where the time goes in v7:
time: 65.9 us; the launch traced here: 65.5 us
  starting transfers between devices  21.9 us (33%)
  blocking collectives  18.2 us (28%)
  Pallas kernels  12.5 us (19%)
  waiting for transfers between devices  9.64 us (15%)
  local copies, waits for them, and re-layouts  2.95 us (4%)
    all_to_all x1, blocking collectives, local(): lax.all_to_all(incr, ('gu', 'gv'), split_axis=0, concat_axis=0, tiled=True)  18.2 us
    all_to_all x1, starting transfers between devices, local(): lax.all_to_all(early, ('gu', 'gv'), split_axis=0, concat_axis=0, tiled=True)  8.61 us
    all_to_all x1, starting transfers between devices, local(): lax.all_to_all(crossed, ('gx', 'gv'), split_axis=0, concat_axis=0, tiled=...  7.62 us
    pallas_call x1, Pallas kernels, local(): pl.pallas_call(functools.partial(gather_kernel, split, blocks), out_shape...  4.02 us
    ppermute x1, starting transfers between devices, local(): second = lax.ppermute(second, 'gx', cross)  3.98 us
    all_to_all x1, waiting for transfers between devices, local(): lax.all_to_all(crossed, ('gx', 'gv'), split_axis=0, concat_axis=0, tiled=...  2.97 us
    pallas_call x1, Pallas kernels, local(): pl.pallas_call(functools.partial(scatter_kernel, split), out_shape=(part_...  2.93 us
    ppermute x1, waiting for transfers between devices, local(): second = lax.ppermute(second, 'gx', cross)  2.44 us
  transfers between devices with their start and end apart: 6, of which 6 were waited for; matrix products, arithmetic and copies ran while one was open for 1% of the time, Pallas kernels for 9%

profile of v7, /device:TPU:2, one launch (start us, length us, event | category | flops | bytes accessed | tf_op | source)
XLA Modules:
  0.0 65.5 jit_solution(7361514438779058437)
XLA Ops:
  0.0 0.0 copy-start
  0.0 0.0 copy-start.9
  0.0 2.3 %early_pack.1 = bf16[8,68,128]{2,1,0:T(8,128)(2,1)} custom-call(f32[1,8,24,384]{3,2,1,0:T(8,128)} %state_ref.3, s32[16,8,128]{2,1,0:T(8,128)} %bitcast.13), custom_call_target="tpu_custom_call" | custom-call | flops 1000000000 | bytes 3000000 | tf_op jit(solution)/shard_map/early_pack/pallas_call | solution.py:365
  2.3 0.0 copy-start.1
  2.3 8.6 %all-to-all-start = ((bf16[8,68,128]{2,1,0:T(8,128)(2,1)}), bf16[8,68,128]{2,1,0:T(8,128)(2,1)S(1)}, u32[]{:S(2)}, u32[]{:S(2)}) async-start(bf16[8,68,128]{2,1,0:T(8,128)(2,1)} %early_pack.1), calls=%async_computation | async-start | bytes 294912 | tf_op jit(solution)/shard_map/all_to_all | solution.py:382
  10.9 0.0 copy-start.10
  10.9 0.0 copy-done.9
  10.9 0.6 copy-done.10
  11.6 0.0 copy-start.2
  11.6 0.0 copy-start.8
  11.6 0.1 bitcast_select_fusion.weight_ref
  11.7 0.0 copy-done.1
  11.7 0.7 %copy-done.2 = s32[1,1,1,128,128]{4,3,2,1,0:T(8,128)S(1)} copy-done((s32[1,1,1,128,128]{4,3,2,1,0:T(8,128)S(1)}, s32[1,1,1,128,128]{4,3,2,1,0:T(8,128)}, u32[]{:S(2)}) %copy-start.2) | copy-done | bytes 65560
  12.4 0.0 copy-done.8
  12.4 4.0 %couple_gather.1 = bf16[32,16,128]{2,1,0:T(8,128)(2,1)S(1)} custom-call(f32[1,8,24,384]{3,2,1,0:T(8,128)S(1)} %copy-done.1, s32[128,128]{1,0:T(8,128)S(1)} %bitcast.11, f32[128,128]{1,0:T(8,128)S(1)} %bitcast_select_fusion.weight_ref, bf16[32,256]{1,0:T(8,128)(2,1)S(1)} %copy-done.8), custom_call_target="tpu_custom_call" | custom-call | flops 4000000000 | bytes 12000000 | tf_op jit(solution)/shard_map/couple_gather/pallas_call | solution.py:388
  16.4 0.0 collective-permute-start
  16.5 1.4 %collective-permute-done = bf16[32,16,128]{2,1,0:T(8,128)(2,1)} collective-permute-done((bf16[32,16,128]{2,1,0:T(8,128)(2,1)S(1)}, bf16[32,16,128]{2,1,0:T(8,128)(2,1)}, u32[]{:S(2)}, u32[]{:S(2)}) %collective-permute-start) | collective-permute-done | bytes 131104 | tf_op jit(solution)/shard_map/ppermute | solution.py:397
  17.9 2.4 %all-to-all-done.early_ref = bf16[8,68,128]{2,1,0:T(8,128)(2,1)S(1)} async-done(((bf16[8,68,128]{2,1,0:T(8,128)(2,1)}), bf16[8,68,128]{2,1,0:T(8,128)(2,1)S(1)}, u32[]{:S(2)}, u32[]{:S(2)}) %all-to-all-start) | async-done | bytes 139296 | tf_op jit(solution)/shard_map/all_to_all | solution.py:382
  20.3 7.6 %all-to-all-start.1 = ((bf16[32,16,128]{2,1,0:T(8,128)(2,1)}), bf16[32,16,128]{2,1,0:T(8,128)(2,1)S(1)}, u32[]{:S(2)}, u32[]{:S(2)}) async-start(bf16[32,16,128]{2,1,0:T(8,128)(2,1)} %collective-permute-done), calls=%async_computation.1 | async-start | bytes 262144 | tf_op jit(solution)/shard_map/all_to_all | solution.py:401
  28.0 0.0 copy-done
  28.0 1.6 %collective-permute-start.1 = (bf16[2,24,384]{2,1,0:T(8,128)(2,1)S(1)}, bf16[2,24,384]{2,1,0:T(8,128)(2,1)S(1)}, u32[]{:S(2)}, u32[]{:S(2)}) collective-permute-start(bf16[2,24,384]{2,1,0:T(8,128)(2,1)S(1)} %fusion), channel_id=1, source_target_pairs={{0,1},{1,0},{2,3},{3,2},{4,5},{5,4},{6,7},{7,6},{8,9},{9,8},{10,11... | collective-permute-start | bytes 110600 | tf_op jit(solution)/shard_map/ppermute | solution.py:400
  29.6 0.1 concatenate.9
  29.7 0.1 copy.14
  29.8 0.0 copy-start.6
  29.8 0.2 concatenate.8
  30.1 0.0 copy-start.5
  30.1 0.2 copy.13
  30.2 0.0 copy-start.7
  30.3 0.5 copy-done.6
  30.8 0.3 copy-done.5
  31.1 0.0 copy-done.7
  31.1 0.7 %circle_filter.1 = (f32[8,16,384]{2,1,0:T(8,128)S(1)}, f32[8,16,384]{2,1,0:T(8,128)S(1)}, s32[8,32,128]{2,1,0:T(8,128)S(1)}, s32[8,32,128]{2,1,0:T(8,128)S(1)}) custom-call(bf16[8,68,128]{2,1,0:T(8,128)(2,1)S(1)} %all-to-all-done.early_ref, f32[2,8,256]{2,1,0:T(8,128)S(1)} %slice_bitcast_fusion.resp_ref, bf16[384,512]{1,0:T(8,128)(2,1)S(1)} %copy-done.6, ...), custom_call_target="tpu_custom_call" | custom-call | flops 2000000000 | bytes 6000000 | tf_op jit(solution)/shard_map/circle_filter/pallas_call | solution.py:414
  31.8 0.3 collective-permute-done.1.mate_ref
  32.1 3.0 %all-to-all-done.1.arrived_ref = bf16[32,16,128]{2,1,0:T(8,128)(2,1)S(1)} async-done(((bf16[32,16,128]{2,1,0:T(8,128)(2,1)}), bf16[32,16,128]{2,1,0:T(8,128)(2,1)S(1)}, u32[]{:S(2)}, u32[]{:S(2)}) %all-to-all-start.1) | async-done | bytes 131104 | tf_op jit(solution)/shard_map/all_to_all | solution.py:401
  35.1 2.9 %couple_scatter.1 = (f32[2,8,24,384]{3,2,1,0:T(8,128)S(1)}, f32[2,8,24,384]{3,2,1,0:T(8,128)S(1)}, bf16[24,384]{1,0:T(8,128)(2,1)S(1)}, bf16[24,384]{1,0:T(8,128)(2,1)S(1)}) custom-call(bf16[32,16,128]{2,1,0:T(8,128)(2,1)S(1)} %all-to-all-done.1.arrived_ref, f32[8,16,384]{2,1,0:T(8,128)S(1)} %get-tuple-element.24.circle_ref, ...), custom_call_target="tpu_custom_call" | custom-call | flops 4000000000 | bytes 12000000 | tf_op jit(solution)/shard_map/couple_scatter/pallas_call | solution.py:425
  38.1 4.0 %collective-permute-start.2 = (bf16[24,384]{1,0:T(8,128)(2,1)S(1)}, bf16[24,384]{1,0:T(8,128)(2,1)S(1)}, u32[]{:S(2)}, u32[]{:S(2)}) collective-permute-start(bf16[24,384]{1,0:T(8,128)(2,1)S(1)} %get-tuple-element.28), channel_id=1, source_target_pairs={{8,16},{16,8},{24,32},{32,24},{40,48},{48,40},{56,64},{64,56},{72,... | collective-permute-start | bytes 55304 | tf_op jit(solution)/shard_map/ppermute | solution.py:440
  42.1 0.1 collective-permute-start.3
  42.2 1.2 %part_filter.1.part_ref = bf16[8,2,24,384]{3,2,1,0:T(8,128)(2,1)S(1)} custom-call(f32[2,8,24,384]{3,2,1,0:T(8,128)S(1)} %get-tuple-element.30.part_ref, f32[2,8,24,384]{3,2,1,0:T(8,128)S(1)} %get-tuple-element.31.x_ref, f32[3,2,8,256]{3,2,1,0:T(8,128)S(1)} %pad.4.resp_ref, bf16[384,512]{1,0:T(8,128)(2,1)S(1)} %copy-done.6, bf16[256,768]{1,0:T(8,128)(2,1)S(1)} %copy-done.5, ...), custom_call_target="tpu_custom_call" | custom-call | flops 3000000000 | bytes 9000000 | tf_op jit(solution)/shard_map/part_filter/pallas_call | solution.py:442
  43.4 2.4 %collective-permute-done.2.second_ref = bf16[24,384]{1,0:T(8,128)(2,1)S(1)} collective-permute-done((bf16[24,384]{1,0:T(8,128)(2,1)S(1)}, bf16[24,384]{1,0:T(8,128)(2,1)S(1)}, u32[]{:S(2)}, u32[]{:S(2)}) %collective-permute-start.2) | collective-permute-done | bytes 18464 | tf_op jit(solution)/shard_map/ppermute | solution.py:440
  45.8 0.1 collective-permute-done.3.first_ref
  45.9 0.5 edge_filter.1
  46.4 0.0 copy-start.3
  46.4 0.0 copy-start.4
  46.4 18.2 %all_to_all.15.back_ref = bf16[8,66,384]{2,1,0:T(8,128)(2,1)S(1)} all-to-all(bf16[8,66,384]{2,1,0:T(8,128)(2,1)S(1)} %edge_filter.1), channel_id=1, replica_groups=mesh['comp'=2,'gx'=16,'gu'=4,'gv'=2] {'gu','gv'}, dimensions={0} | all-to-all | bytes 811008 | tf_op jit(solution)/shard_map/all_to_all | solution.py:460
  64.6 0.0 copy-done.3
  64.6 0.0 copy-done.4
  64.6 0.9 %final_step.1 = f32[1,8,24,384]{3,2,1,0:T(8,128)} custom-call(f32[1,8,24,384]{3,2,1,0:T(8,128)S(1)} %copy-done.1, bf16[8,66,384]{2,1,0:T(8,128)(2,1)S(1)} %all_to_all.15.back_ref, f32[1,24,384]{2,1,0:T(8,128)S(1)} %copy-done.3, s32[24,384]{1,0:T(8,128)S(1)} %copy-done.4), custom_call_target="tpu_custom_call" | custom-call | flops 1000000000 | bytes 3000000 | tf_op jit(solution)/shard_map/final_step/pallas_call | solution.py:461
  (7 shorter events, 0.1 us)
Async XLA Ops:
  0.0 28.0 %copy-start = (f32[1,8,3072]{2,1,0:T(8,128)S(1)}, f32[1,8,3072]{2,1,0:T(8,128)}, u32[]{:S(2)}) copy-start(f32[1,8,3072]{2,1,0:T(8,128)} %param.13) | copy-start | bytes 294916
  0.0 10.9 %copy-start.9 = (f32[1,1,1,128,128]{4,3,2,1,0:T(8,128)S(1)}, f32[1,1,1,128,128]{4,3,2,1,0:T(8,128)}, u32[]{:S(2)}) copy-start(f32[1,1,1,128,128]{4,3,2,1,0:T(8,128)} %param.18) | copy-start | bytes 196612
  2.3 9.4 %copy-start.1 = (f32[1,8,24,384]{3,2,1,0:T(8,128)S(1)}, f32[1,8,24,384]{3,2,1,0:T(8,128)}, u32[]{:S(2)}) copy-start(f32[1,8,24,384]{3,2,1,0:T(8,128)} %state_ref.3) | copy-start | bytes 884740
  2.3 18.0 %all-to-all-start = ((bf16[8,68,128]{2,1,0:T(8,128)(2,1)}), bf16[8,68,128]{2,1,0:T(8,128)(2,1)S(1)}, u32[]{:S(2)}, u32[]{:S(2)}) async-start(bf16[8,68,128]{2,1,0:T(8,128)(2,1)} %early_pack.1), calls=%async_computation | async-start | bytes 294912 | tf_op jit(solution)/shard_map/all_to_all | solution.py:382
  10.9 0.7 %copy-start.10 = (s32[1,1,1,128]{3,2,1,0:T(1,128)S(1)}, s32[1,1,1,128]{3,2,1,0:T(1,128)}, u32[]{:S(2)}) copy-start(s32[1,1,1,128]{3,2,1,0:T(1,128)} %param.19) | copy-start | bytes 1540
  11.6 0.8 %copy-start.2 = (s32[1,1,1,128,128]{4,3,2,1,0:T(8,128)S(1)}, s32[1,1,1,128,128]{4,3,2,1,0:T(8,128)}, u32[]{:S(2)}) copy-start(s32[1,1,1,128,128]{4,3,2,1,0:T(8,128)} %param.16) | copy-start | bytes 196612
  11.6 0.8 %copy-start.8 = (bf16[32,256]{1,0:T(8,128)(2,1)S(1)}, bf16[32,256]{1,0:T(8,128)(2,1)}, u32[]{:S(2)}) copy-start(bf16[32,256]{1,0:T(8,128)(2,1)} %constant.39.clone.pick_ref) | copy-start | bytes 49156
  16.4 1.5 %collective-permute-start = (bf16[32,16,128]{2,1,0:T(8,128)(2,1)S(1)}, bf16[32,16,128]{2,1,0:T(8,128)(2,1)}, u32[]{:S(2)}, u32[]{:S(2)}) collective-permute-start(bf16[32,16,128]{2,1,0:T(8,128)(2,1)S(1)} %couple_gather.1), channel_id=1, source_target_pairs={{0,128},{128,0},{1,129},{129,1},{2,130},{130,2},{3,131},{131,3},{4... | collective-permute-start | bytes 393224 | tf_op jit(solution)/shard_map/ppermute | solution.py:397
  20.3 14.8 %all-to-all-start.1 = ((bf16[32,16,128]{2,1,0:T(8,128)(2,1)}), bf16[32,16,128]{2,1,0:T(8,128)(2,1)S(1)}, u32[]{:S(2)}, u32[]{:S(2)}) async-start(bf16[32,16,128]{2,1,0:T(8,128)(2,1)} %collective-permute-done), calls=%async_computation.1 | async-start | bytes 262144 | tf_op jit(solution)/shard_map/all_to_all | solution.py:401
  28.0 4.1 %collective-permute-start.1 = (bf16[2,24,384]{2,1,0:T(8,128)(2,1)S(1)}, bf16[2,24,384]{2,1,0:T(8,128)(2,1)S(1)}, u32[]{:S(2)}, u32[]{:S(2)}) collective-permute-start(bf16[2,24,384]{2,1,0:T(8,128)(2,1)S(1)} %fusion), channel_id=1, source_target_pairs={{0,1},{1,0},{2,3},{3,2},{4,5},{5,4},{6,7},{7,6},{8,9},{9,8},{10,11... | collective-permute-start | bytes 110600 | tf_op jit(solution)/shard_map/ppermute | solution.py:400
  29.8 1.0 %copy-start.6 = (bf16[384,512]{1,0:T(8,128)(2,1)S(1)}, bf16[384,512]{1,0:T(8,128)(2,1)}, u32[]{:S(2)}) copy-start(bf16[384,512]{1,0:T(8,128)(2,1)} %constant.40.clone.ahead_ref) | copy-start | bytes 1179652
  30.1 1.0 %copy-start.5 = (bf16[256,768]{1,0:T(8,128)(2,1)S(1)}, bf16[256,768]{1,0:T(8,128)(2,1)}, u32[]{:S(2)}) copy-start(bf16[256,768]{1,0:T(8,128)(2,1)} %constant.41.clone.back_ref) | copy-start | bytes 1179652
  30.2 0.9 %copy-start.7 = (f32[2,8,384]{2,1,0:T(8,128)S(1)}, f32[2,8,384]{2,1,0:T(8,128)}, u32[]{:S(2)}) copy-start(f32[2,8,384]{2,1,0:T(8,128)} %constant.42.clone.twiddle_ref) | copy-start | bytes 73732
  38.1 7.8 %collective-permute-start.2 = (bf16[24,384]{1,0:T(8,128)(2,1)S(1)}, bf16[24,384]{1,0:T(8,128)(2,1)S(1)}, u32[]{:S(2)}, u32[]{:S(2)}) collective-permute-start(bf16[24,384]{1,0:T(8,128)(2,1)S(1)} %get-tuple-element.28), channel_id=1, source_target_pairs={{8,16},{16,8},{24,32},{32,24},{40,48},{48,40},{56,64},{64,56},{72,... | collective-permute-start | bytes 55304 | tf_op jit(solution)/shard_map/ppermute | solution.py:440
  42.1 3.8 %collective-permute-start.3 = (bf16[24,384]{1,0:T(8,128)(2,1)S(1)}, bf16[24,384]{1,0:T(8,128)(2,1)S(1)}, u32[]{:S(2)}, u32[]{:S(2)}) collective-permute-start(bf16[24,384]{1,0:T(8,128)(2,1)S(1)} %get-tuple-element.29), channel_id=1, source_target_pairs={{0,8},{8,0},{16,24},{24,16},{32,40},{40,32},{48,56},{56,48},{64,72... | collective-permute-start | bytes 55304 | tf_op jit(solution)/shard_map/ppermute | solution.py:441
  46.4 18.2 %copy-start.3 = (f32[1,24,384]{2,1,0:T(8,128)S(1)}, f32[1,24,384]{2,1,0:T(8,128)}, u32[]{:S(2)}) copy-start(f32[1,24,384]{2,1,0:T(8,128)} %rate_ref.1) | copy-start | bytes 110596
  46.4 18.2 %copy-start.4 = (s32[24,384]{1,0:T(8,128)S(1)}, s32[24,384]{1,0:T(8,128)}, u32[]{:S(2)}) copy-start(s32[24,384]{1,0:T(8,128)} %land_ref.1) | copy-start | bytes 110596

commit v8 on v7

--- a/solution.py
+++ b/solution.py
@@ -76,7 +76,7 @@
         early_ref[z, senders:, :] = tiles(state_ref[u, v * own_rows : (v + 1) * own_rows, :]).astype(BF)
 
 
-def gather_kernel(split, blocks, surf_ref, src_ref, weight_ref, pick_ref, out_ref):
+def gather_kernel(split, blocks, surf_ref, src_ref, all_ref, pick_ref, count_ref, out_ref, weight_ref):
     _, _, rows, cols = surf_ref.shape
     peers, slots = src_ref.shape
     fc = split * out_ref.shape[1] // blocks
@@ -87,6 +87,10 @@
     surface = [tiles(surf_ref[0, c]) for c in range(fc)]
     surface = jnp.concatenate([jnp.concatenate([x[:half], x[shift:]], axis=1) for x in surface], axis=0).astype(BF)
     spot = lax.broadcasted_iota(jnp.int32, (half, slots), 0)
+    slot = lax.broadcasted_iota(jnp.int32, (peers, slots), 1)
+    same = slot == lax.broadcasted_iota(jnp.int32, (peers, slots), 0)
+    limit = jnp.sum(jnp.where(same, count_ref[...].astype(F32), 0.0), axis=1, keepdims=True)
+    weight_ref[...] = jnp.where(slot.astype(F32) < limit, all_ref[...], 0.0)
 
     def step(g, carry):
         base = pl.multiple_of(g * blocks, blocks)
@@ -190,11 +194,12 @@
 
 def part_kernel(scale, part_ref, x_ref, resp_ref, ahead_ref, back_ref, twiddle_ref, out_ref):
     blocks, fields, rows, cols = out_ref.shape
+    xs = [[x_ref[c, h] for h in range(blocks)] for c in range(fields)]
+    resps = [(resp_ref[c, 0], resp_ref[c, 1]) for c in range(fields)]
+    incrs = zonal_sets(xs, resps, ahead_ref, back_ref, twiddle_ref)
     for c in range(fields):
-        x = [x_ref[c, h] for h in range(blocks)]
-        incr = zonal_rows(x, resp_ref[c, 0], resp_ref[c, 1], ahead_ref, back_ref, twiddle_ref)
         for h in range(blocks):
-            out_ref[h, c] = (incr[h] * scale + part_ref[c, h]).astype(BF)
+            out_ref[h, c] = (incrs[c][h] * scale + part_ref[c, h]).astype(BF)
 
 
 def edge_kernel(
@@ -278,10 +283,9 @@
     return resp[r] if isinstance(resp, list) else resp[r : r + 1, :]
 
 
-def zonal_rows(x, resp_cos, resp_sin, ahead_ref, back_ref, twiddle_ref):
+def zonal_ahead(x, twiddle_ref):
     blocks = len(x)
     rows, cols = x[0].shape
-    waves = ahead_ref.shape[1] // 2
     half = math.sqrt(0.5)
     a = [x[i] + x[i + 4] for i in range(4)]
     b = [x[i] - x[i + 4] for i in range(4)]
@@ -304,7 +308,11 @@
         else:
             real.append(re * ct + im * st)
             imag.append(im * ct - re * st)
-    spec = jnp.dot(jnp.concatenate(real + imag, axis=0).astype(BF), ahead_ref[...], preferred_element_type=F32)
+    return real + imag
+
+
+def zonal_middle(spec, blocks, rows, resp_cos, resp_sin):
+    waves = spec.shape[1] // 2
     cosine, sine = [], []
     for r in range(blocks):
         own = spec[r * rows : (r + 1) * rows]
@@ -314,7 +322,12 @@
             c, s = c + other[:, waves:], s - other[:, :waves]
         cosine.append(c * response_row(resp_cos, r))
         sine.append(s * response_row(resp_sin, r))
-    full = jnp.dot(jnp.concatenate(cosine + sine, axis=0).astype(BF), back_ref[...], preferred_element_type=F32)
+    return cosine + sine
+
+
+def zonal_back(full, blocks, rows, twiddle_ref):
+    cols = full.shape[1] // 2
+    half = math.sqrt(0.5)
     u = []
     for r in range(blocks):
         fc = full[r * rows : (r + 1) * rows]
@@ -344,6 +357,24 @@
     return pl.CostEstimate(flops=micros * 10**9, bytes_accessed=micros * 3 * 10**6, transcendentals=0)
 
 
+def zonal_sets(xs, resps, ahead_ref, back_ref, twiddle_ref):
+    blocks = len(xs[0])
+    rows = xs[0][0].shape[0]
+    lines = [line for x in xs for line in zonal_ahead(x, twiddle_ref)]
+    spec = jnp.dot(jnp.concatenate(lines, axis=0).astype(BF), ahead_ref[...], preferred_element_type=F32)
+    each = spec.shape[0] // len(xs)
+    lines = []
+    for at, (resp_cos, resp_sin) in enumerate(resps):
+        lines += zonal_middle(spec[at * each : (at + 1) * each], blocks, rows, resp_cos, resp_sin)
+    full = jnp.dot(jnp.concatenate(lines, axis=0).astype(BF), back_ref[...], preferred_element_type=F32)
+    each = full.shape[0] // len(xs)
+    return [zonal_back(full[at * each : (at + 1) * each], blocks, rows, twiddle_ref) for at in range(len(xs))]
+
+
+def zonal_rows(x, resp_cos, resp_sin, ahead_ref, back_ref, twiddle_ref):
+    return zonal_sets([x], [(resp_cos, resp_sin)], ahead_ref, back_ref, twiddle_ref)[0]
+
+
 def local(
     state, response, diffusion, land_mask, couple_src, couple_dst, couple_weight, couple_count
 ):
@@ -376,9 +407,7 @@
         cost_estimate=cost(1),
         name="early_pack",
     )(state, couple_dst.reshape(groups_x, blocks, slots))
-    after_pack, early = lax.optimization_barrier((lax.axis_index("gx"), early))
-    live = jnp.arange(slots, dtype=jnp.int32)[None, :] + jnp.minimum(after_pack, 0) < couple_count.reshape(peers, 1)
-    weight = jnp.where(live, couple_weight.reshape(peers, slots), jnp.float32(0.0))
+    count, early = lax.optimization_barrier((couple_count.reshape(1, peers), early))
     early = lax.all_to_all(early, ("gu", "gv"), split_axis=0, concat_axis=0, tiled=True)
 
     spot = np.zeros((FC, blocks, blocks, FC, 8), np.float32)
@@ -388,12 +417,13 @@
     outgoing = pl.pallas_call(
         functools.partial(gather_kernel, split, blocks),
         out_shape=jax.ShapeDtypeStruct((senders, each * blocks, slots), BF),
-        in_specs=[VMEM] * 4,
+        in_specs=[VMEM] * 5,
         out_specs=VMEM,
+        scratch_shapes=[pltpu.VMEM((peers, slots), F32)],
         compiler_params=PARAMS,
         cost_estimate=cost(4),
         name="couple_gather",
-    )(state, src_idx, weight, jnp.asarray(spot.reshape(FC * blocks, -1), BF))
+    )(state, src_idx, couple_weight.reshape(peers, slots), jnp.asarray(spot.reshape(FC * blocks, -1), BF), count)
     crossed = lax.ppermute(outgoing, "comp", [(0, 1), (1, 0)])
     mate = lax.dynamic_slice_in_dim(state[0], (1 - gv) * each, each, 0).astype(BF)
     crossed, early, mate, response = lax.optimization_barrier((crossed, early, mate, response))

time: 65.9 us -> 65.1 us (0.988)
  waiting for transfers between devices: 9.64 us -> 10.6 us
  blocking collectives: 18.2 us -> 17.3 us
  local copies, waits for them, and re-layouts: 2.95 us -> 2.19 us
    all_to_all x1, waiting for transfers between devices: 2.4 us -> 3.26 us  [local(): lax.all_to_all(early, ('gu', 'gv'), split_axis=0, concat_axis=0, tiled=True)]
    all_to_all x1, blocking collectives: 18.2 us -> 17.3 us  [local(): lax.all_to_all(incr, ('gu', 'gv'), split_axis=0, concat_axis=0, tiled=True)]
    unnamed x22, local copies, waits for them, and re-layouts: 2.25 us -> 1.48 us
where the time goes in v8:
time: 65.1 us; the launch traced here: 64.7 us
  starting transfers between devices  21.8 us (33%)
  blocking collectives  17.3 us (27%)
  Pallas kernels  12.4 us (19%)
  waiting for transfers between devices  10.6 us (16%)
  local copies, waits for them, and re-layouts  2.19 us (3%)
    all_to_all x1, blocking collectives, local(): lax.all_to_all(incr, ('gu', 'gv'), split_axis=0, concat_axis=0, tiled=True)  17.3 us
    all_to_all x1, starting transfers between devices, local(): lax.all_to_all(early, ('gu', 'gv'), split_axis=0, concat_axis=0, tiled=True)  8.61 us
    all_to_all x1, starting transfers between devices, local(): lax.all_to_all(crossed, ('gx', 'gv'), split_axis=0, concat_axis=0, tiled=...  7.62 us
    pallas_call x1, Pallas kernels, local(): pl.pallas_call(functools.partial(gather_kernel, split, blocks), out_shape...  4.02 us
    ppermute x1, starting transfers between devices, local(): second = lax.ppermute(second, 'gx', cross)  3.97 us
    all_to_all x1, waiting for transfers between devices, local(): lax.all_to_all(early, ('gu', 'gv'), split_axis=0, concat_axis=0, tiled=True)  3.26 us
    all_to_all x1, waiting for transfers between devices, local(): lax.all_to_all(crossed, ('gx', 'gv'), split_axis=0, concat_axis=0, tiled=...  2.97 us
    pallas_call x1, Pallas kernels, local(): pl.pallas_call(functools.partial(scatter_kernel, split), out_shape=(part_...  2.94 us
  transfers between devices with their start and end apart: 6, of which 6 were waited for; matrix products, arithmetic and copies ran while one was open for 1% of the time, Pallas kernels for 9%

profile of v8, /device:TPU:2, one launch (start us, length us, event | category | flops | bytes accessed | tf_op | source)
XLA Modules:
  0.0 64.7 jit_solution(4012110750393489254)
XLA Ops:
  0.0 0.0 copy-start
  0.0 0.0 copy-start.2
  0.0 0.0 copy-start.3
  0.0 0.0 copy-start.10
  0.0 2.3 %early_pack.1 = bf16[8,68,128]{2,1,0:T(8,128)(2,1)} custom-call(f32[1,8,24,384]{3,2,1,0:T(8,128)} %state_ref.3, s32[16,8,128]{2,1,0:T(8,128)} %bitcast.13), custom_call_target="tpu_custom_call" | custom-call | flops 1000000000 | bytes 3000000 | tf_op jit(solution)/shard_map/early_pack/pallas_call | solution.py:396
  2.3 0.0 copy-start.1
  2.3 8.6 %all-to-all-start = ((bf16[8,68,128]{2,1,0:T(8,128)(2,1)}), bf16[8,68,128]{2,1,0:T(8,128)(2,1)S(1)}, u32[]{:S(2)}, u32[]{:S(2)}) async-start(bf16[8,68,128]{2,1,0:T(8,128)(2,1)} %early_pack.1), calls=%async_computation | async-start | bytes 294912 | tf_op jit(solution)/shard_map/all_to_all | solution.py:411
  10.9 0.0 copy-start.6
  10.9 0.0 copy-done.2
  10.9 0.0 copy-done.3
  11.0 0.0 copy-done.10
  11.0 0.0 copy-done.1
  11.0 0.6 copy-done.6
  11.6 4.0 %couple_gather.1 = bf16[32,16,128]{2,1,0:T(8,128)(2,1)S(1)} custom-call(f32[1,8,24,384]{3,2,1,0:T(8,128)S(1)} %copy-done.1, s32[128,128]{1,0:T(8,128)S(1)} %bitcast.10, f32[128,128]{1,0:T(8,128)S(1)} %bitcast.11, bf16[32,256]{1,0:T(8,128)(2,1)S(1)} %copy-done.10, s32[1,128]{1,0:T(1,128)S(1)} %bitcast.12), custom_call_target="tpu_custom_call" | custom-call | flops 4000000000 | bytes 12000000 | tf_op jit(solution)/shard_map/couple_gather/pallas_call | solution.py:417
  15.6 0.0 collective-permute-start
  15.6 1.4 %collective-permute-done = bf16[32,16,128]{2,1,0:T(8,128)(2,1)} collective-permute-done((bf16[32,16,128]{2,1,0:T(8,128)(2,1)S(1)}, bf16[32,16,128]{2,1,0:T(8,128)(2,1)}, u32[]{:S(2)}, u32[]{:S(2)}) %collective-permute-start) | collective-permute-done | bytes 131104 | tf_op jit(solution)/shard_map/ppermute | solution.py:427
  17.1 3.3 %all-to-all-done.early_ref = bf16[8,68,128]{2,1,0:T(8,128)(2,1)S(1)} async-done(((bf16[8,68,128]{2,1,0:T(8,128)(2,1)}), bf16[8,68,128]{2,1,0:T(8,128)(2,1)S(1)}, u32[]{:S(2)}, u32[]{:S(2)}) %all-to-all-start) | async-done | bytes 139296 | tf_op jit(solution)/shard_map/all_to_all | solution.py:411
  20.3 7.6 %all-to-all-start.1 = ((bf16[32,16,128]{2,1,0:T(8,128)(2,1)}), bf16[32,16,128]{2,1,0:T(8,128)(2,1)S(1)}, u32[]{:S(2)}, u32[]{:S(2)}) async-start(bf16[32,16,128]{2,1,0:T(8,128)(2,1)} %collective-permute-done), calls=%async_computation.1 | async-start | bytes 262144 | tf_op jit(solution)/shard_map/all_to_all | solution.py:431
  28.0 0.0 copy-done
  28.1 1.6 %collective-permute-start.1 = (bf16[2,24,384]{2,1,0:T(8,128)(2,1)S(1)}, bf16[2,24,384]{2,1,0:T(8,128)(2,1)S(1)}, u32[]{:S(2)}, u32[]{:S(2)}) collective-permute-start(bf16[2,24,384]{2,1,0:T(8,128)(2,1)S(1)} %fusion), channel_id=1, source_target_pairs={{0,1},{1,0},{2,3},{3,2},{4,5},{5,4},{6,7},{7,6},{8,9},{9,8},{10,11... | collective-permute-start | bytes 110600 | tf_op jit(solution)/shard_map/ppermute | solution.py:430
  29.6 0.1 concatenate.9
  29.7 0.1 copy.14
  29.8 0.0 copy-start.8
  29.8 0.2 concatenate.8
  30.1 0.0 copy-start.7
  30.1 0.2 copy.13
  30.3 0.0 copy-start.9
  30.3 0.5 copy-done.8
  30.9 0.3 copy-done.7
  31.1 0.0 copy-done.9
  31.1 0.7 %circle_filter.1 = (f32[8,16,384]{2,1,0:T(8,128)S(1)}, f32[8,16,384]{2,1,0:T(8,128)S(1)}, s32[8,32,128]{2,1,0:T(8,128)S(1)}, s32[8,32,128]{2,1,0:T(8,128)S(1)}) custom-call(bf16[8,68,128]{2,1,0:T(8,128)(2,1)S(1)} %all-to-all-done.early_ref, f32[2,8,256]{2,1,0:T(8,128)S(1)} %slice_bitcast_fusion.resp_ref, bf16[384,512]{1,0:T(8,128)(2,1)S(1)} %copy-done.8, ...), custom_call_target="tpu_custom_call" | custom-call | flops 2000000000 | bytes 6000000 | tf_op jit(solution)/shard_map/circle_filter/pallas_call | solution.py:444
  31.9 0.3 collective-permute-done.1.mate_ref
  32.2 3.0 %all-to-all-done.1.arrived_ref = bf16[32,16,128]{2,1,0:T(8,128)(2,1)S(1)} async-done(((bf16[32,16,128]{2,1,0:T(8,128)(2,1)}), bf16[32,16,128]{2,1,0:T(8,128)(2,1)S(1)}, u32[]{:S(2)}, u32[]{:S(2)}) %all-to-all-start.1) | async-done | bytes 131104 | tf_op jit(solution)/shard_map/all_to_all | solution.py:431
  35.1 2.9 %couple_scatter.1 = (f32[2,8,24,384]{3,2,1,0:T(8,128)S(1)}, f32[2,8,24,384]{3,2,1,0:T(8,128)S(1)}, bf16[24,384]{1,0:T(8,128)(2,1)S(1)}, bf16[24,384]{1,0:T(8,128)(2,1)S(1)}) custom-call(bf16[32,16,128]{2,1,0:T(8,128)(2,1)S(1)} %all-to-all-done.1.arrived_ref, f32[8,16,384]{2,1,0:T(8,128)S(1)} %get-tuple-element.24.circle_ref, ...), custom_call_target="tpu_custom_call" | custom-call | flops 4000000000 | bytes 12000000 | tf_op jit(solution)/shard_map/couple_scatter/pallas_call | solution.py:455
  38.1 4.0 %collective-permute-start.2 = (bf16[24,384]{1,0:T(8,128)(2,1)S(1)}, bf16[24,384]{1,0:T(8,128)(2,1)S(1)}, u32[]{:S(2)}, u32[]{:S(2)}) collective-permute-start(bf16[24,384]{1,0:T(8,128)(2,1)S(1)} %get-tuple-element.28), channel_id=1, source_target_pairs={{8,16},{16,8},{24,32},{32,24},{40,48},{48,40},{56,64},{64,56},{72,... | collective-permute-start | bytes 55304 | tf_op jit(solution)/shard_map/ppermute | solution.py:470
  42.1 0.1 collective-permute-start.3
  42.2 1.1 %part_filter.1.part_ref = bf16[8,2,24,384]{3,2,1,0:T(8,128)(2,1)S(1)} custom-call(f32[2,8,24,384]{3,2,1,0:T(8,128)S(1)} %get-tuple-element.30.part_ref, f32[2,8,24,384]{3,2,1,0:T(8,128)S(1)} %get-tuple-element.31.x_ref, f32[3,2,8,256]{3,2,1,0:T(8,128)S(1)} %pad.4.resp_ref, bf16[384,512]{1,0:T(8,128)(2,1)S(1)} %copy-done.8, bf16[256,768]{1,0:T(8,128)(2,1)S(1)} %copy-done.7, ...), custom_call_target="tpu_custom_call" | custom-call | flops 3000000000 | bytes 9000000 | tf_op jit(solution)/shard_map/part_filter/pallas_call | solution.py:472
  43.3 2.6 %collective-permute-done.2.second_ref = bf16[24,384]{1,0:T(8,128)(2,1)S(1)} collective-permute-done((bf16[24,384]{1,0:T(8,128)(2,1)S(1)}, bf16[24,384]{1,0:T(8,128)(2,1)S(1)}, u32[]{:S(2)}, u32[]{:S(2)}) %collective-permute-start.2) | collective-permute-done | bytes 18464 | tf_op jit(solution)/shard_map/ppermute | solution.py:470
  45.9 0.1 collective-permute-done.3.first_ref
  45.9 0.5 edge_filter.1
  46.4 0.0 copy-start.4
  46.4 0.0 copy-start.5
  46.5 17.3 %all_to_all.15.back_ref = bf16[8,66,384]{2,1,0:T(8,128)(2,1)S(1)} all-to-all(bf16[8,66,384]{2,1,0:T(8,128)(2,1)S(1)} %edge_filter.1), channel_id=1, replica_groups=mesh['comp'=2,'gx'=16,'gu'=4,'gv'=2] {'gu','gv'}, dimensions={0} | all-to-all | bytes 811008 | tf_op jit(solution)/shard_map/all_to_all | solution.py:490
  63.8 0.0 copy-done.4
  63.8 0.0 copy-done.5
  63.8 0.9 %final_step.1 = f32[1,8,24,384]{3,2,1,0:T(8,128)} custom-call(f32[1,8,24,384]{3,2,1,0:T(8,128)S(1)} %copy-done.1, bf16[8,66,384]{2,1,0:T(8,128)(2,1)S(1)} %all_to_all.15.back_ref, f32[1,24,384]{2,1,0:T(8,128)S(1)} %copy-done.4, s32[24,384]{1,0:T(8,128)S(1)} %copy-done.5), custom_call_target="tpu_custom_call" | custom-call | flops 1000000000 | bytes 3000000 | tf_op jit(solution)/shard_map/final_step/pallas_call | solution.py:491
  (6 shorter events, 0.1 us)
Async XLA Ops:
  0.0 28.0 %copy-start = (f32[1,8,3072]{2,1,0:T(8,128)S(1)}, f32[1,8,3072]{2,1,0:T(8,128)}, u32[]{:S(2)}) copy-start(f32[1,8,3072]{2,1,0:T(8,128)} %param.13) | copy-start | bytes 294916
  0.0 10.9 %copy-start.2 = (s32[1,1,1,128,128]{4,3,2,1,0:T(8,128)S(1)}, s32[1,1,1,128,128]{4,3,2,1,0:T(8,128)}, u32[]{:S(2)}) copy-start(s32[1,1,1,128,128]{4,3,2,1,0:T(8,128)} %param.16) | copy-start | bytes 196612
  0.0 10.9 %copy-start.3 = (f32[1,1,1,128,128]{4,3,2,1,0:T(8,128)S(1)}, f32[1,1,1,128,128]{4,3,2,1,0:T(8,128)}, u32[]{:S(2)}) copy-start(f32[1,1,1,128,128]{4,3,2,1,0:T(8,128)} %param.18) | copy-start | bytes 196612
  0.0 10.9 %copy-start.10 = (bf16[32,256]{1,0:T(8,128)(2,1)S(1)}, bf16[32,256]{1,0:T(8,128)(2,1)}, u32[]{:S(2)}) copy-start(bf16[32,256]{1,0:T(8,128)(2,1)} %constant.33.clone.pick_ref) | copy-start | bytes 49156
  2.3 8.7 %copy-start.1 = (f32[1,8,24,384]{3,2,1,0:T(8,128)S(1)}, f32[1,8,24,384]{3,2,1,0:T(8,128)}, u32[]{:S(2)}) copy-start(f32[1,8,24,384]{3,2,1,0:T(8,128)} %state_ref.3) | copy-start | bytes 884740
  2.3 18.0 %all-to-all-start = ((bf16[8,68,128]{2,1,0:T(8,128)(2,1)}), bf16[8,68,128]{2,1,0:T(8,128)(2,1)S(1)}, u32[]{:S(2)}, u32[]{:S(2)}) async-start(bf16[8,68,128]{2,1,0:T(8,128)(2,1)} %early_pack.1), calls=%async_computation | async-start | bytes 294912 | tf_op jit(solution)/shard_map/all_to_all | solution.py:411
  10.9 0.7 %copy-start.6 = (s32[1,1,1,128]{3,2,1,0:T(1,128)S(1)}, s32[1,1,1,128]{3,2,1,0:T(1,128)}, u32[]{:S(2)}) copy-start(s32[1,1,1,128]{3,2,1,0:T(1,128)} %param.19) | copy-start | bytes 1540
  15.6 1.5 %collective-permute-start = (bf16[32,16,128]{2,1,0:T(8,128)(2,1)S(1)}, bf16[32,16,128]{2,1,0:T(8,128)(2,1)}, u32[]{:S(2)}, u32[]{:S(2)}) collective-permute-start(bf16[32,16,128]{2,1,0:T(8,128)(2,1)S(1)} %couple_gather.1), channel_id=1, source_target_pairs={{0,128},{128,0},{1,129},{129,1},{2,130},{130,2},{3,131},{131,3},{4... | collective-permute-start | bytes 393224 | tf_op jit(solution)/shard_map/ppermute | solution.py:427
  20.3 14.8 %all-to-all-start.1 = ((bf16[32,16,128]{2,1,0:T(8,128)(2,1)}), bf16[32,16,128]{2,1,0:T(8,128)(2,1)S(1)}, u32[]{:S(2)}, u32[]{:S(2)}) async-start(bf16[32,16,128]{2,1,0:T(8,128)(2,1)} %collective-permute-done), calls=%async_computation.1 | async-start | bytes 262144 | tf_op jit(solution)/shard_map/all_to_all | solution.py:431
  28.1 4.1 %collective-permute-start.1 = (bf16[2,24,384]{2,1,0:T(8,128)(2,1)S(1)}, bf16[2,24,384]{2,1,0:T(8,128)(2,1)S(1)}, u32[]{:S(2)}, u32[]{:S(2)}) collective-permute-start(bf16[2,24,384]{2,1,0:T(8,128)(2,1)S(1)} %fusion), channel_id=1, source_target_pairs={{0,1},{1,0},{2,3},{3,2},{4,5},{5,4},{6,7},{7,6},{8,9},{9,8},{10,11... | collective-permute-start | bytes 110600 | tf_op jit(solution)/shard_map/ppermute | solution.py:430
  29.8 1.0 %copy-start.8 = (bf16[384,512]{1,0:T(8,128)(2,1)S(1)}, bf16[384,512]{1,0:T(8,128)(2,1)}, u32[]{:S(2)}) copy-start(bf16[384,512]{1,0:T(8,128)(2,1)} %constant.34.clone.ahead_ref) | copy-start | bytes 1179652
  30.1 1.0 %copy-start.7 = (bf16[256,768]{1,0:T(8,128)(2,1)S(1)}, bf16[256,768]{1,0:T(8,128)(2,1)}, u32[]{:S(2)}) copy-start(bf16[256,768]{1,0:T(8,128)(2,1)} %constant.35.clone.back_ref) | copy-start | bytes 1179652
  30.3 0.9 %copy-start.9 = (f32[2,8,384]{2,1,0:T(8,128)S(1)}, f32[2,8,384]{2,1,0:T(8,128)}, u32[]{:S(2)}) copy-start(f32[2,8,384]{2,1,0:T(8,128)} %constant.36.clone.twiddle_ref) | copy-start | bytes 73732
  38.1 7.8 %collective-permute-start.2 = (bf16[24,384]{1,0:T(8,128)(2,1)S(1)}, bf16[24,384]{1,0:T(8,128)(2,1)S(1)}, u32[]{:S(2)}, u32[]{:S(2)}) collective-permute-start(bf16[24,384]{1,0:T(8,128)(2,1)S(1)} %get-tuple-element.28), channel_id=1, source_target_pairs={{8,16},{16,8},{24,32},{32,24},{40,48},{48,40},{56,64},{64,56},{72,... | collective-permute-start | bytes 55304 | tf_op jit(solution)/shard_map/ppermute | solution.py:470
  42.1 3.8 %collective-permute-start.3 = (bf16[24,384]{1,0:T(8,128)(2,1)S(1)}, bf16[24,384]{1,0:T(8,128)(2,1)S(1)}, u32[]{:S(2)}, u32[]{:S(2)}) collective-permute-start(bf16[24,384]{1,0:T(8,128)(2,1)S(1)} %get-tuple-element.29), channel_id=1, source_target_pairs={{0,8},{8,0},{16,24},{24,16},{32,40},{40,32},{48,56},{56,48},{64,72... | collective-permute-start | bytes 55304 | tf_op jit(solution)/shard_map/ppermute | solution.py:471
  46.4 17.4 %copy-start.4 = (f32[1,24,384]{2,1,0:T(8,128)S(1)}, f32[1,24,384]{2,1,0:T(8,128)}, u32[]{:S(2)}) copy-start(f32[1,24,384]{2,1,0:T(8,128)} %rate_ref.1) | copy-start | bytes 110596
  46.4 17.4 %copy-start.5 = (s32[24,384]{1,0:T(8,128)S(1)}, s32[24,384]{1,0:T(8,128)}, u32[]{:S(2)}) copy-start(s32[24,384]{1,0:T(8,128)} %land_ref.1) | copy-start | bytes 110596

commit v9 on v8

--- a/solution.py
+++ b/solution.py
@@ -133,7 +133,7 @@
 
 
 def scatter_kernel(
-    split, arrived_ref, circle_ref, line_ref, lane_ref, state_ref, mate_ref, part_ref, x_ref, first_ref, second_ref, value_ref, acc_ref
+    split, arrived_ref, circle_ref, line_ref, lane_ref, state_ref, mate_ref, part_ref, x_ref, first_ref, second_ref, value_ref
 ):
     senders, each, slots = arrived_ref.shape
     blocks = circle_ref.shape[0]
@@ -143,39 +143,36 @@
     lines = rows * cols // LANES
     for s in range(senders):
         value_ref[s] = arrived_ref[s].astype(F32)
-    acc_ref[...] = jnp.zeros_like(acc_ref)
     spot = lax.broadcasted_iota(jnp.int32, (lines, slots), 0)
-
-    def step(pair, carry):
-        for h in range(blocks):
+    for h in range(blocks):
+        total = None
+        for pair in range(0, groups, 2):
             spread, pick = [], []
-            for g in (2 * pair, 2 * pair + 1):
+            for g in (pair, pair + 1):
                 for v in range(split):
                     at = v * groups + g
-                    mask = spot == line_ref[h, pl.ds(at, 1), :]
+                    mask = spot == line_ref[h, at : at + 1, :]
                     vals = [
                         jnp.where(mask, value_ref[g * split + v, c * blocks + h : c * blocks + h + 1, :], 0.0)
                         for c in range(fields)
                     ]
                     spread.append(jnp.concatenate(vals, axis=0).astype(BF))
-                    pick.append(one_hot(LANES, lane_ref[h, pl.ds(at, 1), :]))
-            acc_ref[h] += lax.dot_general(
+                    pick.append(one_hot(LANES, lane_ref[h, at : at + 1, :]))
+            part = lax.dot_general(
                 jnp.concatenate(spread, axis=1),
                 jnp.concatenate(pick, axis=1),
                 (((1,), (1,)), ((), ())),
                 preferred_element_type=F32,
             )
-        return carry
-
-    lax.fori_loop(0, groups // 2, step, 0, unroll=4)
+            total = part if total is None else total + part
+        for c in range(fields):
+            x = untile(total[c * lines : (c + 1) * lines], rows)
+            part_ref[c, h] = x
+            x_ref[c, h] = x
     gv = lax.axis_index("gv")
     own = lax.axis_index("gu") * split + gv
     first_level = gv * fields
     for c in range(fields):
-        for h in range(blocks):
-            x = untile(acc_ref[h, c * lines : (c + 1) * lines], rows)
-            part_ref[c, h] = x
-            x_ref[c, h] = x
         x_ref[c, own] += state_ref[0, first_level + c]
         x_ref[c, own + 1 - 2 * gv] += mate_ref[c].astype(F32)
     tops, bottoms = [], []
@@ -459,7 +456,6 @@
         out_specs=(VMEM,) * 4,
         scratch_shapes=[
             pltpu.VMEM((senders, each * blocks, slots), F32),
-            pltpu.VMEM((blocks, each * cell_rows, LANES), F32),
         ],
         compiler_params=PARAMS,
         cost_estimate=cost(4),

time: 65.1 us -> 64.8 us (level)
  no operation moved by 1% of the time
where the time goes in v9:
time: 64.8 us; the launch traced here: 64.4 us
  starting transfers between devices  21.9 us (34%)
  blocking collectives  17.3 us (27%)
  Pallas kernels  12.2 us (19%)
  waiting for transfers between devices  10.6 us (16%)
  local copies, waits for them, and re-layouts  2.19 us (3%)
    all_to_all x1, blocking collectives, local(): lax.all_to_all(incr, ('gu', 'gv'), split_axis=0, concat_axis=0, tiled=True)  17.3 us
    all_to_all x1, starting transfers between devices, local(): lax.all_to_all(early, ('gu', 'gv'), split_axis=0, concat_axis=0, tiled=True)  8.61 us
    all_to_all x1, starting transfers between devices, local(): lax.all_to_all(crossed, ('gx', 'gv'), split_axis=0, concat_axis=0, tiled=...  7.62 us
    pallas_call x1, Pallas kernels, local(): pl.pallas_call(functools.partial(gather_kernel, split, blocks), out_shape...  4.02 us
    ppermute x1, starting transfers between devices, local(): second = lax.ppermute(second, 'gx', cross)  3.97 us
    all_to_all x1, waiting for transfers between devices, local(): lax.all_to_all(early, ('gu', 'gv'), split_axis=0, concat_axis=0, tiled=True)  3.26 us
    all_to_all x1, waiting for transfers between devices, local(): lax.all_to_all(crossed, ('gx', 'gv'), split_axis=0, concat_axis=0, tiled=...  2.97 us
    pallas_call x1, Pallas kernels, local(): pl.pallas_call(functools.partial(scatter_kernel, split), out_shape=(part_...  2.65 us
  transfers between devices with their start and end apart: 6, of which 6 were waited for; matrix products, arithmetic and copies ran while one was open for 1% of the time, Pallas kernels for 9%

profile of v9, /device:TPU:2, one launch (start us, length us, event | category | flops | bytes accessed | tf_op | source)
XLA Modules:
  0.0 64.4 jit_solution(10692649131776191908)
XLA Ops:
  0.0 0.0 copy-start
  0.0 0.0 copy-start.2
  0.0 0.0 copy-start.3
  0.0 0.0 copy-start.10
  0.0 2.3 %early_pack.1 = bf16[8,68,128]{2,1,0:T(8,128)(2,1)} custom-call(f32[1,8,24,384]{3,2,1,0:T(8,128)} %state_ref.3, s32[16,8,128]{2,1,0:T(8,128)} %bitcast.13), custom_call_target="tpu_custom_call" | custom-call | flops 1000000000 | bytes 3000000 | tf_op jit(solution)/shard_map/early_pack/pallas_call | solution.py:393
  2.3 0.0 copy-start.1
  2.3 8.6 %all-to-all-start = ((bf16[8,68,128]{2,1,0:T(8,128)(2,1)}), bf16[8,68,128]{2,1,0:T(8,128)(2,1)S(1)}, u32[]{:S(2)}, u32[]{:S(2)}) async-start(bf16[8,68,128]{2,1,0:T(8,128)(2,1)} %early_pack.1), calls=%async_computation | async-start | bytes 294912 | tf_op jit(solution)/shard_map/all_to_all | solution.py:408
  10.9 0.0 copy-start.6
  10.9 0.0 copy-done.2
  10.9 0.0 copy-done.3
  11.0 0.0 copy-done.10
  11.0 0.0 copy-done.1
  11.0 0.6 copy-done.6
  11.6 4.0 %couple_gather.1 = bf16[32,16,128]{2,1,0:T(8,128)(2,1)S(1)} custom-call(f32[1,8,24,384]{3,2,1,0:T(8,128)S(1)} %copy-done.1, s32[128,128]{1,0:T(8,128)S(1)} %bitcast.10, f32[128,128]{1,0:T(8,128)S(1)} %bitcast.11, bf16[32,256]{1,0:T(8,128)(2,1)S(1)} %copy-done.10, s32[1,128]{1,0:T(1,128)S(1)} %bitcast.12), custom_call_target="tpu_custom_call" | custom-call | flops 4000000000 | bytes 12000000 | tf_op jit(solution)/shard_map/couple_gather/pallas_call | solution.py:414
  15.6 0.0 collective-permute-start
  15.6 1.4 %collective-permute-done = bf16[32,16,128]{2,1,0:T(8,128)(2,1)} collective-permute-done((bf16[32,16,128]{2,1,0:T(8,128)(2,1)S(1)}, bf16[32,16,128]{2,1,0:T(8,128)(2,1)}, u32[]{:S(2)}, u32[]{:S(2)}) %collective-permute-start) | collective-permute-done | bytes 131104 | tf_op jit(solution)/shard_map/ppermute | solution.py:424
  17.1 3.3 %all-to-all-done.early_ref = bf16[8,68,128]{2,1,0:T(8,128)(2,1)S(1)} async-done(((bf16[8,68,128]{2,1,0:T(8,128)(2,1)}), bf16[8,68,128]{2,1,0:T(8,128)(2,1)S(1)}, u32[]{:S(2)}, u32[]{:S(2)}) %all-to-all-start) | async-done | bytes 139296 | tf_op jit(solution)/shard_map/all_to_all | solution.py:408
  20.3 7.6 %all-to-all-start.1 = ((bf16[32,16,128]{2,1,0:T(8,128)(2,1)}), bf16[32,16,128]{2,1,0:T(8,128)(2,1)S(1)}, u32[]{:S(2)}, u32[]{:S(2)}) async-start(bf16[32,16,128]{2,1,0:T(8,128)(2,1)} %collective-permute-done), calls=%async_computation.1 | async-start | bytes 262144 | tf_op jit(solution)/shard_map/all_to_all | solution.py:428
  28.0 0.0 copy-done
  28.1 1.6 %collective-permute-start.1 = (bf16[2,24,384]{2,1,0:T(8,128)(2,1)S(1)}, bf16[2,24,384]{2,1,0:T(8,128)(2,1)S(1)}, u32[]{:S(2)}, u32[]{:S(2)}) collective-permute-start(bf16[2,24,384]{2,1,0:T(8,128)(2,1)S(1)} %fusion), channel_id=1, source_target_pairs={{0,1},{1,0},{2,3},{3,2},{4,5},{5,4},{6,7},{7,6},{8,9},{9,8},{10,11... | collective-permute-start | bytes 110600 | tf_op jit(solution)/shard_map/ppermute | solution.py:427
  29.6 0.1 concatenate.9
  29.7 0.1 copy.14
  29.8 0.0 copy-start.8
  29.8 0.2 concatenate.8
  30.1 0.0 copy-start.7
  30.1 0.2 copy.13
  30.3 0.0 copy-start.9
  30.3 0.5 copy-done.8
  30.9 0.3 copy-done.7
  31.1 0.0 copy-done.9
  31.1 0.7 %circle_filter.1 = (f32[8,16,384]{2,1,0:T(8,128)S(1)}, f32[8,16,384]{2,1,0:T(8,128)S(1)}, s32[8,32,128]{2,1,0:T(8,128)S(1)}, s32[8,32,128]{2,1,0:T(8,128)S(1)}) custom-call(bf16[8,68,128]{2,1,0:T(8,128)(2,1)S(1)} %all-to-all-done.early_ref, f32[2,8,256]{2,1,0:T(8,128)S(1)} %slice_bitcast_fusion.resp_ref, bf16[384,512]{1,0:T(8,128)(2,1)S(1)} %copy-done.8, ...), custom_call_target="tpu_custom_call" | custom-call | flops 2000000000 | bytes 6000000 | tf_op jit(solution)/shard_map/circle_filter/pallas_call | solution.py:441
  31.9 0.3 collective-permute-done.1.mate_ref
  32.2 3.0 %all-to-all-done.1.arrived_ref = bf16[32,16,128]{2,1,0:T(8,128)(2,1)S(1)} async-done(((bf16[32,16,128]{2,1,0:T(8,128)(2,1)}), bf16[32,16,128]{2,1,0:T(8,128)(2,1)S(1)}, u32[]{:S(2)}, u32[]{:S(2)}) %all-to-all-start.1) | async-done | bytes 131104 | tf_op jit(solution)/shard_map/all_to_all | solution.py:428
  35.1 2.6 %couple_scatter.1 = (f32[2,8,24,384]{3,2,1,0:T(8,128)S(1)}, f32[2,8,24,384]{3,2,1,0:T(8,128)S(1)}, bf16[24,384]{1,0:T(8,128)(2,1)S(1)}, bf16[24,384]{1,0:T(8,128)(2,1)S(1)}) custom-call(bf16[32,16,128]{2,1,0:T(8,128)(2,1)S(1)} %all-to-all-done.1.arrived_ref, f32[8,16,384]{2,1,0:T(8,128)S(1)} %get-tuple-element.24.circle_ref, ...), custom_call_target="tpu_custom_call" | custom-call | flops 4000000000 | bytes 12000000 | tf_op jit(solution)/shard_map/couple_scatter/pallas_call | solution.py:452
  37.8 4.0 %collective-permute-start.2 = (bf16[24,384]{1,0:T(8,128)(2,1)S(1)}, bf16[24,384]{1,0:T(8,128)(2,1)S(1)}, u32[]{:S(2)}, u32[]{:S(2)}) collective-permute-start(bf16[24,384]{1,0:T(8,128)(2,1)S(1)} %get-tuple-element.28), channel_id=1, source_target_pairs={{8,16},{16,8},{24,32},{32,24},{40,48},{48,40},{56,64},{64,56},{72,... | collective-permute-start | bytes 55304 | tf_op jit(solution)/shard_map/ppermute | solution.py:466
  41.8 0.1 collective-permute-start.3
  41.9 1.1 %part_filter.1.part_ref = bf16[8,2,24,384]{3,2,1,0:T(8,128)(2,1)S(1)} custom-call(f32[2,8,24,384]{3,2,1,0:T(8,128)S(1)} %get-tuple-element.30.part_ref, f32[2,8,24,384]{3,2,1,0:T(8,128)S(1)} %get-tuple-element.31.x_ref, f32[3,2,8,256]{3,2,1,0:T(8,128)S(1)} %pad.4.resp_ref, bf16[384,512]{1,0:T(8,128)(2,1)S(1)} %copy-done.8, bf16[256,768]{1,0:T(8,128)(2,1)S(1)} %copy-done.7, ...), custom_call_target="tpu_custom_call" | custom-call | flops 3000000000 | bytes 9000000 | tf_op jit(solution)/shard_map/part_filter/pallas_call | solution.py:468
  43.0 2.6 %collective-permute-done.2.second_ref = bf16[24,384]{1,0:T(8,128)(2,1)S(1)} collective-permute-done((bf16[24,384]{1,0:T(8,128)(2,1)S(1)}, bf16[24,384]{1,0:T(8,128)(2,1)S(1)}, u32[]{:S(2)}, u32[]{:S(2)}) %collective-permute-start.2) | collective-permute-done | bytes 18464 | tf_op jit(solution)/shard_map/ppermute | solution.py:466
  45.6 0.1 collective-permute-done.3.first_ref
  45.6 0.5 edge_filter.1
  46.1 0.0 copy-start.4
  46.2 0.0 copy-start.5
  46.2 17.3 %all_to_all.15.back_ref = bf16[8,66,384]{2,1,0:T(8,128)(2,1)S(1)} all-to-all(bf16[8,66,384]{2,1,0:T(8,128)(2,1)S(1)} %edge_filter.1), channel_id=1, replica_groups=mesh['comp'=2,'gx'=16,'gu'=4,'gv'=2] {'gu','gv'}, dimensions={0} | all-to-all | bytes 811008 | tf_op jit(solution)/shard_map/all_to_all | solution.py:486
  63.5 0.0 copy-done.4
  63.5 0.0 copy-done.5
  63.5 0.9 %final_step.1 = f32[1,8,24,384]{3,2,1,0:T(8,128)} custom-call(f32[1,8,24,384]{3,2,1,0:T(8,128)S(1)} %copy-done.1, bf16[8,66,384]{2,1,0:T(8,128)(2,1)S(1)} %all_to_all.15.back_ref, f32[1,24,384]{2,1,0:T(8,128)S(1)} %copy-done.4, s32[24,384]{1,0:T(8,128)S(1)} %copy-done.5), custom_call_target="tpu_custom_call" | custom-call | flops 1000000000 | bytes 3000000 | tf_op jit(solution)/shard_map/final_step/pallas_call | solution.py:487
  (6 shorter events, 0.1 us)
Async XLA Ops:
  0.0 28.0 %copy-start = (f32[1,8,3072]{2,1,0:T(8,128)S(1)}, f32[1,8,3072]{2,1,0:T(8,128)}, u32[]{:S(2)}) copy-start(f32[1,8,3072]{2,1,0:T(8,128)} %param.13) | copy-start | bytes 294916
  0.0 10.9 %copy-start.2 = (s32[1,1,1,128,128]{4,3,2,1,0:T(8,128)S(1)}, s32[1,1,1,128,128]{4,3,2,1,0:T(8,128)}, u32[]{:S(2)}) copy-start(s32[1,1,1,128,128]{4,3,2,1,0:T(8,128)} %param.16) | copy-start | bytes 196612
  0.0 10.9 %copy-start.3 = (f32[1,1,1,128,128]{4,3,2,1,0:T(8,128)S(1)}, f32[1,1,1,128,128]{4,3,2,1,0:T(8,128)}, u32[]{:S(2)}) copy-start(f32[1,1,1,128,128]{4,3,2,1,0:T(8,128)} %param.18) | copy-start | bytes 196612
  0.0 10.9 %copy-start.10 = (bf16[32,256]{1,0:T(8,128)(2,1)S(1)}, bf16[32,256]{1,0:T(8,128)(2,1)}, u32[]{:S(2)}) copy-start(bf16[32,256]{1,0:T(8,128)(2,1)} %constant.33.clone.pick_ref) | copy-start | bytes 49156
  2.3 8.7 %copy-start.1 = (f32[1,8,24,384]{3,2,1,0:T(8,128)S(1)}, f32[1,8,24,384]{3,2,1,0:T(8,128)}, u32[]{:S(2)}) copy-start(f32[1,8,24,384]{3,2,1,0:T(8,128)} %state_ref.3) | copy-start | bytes 884740
  2.3 18.0 %all-to-all-start = ((bf16[8,68,128]{2,1,0:T(8,128)(2,1)}), bf16[8,68,128]{2,1,0:T(8,128)(2,1)S(1)}, u32[]{:S(2)}, u32[]{:S(2)}) async-start(bf16[8,68,128]{2,1,0:T(8,128)(2,1)} %early_pack.1), calls=%async_computation | async-start | bytes 294912 | tf_op jit(solution)/shard_map/all_to_all | solution.py:408
  10.9 0.7 %copy-start.6 = (s32[1,1,1,128]{3,2,1,0:T(1,128)S(1)}, s32[1,1,1,128]{3,2,1,0:T(1,128)}, u32[]{:S(2)}) copy-start(s32[1,1,1,128]{3,2,1,0:T(1,128)} %param.19) | copy-start | bytes 1540
  15.6 1.5 %collective-permute-start = (bf16[32,16,128]{2,1,0:T(8,128)(2,1)S(1)}, bf16[32,16,128]{2,1,0:T(8,128)(2,1)}, u32[]{:S(2)}, u32[]{:S(2)}) collective-permute-start(bf16[32,16,128]{2,1,0:T(8,128)(2,1)S(1)} %couple_gather.1), channel_id=1, source_target_pairs={{0,128},{128,0},{1,129},{129,1},{2,130},{130,2},{3,131},{131,3},{4... | collective-permute-start | bytes 393224 | tf_op jit(solution)/shard_map/ppermute | solution.py:424
  20.3 14.8 %all-to-all-start.1 = ((bf16[32,16,128]{2,1,0:T(8,128)(2,1)}), bf16[32,16,128]{2,1,0:T(8,128)(2,1)S(1)}, u32[]{:S(2)}, u32[]{:S(2)}) async-start(bf16[32,16,128]{2,1,0:T(8,128)(2,1)} %collective-permute-done), calls=%async_computation.1 | async-start | bytes 262144 | tf_op jit(solution)/shard_map/all_to_all | solution.py:428
  28.1 4.1 %collective-permute-start.1 = (bf16[2,24,384]{2,1,0:T(8,128)(2,1)S(1)}, bf16[2,24,384]{2,1,0:T(8,128)(2,1)S(1)}, u32[]{:S(2)}, u32[]{:S(2)}) collective-permute-start(bf16[2,24,384]{2,1,0:T(8,128)(2,1)S(1)} %fusion), channel_id=1, source_target_pairs={{0,1},{1,0},{2,3},{3,2},{4,5},{5,4},{6,7},{7,6},{8,9},{9,8},{10,11... | collective-permute-start | bytes 110600 | tf_op jit(solution)/shard_map/ppermute | solution.py:427
  29.8 1.0 %copy-start.8 = (bf16[384,512]{1,0:T(8,128)(2,1)S(1)}, bf16[384,512]{1,0:T(8,128)(2,1)}, u32[]{:S(2)}) copy-start(bf16[384,512]{1,0:T(8,128)(2,1)} %constant.34.clone.ahead_ref) | copy-start | bytes 1179652
  30.1 1.0 %copy-start.7 = (bf16[256,768]{1,0:T(8,128)(2,1)S(1)}, bf16[256,768]{1,0:T(8,128)(2,1)}, u32[]{:S(2)}) copy-start(bf16[256,768]{1,0:T(8,128)(2,1)} %constant.35.clone.back_ref) | copy-start | bytes 1179652
  30.3 0.9 %copy-start.9 = (f32[2,8,384]{2,1,0:T(8,128)S(1)}, f32[2,8,384]{2,1,0:T(8,128)}, u32[]{:S(2)}) copy-start(f32[2,8,384]{2,1,0:T(8,128)} %constant.36.clone.twiddle_ref) | copy-start | bytes 73732
  37.8 7.8 %collective-permute-start.2 = (bf16[24,384]{1,0:T(8,128)(2,1)S(1)}, bf16[24,384]{1,0:T(8,128)(2,1)S(1)}, u32[]{:S(2)}, u32[]{:S(2)}) collective-permute-start(bf16[24,384]{1,0:T(8,128)(2,1)S(1)} %get-tuple-element.28), channel_id=1, source_target_pairs={{8,16},{16,8},{24,32},{32,24},{40,48},{48,40},{56,64},{64,56},{72,... | collective-permute-start | bytes 55304 | tf_op jit(solution)/shard_map/ppermute | solution.py:466
  41.8 3.8 %collective-permute-start.3 = (bf16[24,384]{1,0:T(8,128)(2,1)S(1)}, bf16[24,384]{1,0:T(8,128)(2,1)S(1)}, u32[]{:S(2)}, u32[]{:S(2)}) collective-permute-start(bf16[24,384]{1,0:T(8,128)(2,1)S(1)} %get-tuple-element.29), channel_id=1, source_target_pairs={{0,8},{8,0},{16,24},{24,16},{32,40},{40,32},{48,56},{56,48},{64,72... | collective-permute-start | bytes 55304 | tf_op jit(solution)/shard_map/ppermute | solution.py:467
  46.1 17.4 %copy-start.4 = (f32[1,24,384]{2,1,0:T(8,128)S(1)}, f32[1,24,384]{2,1,0:T(8,128)}, u32[]{:S(2)}) copy-start(f32[1,24,384]{2,1,0:T(8,128)} %rate_ref.1) | copy-start | bytes 110596
  46.2 17.3 %copy-start.5 = (s32[24,384]{1,0:T(8,128)S(1)}, s32[24,384]{1,0:T(8,128)}, u32[]{:S(2)}) copy-start(s32[24,384]{1,0:T(8,128)} %land_ref.1) | copy-start | bytes 110596

commit v10 on v9

--- a/solution.py
+++ b/solution.py
@@ -92,12 +92,13 @@
     limit = jnp.sum(jnp.where(same, count_ref[...].astype(F32), 0.0), axis=1, keepdims=True)
     weight_ref[...] = jnp.where(slot.astype(F32) < limit, all_ref[...], 0.0)
 
-    def step(g, carry):
-        base = pl.multiple_of(g * blocks, blocks)
-        line, col = split_lines(src_ref[pl.ds(base, blocks), :], rows, cols)
-        upper = line >= half
-        line = line - jnp.where(upper, shift, 0)
-        col = col + jnp.where(upper, LANES, 0)
+    lines_all, cols_all = split_lines(src_ref[...], rows, cols)
+    upper = lines_all >= half
+    lines_all = lines_all - jnp.where(upper, shift, 0)
+    cols_all = cols_all + jnp.where(upper, LANES, 0)
+    for g in range(peers // blocks):
+        base = g * blocks
+        line, col = lines_all[base : base + blocks], cols_all[base : base + blocks]
         found = []
         for i in range(0, blocks, 2):
             pick = jnp.concatenate([one_hot(2 * LANES, col[j : j + 1]) for j in (i, i + 1)], axis=1)
@@ -107,13 +108,10 @@
                 own = jnp.where((spot == line[i + j : i + j + 1])[None], own, 0.0)
                 found.append(jnp.sum(own.reshape(fc, half // 8, 8, slots), axis=1).reshape(fc * 8, slots))
         value = jnp.dot(pick_ref[...], jnp.concatenate(found, axis=0).astype(BF), preferred_element_type=F32)
-        weight = weight_ref[pl.ds(base, blocks), :]
+        weight = weight_ref[base : base + blocks, :]
         value = value * jnp.concatenate([weight] * fc, axis=0)
         for v in range(split):
             out_ref[g * split + v] = value[v * each : (v + 1) * each].astype(BF)
-        return carry
-
-    lax.fori_loop(0, peers // blocks, step, 0, unroll=16)
 
 
 def circle_kernel(scale, early_ref, resp_ref, ahead_ref, back_ref, twiddle_ref, x_ref, incr_ref, line_ref, lane_ref):
@@ -146,9 +144,9 @@
     spot = lax.broadcasted_iota(jnp.int32, (lines, slots), 0)
     for h in range(blocks):
         total = None
-        for pair in range(0, groups, 2):
+        for four in range(0, groups, 4):
             spread, pick = [], []
-            for g in (pair, pair + 1):
+            for g in range(four, four + 4):
                 for v in range(split):
                     at = v * groups + g
                     mask = spot == line_ref[h, at : at + 1, :]

time: 64.8 us -> 64.8 us (level)
  no operation moved by 1% of the time
where the time goes in v10:
time: 64.8 us; the launch traced here: 64.4 us
  starting transfers between devices  21.9 us (34%)
  blocking collectives  17.3 us (27%)
  Pallas kernels  12.2 us (19%)
  waiting for transfers between devices  10.6 us (16%)
  local copies, waits for them, and re-layouts  2.19 us (3%)
    all_to_all x1, blocking collectives, local(): lax.all_to_all(incr, ('gu', 'gv'), split_axis=0, concat_axis=0, tiled=True)  17.3 us
    all_to_all x1, starting transfers between devices, local(): lax.all_to_all(early, ('gu', 'gv'), split_axis=0, concat_axis=0, tiled=True)  8.61 us
    all_to_all x1, starting transfers between devices, local(): lax.all_to_all(crossed, ('gx', 'gv'), split_axis=0, concat_axis=0, tiled=...  7.62 us
    pallas_call x1, Pallas kernels, local(): pl.pallas_call(functools.partial(gather_kernel, split, blocks), out_shape...  4.02 us
    ppermute x1, starting transfers between devices, local(): second = lax.ppermute(second, 'gx', cross)  3.97 us
    all_to_all x1, waiting for transfers between devices, local(): lax.all_to_all(early, ('gu', 'gv'), split_axis=0, concat_axis=0, tiled=True)  3.26 us
    all_to_all x1, waiting for transfers between devices, local(): lax.all_to_all(crossed, ('gx', 'gv'), split_axis=0, concat_axis=0, tiled=...  2.97 us
    pallas_call x1, Pallas kernels, local(): pl.pallas_call(functools.partial(scatter_kernel, split), out_shape=(part_...  2.65 us
  transfers between devices with their start and end apart: 6, of which 6 were waited for; matrix products, arithmetic and copies ran while one was open for 1% of the time, Pallas kernels for 9%

profile of v10, /device:TPU:2, one launch (start us, length us, event | category | flops | bytes accessed | tf_op | source)
XLA Modules:
  0.0 64.4 jit_solution(5545198356453487016)
XLA Ops:
  0.0 0.0 copy-start
  0.0 0.0 copy-start.2
  0.0 0.0 copy-start.3
  0.0 0.0 copy-start.10
  0.0 2.3 %early_pack.1 = bf16[8,68,128]{2,1,0:T(8,128)(2,1)} custom-call(f32[1,8,24,384]{3,2,1,0:T(8,128)} %state_ref.3, s32[16,8,128]{2,1,0:T(8,128)} %bitcast.13), custom_call_target="tpu_custom_call" | custom-call | flops 1000000000 | bytes 3000000 | tf_op jit(solution)/shard_map/early_pack/pallas_call | solution.py:391
  2.3 0.0 copy-start.1
  2.3 8.6 %all-to-all-start = ((bf16[8,68,128]{2,1,0:T(8,128)(2,1)}), bf16[8,68,128]{2,1,0:T(8,128)(2,1)S(1)}, u32[]{:S(2)}, u32[]{:S(2)}) async-start(bf16[8,68,128]{2,1,0:T(8,128)(2,1)} %early_pack.1), calls=%async_computation | async-start | bytes 294912 | tf_op jit(solution)/shard_map/all_to_all | solution.py:406
  10.9 0.0 copy-start.6
  10.9 0.0 copy-done.2
  10.9 0.0 copy-done.3
  11.0 0.0 copy-done.10
  11.0 0.0 copy-done.1
  11.0 0.6 copy-done.6
  11.6 4.0 %couple_gather.1 = bf16[32,16,128]{2,1,0:T(8,128)(2,1)S(1)} custom-call(f32[1,8,24,384]{3,2,1,0:T(8,128)S(1)} %copy-done.1, s32[128,128]{1,0:T(8,128)S(1)} %bitcast.10, f32[128,128]{1,0:T(8,128)S(1)} %bitcast.11, bf16[32,256]{1,0:T(8,128)(2,1)S(1)} %copy-done.10, s32[1,128]{1,0:T(1,128)S(1)} %bitcast.12), custom_call_target="tpu_custom_call" | custom-call | flops 4000000000 | bytes 12000000 | tf_op jit(solution)/shard_map/couple_gather/pallas_call | solution.py:412
  15.6 0.0 collective-permute-start
  15.6 1.4 %collective-permute-done = bf16[32,16,128]{2,1,0:T(8,128)(2,1)} collective-permute-done((bf16[32,16,128]{2,1,0:T(8,128)(2,1)S(1)}, bf16[32,16,128]{2,1,0:T(8,128)(2,1)}, u32[]{:S(2)}, u32[]{:S(2)}) %collective-permute-start) | collective-permute-done | bytes 131104 | tf_op jit(solution)/shard_map/ppermute | solution.py:422
  17.1 3.3 %all-to-all-done.early_ref = bf16[8,68,128]{2,1,0:T(8,128)(2,1)S(1)} async-done(((bf16[8,68,128]{2,1,0:T(8,128)(2,1)}), bf16[8,68,128]{2,1,0:T(8,128)(2,1)S(1)}, u32[]{:S(2)}, u32[]{:S(2)}) %all-to-all-start) | async-done | bytes 139296 | tf_op jit(solution)/shard_map/all_to_all | solution.py:406
  20.3 7.6 %all-to-all-start.1 = ((bf16[32,16,128]{2,1,0:T(8,128)(2,1)}), bf16[32,16,128]{2,1,0:T(8,128)(2,1)S(1)}, u32[]{:S(2)}, u32[]{:S(2)}) async-start(bf16[32,16,128]{2,1,0:T(8,128)(2,1)} %collective-permute-done), calls=%async_computation.1 | async-start | bytes 262144 | tf_op jit(solution)/shard_map/all_to_all | solution.py:426
  28.0 0.0 copy-done
  28.1 1.6 %collective-permute-start.1 = (bf16[2,24,384]{2,1,0:T(8,128)(2,1)S(1)}, bf16[2,24,384]{2,1,0:T(8,128)(2,1)S(1)}, u32[]{:S(2)}, u32[]{:S(2)}) collective-permute-start(bf16[2,24,384]{2,1,0:T(8,128)(2,1)S(1)} %fusion), channel_id=1, source_target_pairs={{0,1},{1,0},{2,3},{3,2},{4,5},{5,4},{6,7},{7,6},{8,9},{9,8},{10,11... | collective-permute-start | bytes 110600 | tf_op jit(solution)/shard_map/ppermute | solution.py:425
  29.6 0.1 concatenate.9
  29.7 0.1 copy.14
  29.8 0.0 copy-start.8
  29.8 0.2 concatenate.8
  30.1 0.0 copy-start.7
  30.1 0.2 copy.13
  30.3 0.0 copy-start.9
  30.3 0.5 copy-done.8
  30.9 0.3 copy-done.7
  31.1 0.0 copy-done.9
  31.1 0.7 %circle_filter.1 = (f32[8,16,384]{2,1,0:T(8,128)S(1)}, f32[8,16,384]{2,1,0:T(8,128)S(1)}, s32[8,32,128]{2,1,0:T(8,128)S(1)}, s32[8,32,128]{2,1,0:T(8,128)S(1)}) custom-call(bf16[8,68,128]{2,1,0:T(8,128)(2,1)S(1)} %all-to-all-done.early_ref, f32[2,8,256]{2,1,0:T(8,128)S(1)} %slice_bitcast_fusion.resp_ref, bf16[384,512]{1,0:T(8,128)(2,1)S(1)} %copy-done.8, ...), custom_call_target="tpu_custom_call" | custom-call | flops 2000000000 | bytes 6000000 | tf_op jit(solution)/shard_map/circle_filter/pallas_call | solution.py:439
  31.9 0.3 collective-permute-done.1.mate_ref
  32.2 3.0 %all-to-all-done.1.arrived_ref = bf16[32,16,128]{2,1,0:T(8,128)(2,1)S(1)} async-done(((bf16[32,16,128]{2,1,0:T(8,128)(2,1)}), bf16[32,16,128]{2,1,0:T(8,128)(2,1)S(1)}, u32[]{:S(2)}, u32[]{:S(2)}) %all-to-all-start.1) | async-done | bytes 131104 | tf_op jit(solution)/shard_map/all_to_all | solution.py:426
  35.1 2.6 %couple_scatter.1 = (f32[2,8,24,384]{3,2,1,0:T(8,128)S(1)}, f32[2,8,24,384]{3,2,1,0:T(8,128)S(1)}, bf16[24,384]{1,0:T(8,128)(2,1)S(1)}, bf16[24,384]{1,0:T(8,128)(2,1)S(1)}) custom-call(bf16[32,16,128]{2,1,0:T(8,128)(2,1)S(1)} %all-to-all-done.1.arrived_ref, f32[8,16,384]{2,1,0:T(8,128)S(1)} %get-tuple-element.24.circle_ref, ...), custom_call_target="tpu_custom_call" | custom-call | flops 4000000000 | bytes 12000000 | tf_op jit(solution)/shard_map/couple_scatter/pallas_call | solution.py:450
  37.8 4.0 %collective-permute-start.2 = (bf16[24,384]{1,0:T(8,128)(2,1)S(1)}, bf16[24,384]{1,0:T(8,128)(2,1)S(1)}, u32[]{:S(2)}, u32[]{:S(2)}) collective-permute-start(bf16[24,384]{1,0:T(8,128)(2,1)S(1)} %get-tuple-element.28), channel_id=1, source_target_pairs={{8,16},{16,8},{24,32},{32,24},{40,48},{48,40},{56,64},{64,56},{72,... | collective-permute-start | bytes 55304 | tf_op jit(solution)/shard_map/ppermute | solution.py:464
  41.8 0.1 collective-permute-start.3
  41.9 1.1 %part_filter.1.part_ref = bf16[8,2,24,384]{3,2,1,0:T(8,128)(2,1)S(1)} custom-call(f32[2,8,24,384]{3,2,1,0:T(8,128)S(1)} %get-tuple-element.30.part_ref, f32[2,8,24,384]{3,2,1,0:T(8,128)S(1)} %get-tuple-element.31.x_ref, f32[3,2,8,256]{3,2,1,0:T(8,128)S(1)} %pad.4.resp_ref, bf16[384,512]{1,0:T(8,128)(2,1)S(1)} %copy-done.8, bf16[256,768]{1,0:T(8,128)(2,1)S(1)} %copy-done.7, ...), custom_call_target="tpu_custom_call" | custom-call | flops 3000000000 | bytes 9000000 | tf_op jit(solution)/shard_map/part_filter/pallas_call | solution.py:466
  43.0 2.6 %collective-permute-done.2.second_ref = bf16[24,384]{1,0:T(8,128)(2,1)S(1)} collective-permute-done((bf16[24,384]{1,0:T(8,128)(2,1)S(1)}, bf16[24,384]{1,0:T(8,128)(2,1)S(1)}, u32[]{:S(2)}, u32[]{:S(2)}) %collective-permute-start.2) | collective-permute-done | bytes 18464 | tf_op jit(solution)/shard_map/ppermute | solution.py:464
  45.6 0.1 collective-permute-done.3.first_ref
  45.6 0.5 edge_filter.1
  46.1 0.0 copy-start.4
  46.2 0.0 copy-start.5
  46.2 17.3 %all_to_all.15.back_ref = bf16[8,66,384]{2,1,0:T(8,128)(2,1)S(1)} all-to-all(bf16[8,66,384]{2,1,0:T(8,128)(2,1)S(1)} %edge_filter.1), channel_id=1, replica_groups=mesh['comp'=2,'gx'=16,'gu'=4,'gv'=2] {'gu','gv'}, dimensions={0} | all-to-all | bytes 811008 | tf_op jit(solution)/shard_map/all_to_all | solution.py:484
  63.5 0.0 copy-done.4
  63.5 0.0 copy-done.5
  63.5 0.9 %final_step.1 = f32[1,8,24,384]{3,2,1,0:T(8,128)} custom-call(f32[1,8,24,384]{3,2,1,0:T(8,128)S(1)} %copy-done.1, bf16[8,66,384]{2,1,0:T(8,128)(2,1)S(1)} %all_to_all.15.back_ref, f32[1,24,384]{2,1,0:T(8,128)S(1)} %copy-done.4, s32[24,384]{1,0:T(8,128)S(1)} %copy-done.5), custom_call_target="tpu_custom_call" | custom-call | flops 1000000000 | bytes 3000000 | tf_op jit(solution)/shard_map/final_step/pallas_call | solution.py:485
  (6 shorter events, 0.1 us)
Async XLA Ops:
  0.0 28.0 %copy-start = (f32[1,8,3072]{2,1,0:T(8,128)S(1)}, f32[1,8,3072]{2,1,0:T(8,128)}, u32[]{:S(2)}) copy-start(f32[1,8,3072]{2,1,0:T(8,128)} %param.13) | copy-start | bytes 294916
  0.0 10.9 %copy-start.2 = (s32[1,1,1,128,128]{4,3,2,1,0:T(8,128)S(1)}, s32[1,1,1,128,128]{4,3,2,1,0:T(8,128)}, u32[]{:S(2)}) copy-start(s32[1,1,1,128,128]{4,3,2,1,0:T(8,128)} %param.16) | copy-start | bytes 196612
  0.0 10.9 %copy-start.3 = (f32[1,1,1,128,128]{4,3,2,1,0:T(8,128)S(1)}, f32[1,1,1,128,128]{4,3,2,1,0:T(8,128)}, u32[]{:S(2)}) copy-start(f32[1,1,1,128,128]{4,3,2,1,0:T(8,128)} %param.18) | copy-start | bytes 196612
  0.0 10.9 %copy-start.10 = (bf16[32,256]{1,0:T(8,128)(2,1)S(1)}, bf16[32,256]{1,0:T(8,128)(2,1)}, u32[]{:S(2)}) copy-start(bf16[32,256]{1,0:T(8,128)(2,1)} %constant.33.clone.pick_ref) | copy-start | bytes 49156
  2.3 8.7 %copy-start.1 = (f32[1,8,24,384]{3,2,1,0:T(8,128)S(1)}, f32[1,8,24,384]{3,2,1,0:T(8,128)}, u32[]{:S(2)}) copy-start(f32[1,8,24,384]{3,2,1,0:T(8,128)} %state_ref.3) | copy-start | bytes 884740
  2.3 18.0 %all-to-all-start = ((bf16[8,68,128]{2,1,0:T(8,128)(2,1)}), bf16[8,68,128]{2,1,0:T(8,128)(2,1)S(1)}, u32[]{:S(2)}, u32[]{:S(2)}) async-start(bf16[8,68,128]{2,1,0:T(8,128)(2,1)} %early_pack.1), calls=%async_computation | async-start | bytes 294912 | tf_op jit(solution)/shard_map/all_to_all | solution.py:406
  10.9 0.7 %copy-start.6 = (s32[1,1,1,128]{3,2,1,0:T(1,128)S(1)}, s32[1,1,1,128]{3,2,1,0:T(1,128)}, u32[]{:S(2)}) copy-start(s32[1,1,1,128]{3,2,1,0:T(1,128)} %param.19) | copy-start | bytes 1540
  15.6 1.5 %collective-permute-start = (bf16[32,16,128]{2,1,0:T(8,128)(2,1)S(1)}, bf16[32,16,128]{2,1,0:T(8,128)(2,1)}, u32[]{:S(2)}, u32[]{:S(2)}) collective-permute-start(bf16[32,16,128]{2,1,0:T(8,128)(2,1)S(1)} %couple_gather.1), channel_id=1, source_target_pairs={{0,128},{128,0},{1,129},{129,1},{2,130},{130,2},{3,131},{131,3},{4... | collective-permute-start | bytes 393224 | tf_op jit(solution)/shard_map/ppermute | solution.py:422
  20.3 14.8 %all-to-all-start.1 = ((bf16[32,16,128]{2,1,0:T(8,128)(2,1)}), bf16[32,16,128]{2,1,0:T(8,128)(2,1)S(1)}, u32[]{:S(2)}, u32[]{:S(2)}) async-start(bf16[32,16,128]{2,1,0:T(8,128)(2,1)} %collective-permute-done), calls=%async_computation.1 | async-start | bytes 262144 | tf_op jit(solution)/shard_map/all_to_all | solution.py:426
  28.1 4.1 %collective-permute-start.1 = (bf16[2,24,384]{2,1,0:T(8,128)(2,1)S(1)}, bf16[2,24,384]{2,1,0:T(8,128)(2,1)S(1)}, u32[]{:S(2)}, u32[]{:S(2)}) collective-permute-start(bf16[2,24,384]{2,1,0:T(8,128)(2,1)S(1)} %fusion), channel_id=1, source_target_pairs={{0,1},{1,0},{2,3},{3,2},{4,5},{5,4},{6,7},{7,6},{8,9},{9,8},{10,11... | collective-permute-start | bytes 110600 | tf_op jit(solution)/shard_map/ppermute | solution.py:425
  29.8 1.0 %copy-start.8 = (bf16[384,512]{1,0:T(8,128)(2,1)S(1)}, bf16[384,512]{1,0:T(8,128)(2,1)}, u32[]{:S(2)}) copy-start(bf16[384,512]{1,0:T(8,128)(2,1)} %constant.34.clone.ahead_ref) | copy-start | bytes 1179652
  30.1 1.0 %copy-start.7 = (bf16[256,768]{1,0:T(8,128)(2,1)S(1)}, bf16[256,768]{1,0:T(8,128)(2,1)}, u32[]{:S(2)}) copy-start(bf16[256,768]{1,0:T(8,128)(2,1)} %constant.35.clone.back_ref) | copy-start | bytes 1179652
  30.3 0.9 %copy-start.9 = (f32[2,8,384]{2,1,0:T(8,128)S(1)}, f32[2,8,384]{2,1,0:T(8,128)}, u32[]{:S(2)}) copy-start(f32[2,8,384]{2,1,0:T(8,128)} %constant.36.clone.twiddle_ref) | copy-start | bytes 73732
  37.8 7.8 %collective-permute-start.2 = (bf16[24,384]{1,0:T(8,128)(2,1)S(1)}, bf16[24,384]{1,0:T(8,128)(2,1)S(1)}, u32[]{:S(2)}, u32[]{:S(2)}) collective-permute-start(bf16[24,384]{1,0:T(8,128)(2,1)S(1)} %get-tuple-element.28), channel_id=1, source_target_pairs={{8,16},{16,8},{24,32},{32,24},{40,48},{48,40},{56,64},{64,56},{72,... | collective-permute-start | bytes 55304 | tf_op jit(solution)/shard_map/ppermute | solution.py:464
  41.8 3.8 %collective-permute-start.3 = (bf16[24,384]{1,0:T(8,128)(2,1)S(1)}, bf16[24,384]{1,0:T(8,128)(2,1)S(1)}, u32[]{:S(2)}, u32[]{:S(2)}) collective-permute-start(bf16[24,384]{1,0:T(8,128)(2,1)S(1)} %get-tuple-element.29), channel_id=1, source_target_pairs={{0,8},{8,0},{16,24},{24,16},{32,40},{40,32},{48,56},{56,48},{64,72... | collective-permute-start | bytes 55304 | tf_op jit(solution)/shard_map/ppermute | solution.py:465
  46.1 17.4 %copy-start.4 = (f32[1,24,384]{2,1,0:T(8,128)S(1)}, f32[1,24,384]{2,1,0:T(8,128)}, u32[]{:S(2)}) copy-start(f32[1,24,384]{2,1,0:T(8,128)} %rate_ref.1) | copy-start | bytes 110596
  46.2 17.3 %copy-start.5 = (s32[24,384]{1,0:T(8,128)S(1)}, s32[24,384]{1,0:T(8,128)}, u32[]{:S(2)}) copy-start(s32[24,384]{1,0:T(8,128)} %land_ref.1) | copy-start | bytes 110596
